TPU v7x, 256 devices: a whole 4x4x8 slice. The times are simulated.
256 devices in a mesh: blk: 32 (over y, x, z_lo), grp: 8 (over z_hi, core).
Axes of the slice: x: 4, y: 4, z: 8 (z_hi: 4, z_lo: 2; z = z_hi * 2 + z_lo), core: 2. Of those that a mesh axis runs over, the one named last changes fastest.
Arguments:
- patch_input: bfloat16 [131072, 1536], P(('blk', 'grp')), may hold values from -6 to 6
- hidden_pre: bfloat16 [73728, 3072], P(('blk', 'grp')), may hold values from -6 to 6
- down_weight: bfloat16 [3072, 1536], replicated, may hold values from -0.109375 to 0.109375
- text_features: bfloat16 [4096, 1536], P(('blk', 'grp')), may hold values from -6 to 6
- patch_counts: int32 [4096], P(('blk', 'grp')), may hold values from 1 to 497, as said below
- owners: int32 [131072], P(('blk', 'grp')), may hold values from -1 to 31, as said below
- pair_labels: int32 [4096], P(('blk', 'grp')), may hold values from 0 to 4095, as said below
Outputs:
- d_patches: bfloat16 [131072, 1536], P(('blk', 'grp'))
- d_hidden: bfloat16 [73728, 3072], P(('blk', 'grp'))
Inputs may be any that keep to these rules, and one draw needn't show every extreme that they name: `patch_counts`: each block of 512 patch slots holds 16 images; their counts sum to the block's live slots, which are the block's first slots; at least 64 are live, and in each grp index some block has all 512 live. Some image has exactly 497 patches. owners is -1 exactly on the slots that no image takes. Among the blocks of one grp index, every blk index is named by exactly 288 live slots; one block names one blk index at most 17 times, exactly 17 in some block of each grp index. `pair_labels`: the paired text of image i lies in a group 0 to 3 groups before image i's group, cyclically over 32 groups.
All inputs are finite; a program needn't handle non-finite values.
Results may differ from a plain program's by a relative error of at most 0.0065.
Values may be sent and summed in bfloat16 or wider, within the bound.
No kernel may reach another device: no remote copies, remote signals or barrier semaphores. Data moves between devices by JAX's collectives and lax.ppermute only.
A program may use at most 128 MiB of HBM per device.

v0:
```python
import jax
import jax.numpy as jnp
from jax import lax
from jax.sharding import PartitionSpec as P

STEPS = 4


GELU_A = 0.7978845608028654
GELU_B = 0.044715
LOGIT_SCALE_TEMP = 10.0
LOGIT_BIAS_SHIFT = -2.0
LOSS_SCALE_FACTOR = 128.0


def passed_along(block, axis, distance):
    devices = range(lax.axis_size(axis))
    route = [((i - distance) % len(devices), i) for i in devices]
    return lax.ppermute(block, axis, route)


def gelu_tanh(entries):
    inside = GELU_A * (entries + GELU_B * entries * entries * entries)
    return 0.5 * entries * (1.0 + jnp.tanh(inside))


def gelu_slope(entries):
    inside = GELU_A * (entries + GELU_B * entries * entries * entries)
    tangent = jnp.tanh(inside)
    return 0.5 * (1.0 + tangent) + 0.5 * entries * (1.0 - tangent * tangent) * GELU_A * (
        1.0 + 3.0 * GELU_B * entries * entries
    )


def spread_rows(rows, target, buffer_rows):
    buffer = jnp.zeros((buffer_rows, rows.shape[1]), rows.dtype)
    return buffer.at[target].set(rows, mode="drop")


def on_device(
    patch_input, hidden_pre, down_weight, text_features, patch_counts, owners, pair_labels
):
    blk_count = lax.axis_size("blk")
    grp_count = lax.axis_size("grp")
    slot_total = patch_input.shape[0]
    row_total = hidden_pre.shape[0]
    image_total = text_features.shape[0]
    model_width = patch_input.shape[1]
    capacity = slot_total // blk_count + 1
    buffer_rows = blk_count * capacity
    blk_position = lax.axis_index("blk")
    owner_ids = jnp.arange(blk_count, dtype=jnp.int32)
    owner_hits = (owners[:, None] == owner_ids[None, :]).astype(jnp.int32)
    owner_rank = jnp.sum((jnp.cumsum(owner_hits, axis=0) - 1) * owner_hits, axis=1)
    is_live = owners >= 0
    target = jnp.where(is_live, owners * capacity + owner_rank, buffer_rows)
    tallies = jnp.sum(owner_hits, axis=0)
    all_tallies = lax.all_gather(tallies, "blk", axis=0, tiled=True).reshape(blk_count, blk_count)
    column = lax.dynamic_slice_in_dim(all_tallies, blk_position, 1, 1)[:, 0]
    running = jnp.cumsum(column)
    row_ids = jnp.arange(row_total, dtype=jnp.int32)
    source_of = jnp.sum((row_ids[:, None] >= running[None, :]).astype(jnp.int32), axis=1)
    start_of = jnp.sum(
        (owner_ids[None, :] == source_of[:, None]).astype(jnp.int32) * (running - column)[None, :],
        axis=1,
    )
    slot_place = source_of * capacity + row_ids - start_of
    outgoing = spread_rows(hidden_pre, slot_place, buffer_rows).reshape(
        blk_count, capacity, hidden_pre.shape[1]
    )
    arrived = lax.all_to_all(outgoing, "blk", split_axis=0, concat_axis=0, tiled=True).reshape(
        buffer_rows, hidden_pre.shape[1]
    )
    hidden_rows = jnp.take(arrived, target, axis=0, mode="fill", fill_value=0)
    active = gelu_tanh(hidden_rows.astype(jnp.float32)).astype(jnp.bfloat16)
    branch = jnp.dot(active, down_weight, preferred_element_type=jnp.float32)
    summed = patch_input.astype(jnp.float32) + branch
    centered = summed - jnp.mean(summed, axis=-1, keepdims=True)
    scale_inv = lax.rsqrt(jnp.mean(centered * centered, axis=-1, keepdims=True) + 1e-06)
    normed = centered * scale_inv
    image_ends = jnp.cumsum(patch_counts)
    slot_ids = jnp.arange(slot_total, dtype=jnp.int32)
    image_of = jnp.sum((slot_ids[:, None] >= image_ends[None, :]).astype(jnp.int32), axis=1)
    member = (jnp.arange(image_total, dtype=jnp.int32)[:, None] == image_of[None, :]).astype(
        jnp.float32
    )
    image_sizes = patch_counts.astype(jnp.float32)[:, None]
    pooled = jnp.dot(member, normed, precision=lax.Precision.HIGHEST) / image_sizes
    embed_norm = jnp.sqrt(jnp.sum(pooled * pooled, axis=-1, keepdims=True) + 1e-06)
    embedding = pooled / embed_norm
    embed_b = embedding.astype(jnp.bfloat16)
    text = text_features.astype(jnp.float32)
    text_b = (text / jnp.sqrt(jnp.sum(text * text, axis=-1, keepdims=True) + 1e-06)).astype(
        jnp.bfloat16
    )
    group_rows = grp_count * image_total
    columns = jnp.arange(group_rows, dtype=jnp.int32)
    embed_grad = jnp.zeros((image_total, model_width), jnp.float32)
    current_text_block = lax.all_gather(text_b, "grp", axis=0, tiled=True)
    for rotation in range(STEPS):
        if rotation > 0:
            current_text_block = passed_along(current_text_block, "blk", 1)
        source = (blk_position - rotation) % blk_count
        pair_scores_matrix = (
            LOGIT_SCALE_TEMP
            * lax.dot_general(
                embed_b,
                current_text_block,
                (((1,), (1,)), ((), ())),
                preferred_element_type=jnp.float32,
            )
            + LOGIT_BIAS_SHIFT
        )
        positive_mask = (pair_labels[:, None] == source * group_rows + columns[None, :]).astype(
            jnp.float32
        )
        pair_weight_matrix = (
            LOSS_SCALE_FACTOR
            * LOGIT_SCALE_TEMP
            * (jax.nn.sigmoid(pair_scores_matrix) - positive_mask)
        ).astype(jnp.bfloat16)
        embed_grad = embed_grad + jnp.dot(
            pair_weight_matrix, current_text_block, preferred_element_type=jnp.float32
        )
    radial = jnp.sum(embedding * embed_grad, axis=-1, keepdims=True)
    pooled_grad = (embed_grad - embedding * radial) / embed_norm
    spread = pooled_grad / image_sizes
    normed_grad = lax.dot_general(
        member, spread, (((0,), (0,)), ((), ())), precision=lax.Precision.HIGHEST
    )
    mean_grad = jnp.mean(normed_grad, axis=-1, keepdims=True)
    mean_cross = jnp.mean(normed_grad * normed, axis=-1, keepdims=True)
    summed_grad = (normed_grad - mean_grad - normed * mean_cross) * scale_inv
    d_patches = summed_grad.astype(jnp.bfloat16)
    active_grad = lax.dot_general(
        d_patches, down_weight, (((1,), (1,)), ((), ())), preferred_element_type=jnp.float32
    )
    slot_grad = (gelu_slope(hidden_rows.astype(jnp.float32)) * active_grad).astype(jnp.bfloat16)
    outgoing = spread_rows(slot_grad, target, buffer_rows).reshape(
        blk_count, capacity, slot_grad.shape[1]
    )
    arrived = lax.all_to_all(outgoing, "blk", split_axis=0, concat_axis=0, tiled=True).reshape(
        buffer_rows, slot_grad.shape[1]
    )
    d_hidden = jnp.take(arrived, slot_place, axis=0)
    return (d_patches, d_hidden)


def solution(mesh):
    in_specs = (
        P(("blk", "grp"), None),
        P(("blk", "grp"), None),
        P(),
        P(("blk", "grp"), None),
        P(("blk", "grp")),
        P(("blk", "grp")),
        P(("blk", "grp")),
    )
    out_specs = (P(("blk", "grp"), None), P(("blk", "grp"), None))
    return jax.shard_map(
        on_device, mesh=mesh, in_specs=in_specs, out_specs=out_specs, check_vma=False
    )
```

profile of v0, /device:TPU:2, one launch (start us, length us, event | category | flops | bytes accessed | tf_op | source)
XLA Modules:
  0.0 392.6 jit_solution(18352006675948387672)
XLA Ops:
  5.9 155.4 %all-reduce.1 = s32[32,32]{1,0:T(8,128)S(1)} all-reduce(s32[32,32]{1,0:T(8,128)S(1)} %reshape.189), channel_id=1, replica_groups=mesh['blk'=32,'grp'=8] {'blk'}, use_global_device_ids=true, to_apply=%add | all-reduce | flops 1024 | bytes 8192
  162.4 5.1 %scatter_custom_fusion = bf16[544,3072]{1,0:T(8,128)(2,1)S(1)} fusion(s32[288]{0:T(512)S(1)} %fusion.101, bf16[288,3072]{1,0:T(8,128)(2,1)} %param.8, bf16[]{:T(256)} %constant.102.clone.1), kind=kCustom, calls=%fused_computation.39 | custom fusion | bytes 3342848 | tf_op jit(solution)/shard_map/scatter | solution.py:37
  167.5 3.2 reshape.191
  170.7 9.8 %all-to-all-start = ((bf16[32,17,3072]{2,1,0:T(8,128)(2,1)}), bf16[32,17,3072]{2,1,0:T(8,128)(2,1)}, u32[]{:S(2)}, u32[]{:S(2)}) async-start(bf16[32,17,3072]{2,1,0:T(8,128)(2,1)} %reshape.191), calls=%async_computation | async-start | bytes 9437184 | tf_op jit(solution)/shard_map/all_to_all | solution.py:71
  180.7 47.9 %all_gather.7 = bf16[128,1536]{1,0:T(8,128)(2,1)S(1)} all-gather(bf16[16,1536]{1,0:T(8,128)(2,1)S(1)} %fusion.57), channel_id=1, replica_groups=mesh['blk'=32,'grp'=8] {'grp'}, dimensions={0}, use_global_device_ids=true | all-gather | bytes 442368 | tf_op jit(solution)/shard_map/all_gather | solution.py:99
  229.7 11.2 %collective-permute-done = bf16[128,1536]{1,0:T(8,128)(2,1)S(1)} collective-permute-done((bf16[128,1536]{1,0:T(8,128)(2,1)S(1)}, bf16[128,1536]{1,0:T(8,128)(2,1)S(1)}, u32[]{:S(2)}, u32[]{:S(2)}) %collective-permute-start) | collective-permute-done | bytes 393248 | tf_op jit(solution)/shard_map/ppermute | solution.py:19
  244.1 8.4 %collective-permute-done.1 = bf16[128,1536]{1,0:T(8,128)(2,1)} collective-permute-done((bf16[128,1536]{1,0:T(8,128)(2,1)S(1)}, bf16[128,1536]{1,0:T(8,128)(2,1)}, u32[]{:S(2)}, u32[]{:S(2)}) %collective-permute-start.1) | collective-permute-done | bytes 393248 | tf_op jit(solution)/shard_map/ppermute | solution.py:19
  253.6 3.6 reshape.192
  257.2 3.8 gather_fusion
  261.0 10.7 %fusion.126 = (f32[512]{0:T(512)S(1)}, f32[512,1536]{1,0:T(8,128)S(1)}) fusion(bf16[3072,1536]{1,0:T(8,128)(2,1)} %param.9, bf16[512,3072]{1,0:T(8,128)(2,1)} %gather_fusion, pred[512]{0:T(512)(128)(4,1)S(1)} %get-tuple-element.6, bf16[512,1536]{1,0:T(8,128)(2,1)} %param.7), kind=kOutput, calls=%fused_computation.187 | convolution fusion | flops 4851498496 | bytes 17304064 | tf_op jit(solution)/shard_map/dot_general | solution.py:76
  272.5 2.1 multiply_reduce_fusion.3
  275.2 2.1 fusion.55
  277.3 1.8 convolution_add_fusion.3
  279.1 1.7 convolution_add_fusion.2
  280.8 1.9 multiply_reduce_fusion.2
  282.7 2.1 fusion.124
  286.9 11.9 %fusion.7 = bf16[512,3072]{1,0:T(8,128)(2,1)} fusion(bf16[512,1536]{1,0:T(8,128)(2,1)S(1)} %multiply_convert_fusion, bf16[3072,1536]{1,0:T(8,128)(2,1)} %param.9, bf16[512,3072]{1,0:T(8,128)(2,1)S(1)} %copy-done.2, pred[512]{0:T(512)(128)(4,1)S(1)} %copy-done.17), kind=kOutput, calls=%fused_computation.18 | convolution fusion | flops 4864868352 | bytes 17302016 | tf_op jit(solution)/shard_map/dot_general | solution.py:135
  298.8 7.2 %scatter_custom_fusion.1 = bf16[544,3072]{1,0:T(8,128)(2,1)S(1)} fusion(s32[512]{0:T(512)} %copy-done.13, bf16[512,3072]{1,0:T(8,128)(2,1)} %fusion.7, bf16[]{:T(256)} %constant.102.clone.1), kind=kCustom, calls=%fused_computation.37 | custom fusion | bytes 3342848 | tf_op jit(solution)/shard_map/scatter | solution.py:37
  306.0 3.2 reshape.193
  309.2 14.1 %all-to-all-start.1 = ((bf16[32,17,3072]{2,1,0:T(8,128)(2,1)}), bf16[32,17,3072]{2,1,0:T(8,128)(2,1)}, u32[]{:S(2)}, u32[]{:S(2)}) async-start(bf16[32,17,3072]{2,1,0:T(8,128)(2,1)} %reshape.193), calls=%async_computation.1 | async-start | bytes 9437184 | tf_op jit(solution)/shard_map/all_to_all | solution.py:142
  323.4 59.3 %all-to-all-done.1 = bf16[32,17,3072]{2,1,0:T(8,128)(2,1)} async-done(((bf16[32,17,3072]{2,1,0:T(8,128)(2,1)}), bf16[32,17,3072]{2,1,0:T(8,128)(2,1)}, u32[]{:S(2)}, u32[]{:S(2)}) %all-to-all-start.1) | async-done | bytes 3342368 | tf_op jit(solution)/shard_map/all_to_all | solution.py:142
  382.7 3.6 reshape.194
  386.3 3.4 gather_fusion.1
  389.7 2.9 broadcast_select_fusion.1
  (83 shorter events, 14.7 us)
Async XLA Ops:
  161.8 0.6 copy-start.8
  162.4 8.3 %copy-start.11 = (s32[288]{0:T(512)}, s32[288]{0:T(512)S(1)}, u32[]{:S(2)}) copy-start(s32[288]{0:T(512)S(1)} %fusion.101) | copy-start | bytes 3460
  170.7 9.8 %copy-start.6 = (bf16[16,1536]{1,0:T(8,128)(2,1)S(1)}, bf16[16,1536]{1,0:T(8,128)(2,1)}, u32[]{:S(2)}) copy-start(bf16[16,1536]{1,0:T(8,128)(2,1)} %param.10) | copy-start | bytes 147460
  170.7 59.0 %copy-start.7 = (s32[512]{0:T(512)S(1)}, s32[512]{0:T(512)}, u32[]{:S(2)}) copy-start(s32[512]{0:T(512)} %param.12) | copy-start | bytes 6148
  170.7 71.9 %copy-start.14 = (s32[16]{0:T(128)S(1)}, s32[16]{0:T(128)}, u32[]{:S(2)}) copy-start(s32[16]{0:T(128)} %param.11) | copy-start | bytes 196
  170.7 82.9 %all-to-all-start = ((bf16[32,17,3072]{2,1,0:T(8,128)(2,1)}), bf16[32,17,3072]{2,1,0:T(8,128)(2,1)}, u32[]{:S(2)}, u32[]{:S(2)}) async-start(bf16[32,17,3072]{2,1,0:T(8,128)(2,1)} %reshape.191), calls=%async_computation | async-start | bytes 9437184 | tf_op jit(solution)/shard_map/all_to_all | solution.py:71
  228.6 24.9 %copy-start = (bf16[128,1536]{1,0:T(8,128)(2,1)}, bf16[128,1536]{1,0:T(8,128)(2,1)S(1)}, u32[]{:S(2)}) copy-start(bf16[128,1536]{1,0:T(8,128)(2,1)S(1)} %all_gather.7) | copy-start | bytes 1179652
  228.6 12.3 %collective-permute-start = (bf16[128,1536]{1,0:T(8,128)(2,1)S(1)}, bf16[128,1536]{1,0:T(8,128)(2,1)S(1)}, u32[]{:S(2)}, u32[]{:S(2)}) collective-permute-start(bf16[128,1536]{1,0:T(8,128)(2,1)S(1)} %all_gather.7), channel_id=1, source_target_pairs={{248,0},{0,8},{8,16},{16,24},{24,32},{32,40},{40,48},{48,56},{56,6... | collective-permute-start | bytes 1179656 | tf_op jit(solution)/shard_map/ppermute | solution.py:19
  229.7 27.5 %copy-start.13 = (s32[512]{0:T(512)}, s32[512]{0:T(512)S(1)}, u32[]{:S(2)}) copy-start(s32[512]{0:T(512)S(1)} %get-tuple-element.7) | copy-start | bytes 6148
  229.7 31.3 %copy-start.16 = (pred[512]{0:T(512)(128)(4,1)}, pred[512]{0:T(512)(128)(4,1)S(1)}, u32[]{:S(2)}) copy-start(pred[512]{0:T(512)(128)(4,1)S(1)} %get-tuple-element.6) | copy-start | bytes 1540
  240.9 12.7 %copy-start.4 = (bf16[128,1536]{1,0:T(8,128)(2,1)}, bf16[128,1536]{1,0:T(8,128)(2,1)S(1)}, u32[]{:S(2)}) copy-start(bf16[128,1536]{1,0:T(8,128)(2,1)S(1)} %collective-permute-done) | copy-start | bytes 1179652
  240.9 11.6 %collective-permute-start.1 = (bf16[128,1536]{1,0:T(8,128)(2,1)S(1)}, bf16[128,1536]{1,0:T(8,128)(2,1)}, u32[]{:S(2)}, u32[]{:S(2)}) collective-permute-start(bf16[128,1536]{1,0:T(8,128)(2,1)S(1)} %collective-permute-done), channel_id=1, source_target_pairs={{248,0},{0,8},{8,16},{16,24},{24,32},{32,40},{40,48},{48,56},{56,6... | collective-permute-start | bytes 1179656 | tf_op jit(solution)/shard_map/ppermute | solution.py:19
  252.5 28.4 %collective-permute-start.2 = (bf16[128,1536]{1,0:T(8,128)(2,1)}, bf16[128,1536]{1,0:T(8,128)(2,1)}, u32[]{:S(2)}, u32[]{:S(2)}) collective-permute-start(bf16[128,1536]{1,0:T(8,128)(2,1)} %collective-permute-done.1), channel_id=1, source_target_pairs={{248,0},{0,8},{8,16},{16,24},{24,32},{32,40},{40,48},{48,56},{56,6... | collective-permute-start | bytes 1179656 | tf_op jit(solution)/shard_map/ppermute | solution.py:19
  271.8 0.7 copy-start.18
  271.8 2.8 copy-start.15
  271.8 3.4 copy-start.1
  277.3 5.4 %copy-start.3 = (f32[16,1536]{1,0:T(8,128)S(1)}, f32[16,1536]{1,0:T(8,128)}, u32[]{:S(2)}) copy-start(f32[16,1536]{1,0:T(8,128)} %get-tuple-element.13) | copy-start | bytes 294916
  277.3 5.4 %copy-start.10 = (f32[16]{0:T(128)S(1)}, f32[16]{0:T(128)}, u32[]{:S(2)}) copy-start(f32[16]{0:T(128)} %sqrt_multiply_fusion) | copy-start | bytes 196
  284.8 2.1 copy-start.2
  284.8 2.1 copy-start.17
  285.7 1.1 copy-start.5
  309.2 14.2 %copy-start.12 = (s32[288]{0:T(512)S(1)}, s32[288]{0:T(512)}, u32[]{:S(2)}) copy-start(s32[288]{0:T(512)} %copy-done.11) | copy-start | bytes 3460
  309.2 14.2 %copy-start.9 = (s32[288]{0:T(512)S(1)}, s32[288]{0:T(512)}, u32[]{:S(2)}) copy-start(s32[288]{0:T(512)} %copy-done.8) | copy-start | bytes 3460
  309.2 73.5 %all-to-all-start.1 = ((bf16[32,17,3072]{2,1,0:T(8,128)(2,1)}), bf16[32,17,3072]{2,1,0:T(8,128)(2,1)}, u32[]{:S(2)}, u32[]{:S(2)}) async-start(bf16[32,17,3072]{2,1,0:T(8,128)(2,1)} %reshape.193), calls=%async_computation.1 | async-start | bytes 9437184 | tf_op jit(solution)/shard_map/all_to_all | solution.py:142
where the time goes:
time: 394 us; the launch traced here: 393 us
  blocking collectives  203 us (52%)
  waiting for transfers between devices  78.9 us (20%)
  local copies, waits for them, and re-layouts  37.1 us (9%)
  matrix products  34.3 us (9%)
  starting transfers between devices  26.2 us (7%)
  other arithmetic  11.2 us (3%)
    unnamed x1, blocking collectives  155 us
    all_to_all x2, waiting for transfers between devices, on_device(): lax.all_to_all(outgoing, 'blk', split_axis=0, concat_axis=0, tiled=True)  59.3 us
    all_gather x1, blocking collectives, on_device(): current_text_block = lax.all_gather(text_b, 'grp', axis=0, tiled=True)  47.9 us
    all_to_all x2, starting transfers between devices, on_device(): lax.all_to_all(outgoing, 'blk', split_axis=0, concat_axis=0, tiled=True)  23.9 us
    ppermute x3, waiting for transfers between devices, passed_along(): return lax.ppermute(block, axis, route)  19.6 us
    scatter x2, local copies, waits for them, and re-layouts, spread_rows(): return buffer.at[target].set(rows, mode='drop')  12.3 us
    dot_general x1, matrix products, on_device(): lax.dot_general(d_patches, down_weight, (((1,), (1,)), ((), ())), preferr...  11.9 us
    dot_general x1, matrix products, on_device(): branch = jnp.dot(active, down_weight, preferred_element_type=jnp.float32)  10.7 us
  transfers between devices with their start and end apart: 5, of which 3 were waited for; matrix products, arithmetic and copies ran while one was open for 8% of the time, Pallas kernels for 0%

commit v1 on v0

v1 whole, which is shorter than its diff:
```python
import jax
import jax.numpy as jnp
from jax import lax
from jax.experimental import pallas as pl
from jax.experimental.pallas import tpu as pltpu
from jax.sharding import PartitionSpec as P

STEPS = 4
GELU_A = 0.7978845608028654
GELU_B = 0.044715
LOGIT_SCALE_TEMP = 10.0
LOGIT_BIAS_SHIFT = -2.0
LOSS_SCALE_FACTOR = 128.0

BLK = 32
CAP = 16
D = 1536
FF = 3072
SLOTS = 512
ROWS = 288
IMAGES = 16
LANES = 128
TILES = D // LANES
MSG = (TILES + 1) * CAP
WIDE = BLK * CAP
SLOT_K = 640
F32 = jnp.float32
BF16 = jnp.bfloat16
I32 = jnp.int32


def iota(shape, axis):
    return lax.broadcasted_iota(I32, shape, axis)


def vmem(count):
    return [pl.BlockSpec(memory_space=pltpu.VMEM)] * count


def params(mib):
    return pltpu.CompilerParams(vmem_limit_bytes=mib * 2**20)


def forward_kernel(hidden_ref, weight_ref, branch_ref, total):
    step = pl.program_id(0)
    entries = hidden_ref[...].astype(F32)
    inside = GELU_A * (entries + GELU_B * entries * entries * entries)
    active = (0.5 * entries * (1.0 + jnp.tanh(inside))).astype(BF16)
    part = jnp.dot(active, weight_ref[...], preferred_element_type=F32)

    @pl.when(step == 0)
    def _():
        total[...] = part

    @pl.when(step > 0)
    def _():
        total[...] += part

    @pl.when(step == pl.num_programs(0) - 1)
    def _():
        branch_ref[...] = total[...].astype(BF16)


def forward(hidden, weight):
    chunk = 512
    return pl.pallas_call(
        forward_kernel,
        grid=(FF // chunk,),
        in_specs=[
            pl.BlockSpec((ROWS, chunk), lambda k: (0, k)),
            pl.BlockSpec((chunk, D), lambda k: (k, 0)),
        ],
        out_specs=pl.BlockSpec((ROWS, D), lambda k: (0, 0)),
        out_shape=jax.ShapeDtypeStruct((ROWS, D), BF16),
        scratch_shapes=[pltpu.VMEM((ROWS, D), F32)],
        compiler_params=params(24),
        cost_estimate=pl.CostEstimate(
            flops=2 * ROWS * FF * D, bytes_accessed=2 * (FF * D + ROWS * FF), transcendentals=ROWS * FF
        ),
        name="owner_forward",
    )(hidden, weight)


def put_message(send_ref, wide, extra):
    for tile in range(TILES):
        send_ref[:, tile * CAP : (tile + 1) * CAP, :] = wide[
            :, tile * LANES : (tile + 1) * LANES
        ].reshape(BLK, CAP, LANES)
    stacked = jnp.concatenate(
        [extra[:, tile * LANES : (tile + 1) * LANES] for tile in range(TILES)], axis=0
    )
    row = iota((WIDE, TILES * BLK), 0)
    column = iota((WIDE, TILES * BLK), 1)
    pick = ((row >> 4) == (column & 31)) & ((row & 15) == (column >> 5))
    last = jnp.dot(pick.astype(F32).astype(BF16), stacked, preferred_element_type=F32)
    send_ref[:, TILES * CAP :, :] = last.astype(BF16).reshape(BLK, CAP, LANES)


def take_message(arrived_ref, rows_ref):
    for tile in range(TILES):
        rows_ref[0:WIDE, tile * LANES : (tile + 1) * LANES] = arrived_ref[
            :, tile * CAP : (tile + 1) * CAP, :
        ].reshape(WIDE, LANES)
    last = arrived_ref[:, TILES * CAP :, :].reshape(WIDE, LANES)
    row = iota((TILES * BLK, WIDE), 0)
    column = iota((TILES * BLK, WIDE), 1)
    pick = ((column >> 4) == (row & 31)) & ((column & 15) == (row >> 5))
    stacked = jnp.dot(pick.astype(F32).astype(BF16), last, preferred_element_type=F32).astype(BF16)
    for tile in range(TILES):
        rows_ref[WIDE : WIDE + BLK, tile * LANES : (tile + 1) * LANES] = stacked[
            tile * BLK : (tile + 1) * BLK, :
        ]
    rows_ref[WIDE + BLK :, :] = jnp.zeros((SLOT_K - WIDE - BLK, D), BF16)


def starts_of(counts):
    before = (iota((BLK, BLK), 0) > iota((BLK, BLK), 1)).astype(F32).astype(BF16)
    return jnp.dot(before, counts.astype(BF16), preferred_element_type=F32)


def pack_kernel(counts_ref, branch_ref, send_ref):
    counts = counts_ref[...].astype(F32)
    starts = starts_of(counts)
    counts_wide = jnp.broadcast_to(counts[:, None, :], (BLK, CAP, LANES)).reshape(WIDE, LANES)[:, :1]
    starts_wide = jnp.broadcast_to(starts[:, None, :], (BLK, CAP, LANES)).reshape(WIDE, LANES)[:, :1]
    rank = (iota((WIDE, 1), 0) & 15).astype(F32)
    key = jnp.where(rank < counts_wide, starts_wide + rank, -1.0)
    pick = (iota((WIDE, ROWS), 1).astype(F32) == key).astype(F32).astype(BF16)
    branch = branch_ref[...]
    wide = jnp.dot(pick, branch, preferred_element_type=F32).astype(BF16)
    key = jnp.where(counts[:, :1] > CAP, starts[:, :1] + CAP, -1.0)
    pick = (iota((BLK, ROWS), 1).astype(F32) == key).astype(F32).astype(BF16)
    extra = jnp.dot(pick, branch, preferred_element_type=F32).astype(BF16)
    put_message(send_ref, wide, extra)


def pack(counts, branch):
    return pl.pallas_call(
        pack_kernel,
        in_specs=vmem(2),
        out_specs=pl.BlockSpec(memory_space=pltpu.VMEM),
        out_shape=jax.ShapeDtypeStruct((BLK, MSG, LANES), BF16),
        compiler_params=params(24),
        cost_estimate=pl.CostEstimate(
            flops=2 * WIDE * ROWS * D, bytes_accessed=2 * (BLK * MSG * LANES + ROWS * D), transcendentals=0
        ),
        name="owner_pack",
    )(counts, branch)


def prepare_kernel(
    owners_row_ref, owners_col_ref, sizes_row_ref, sizes_col_ref, counts_ref,
    to_slots_ref, to_message_ref, to_rows_ref, member_ref, member3_ref,
):
    owners = owners_col_ref[...]
    hits = owners == iota((SLOTS, BLK), 1)
    earlier = (iota((SLOTS, SLOTS), 0) > iota((SLOTS, SLOTS), 1)).astype(F32).astype(BF16)
    prefix = jnp.dot(earlier, hits.astype(F32).astype(BF16), preferred_element_type=F32)
    rank = jnp.sum(jnp.where(hits, prefix, 0.0), axis=1, keepdims=True).astype(I32)
    place = jnp.where(rank < CAP, owners * CAP + rank, WIDE + owners)
    place = jnp.where(owners >= 0, place, -1)
    to_slots_ref[...] = (iota((SLOTS, SLOT_K), 1) == place).astype(F32).astype(BF16)

    owners = owners_row_ref[...]
    hits = owners == iota((BLK, SLOTS), 0)
    earlier = (iota((SLOTS, SLOTS), 0) < iota((SLOTS, SLOTS), 1)).astype(F32).astype(BF16)
    prefix = jnp.dot(hits.astype(F32).astype(BF16), earlier, preferred_element_type=F32)
    rank = jnp.sum(jnp.where(hits, prefix, 0.0), axis=0, keepdims=True).astype(I32)
    place = jnp.where(rank < CAP, owners * CAP + rank, WIDE + owners)
    place = jnp.where(owners >= 0, place, -1)
    to_message_ref[...] = (iota((WIDE + BLK, SLOTS), 0) == place).astype(F32).astype(BF16)

    counts = counts_ref[...].astype(F32)
    starts = starts_of(counts)
    own = iota((BLK, SLOT_K), 0)
    lane = iota((BLK, SLOT_K), 1)
    extra = lane >= WIDE
    mine = jnp.where(extra, lane - WIDE, lane >> 4) == own
    rank = jnp.where(extra, CAP, lane & 15).astype(F32)
    valid = mine & (rank < counts[:, :1])
    key = jnp.sum(jnp.where(valid, starts[:, :1] + rank + 1.0, 0.0), axis=0, keepdims=True) - 1.0
    to_rows_ref[...] = (iota((ROWS, SLOT_K), 0).astype(F32) == key).astype(F32).astype(BF16)

    sizes_row = sizes_row_ref[...].astype(F32)
    sizes_col = sizes_col_ref[...].astype(F32)
    row = iota((IMAGES, IMAGES), 0)
    column = iota((IMAGES, IMAGES), 1)
    begin = jnp.sum(jnp.where(column < row, sizes_row, 0.0), axis=1, keepdims=True)
    slot = iota((IMAGES, SLOTS), 1).astype(F32)
    member_ref[...] = ((slot >= begin) & (slot < begin + sizes_col)).astype(F32).astype(BF16)
    begin = jnp.sum(jnp.where(row < column, sizes_col, 0.0), axis=0, keepdims=True)
    slot = iota((SLOTS, IMAGES), 0).astype(F32)
    member = ((slot >= begin) & (slot < begin + sizes_row)).astype(F32)
    member3_ref[...] = jnp.concatenate([member, member, member], axis=1).astype(BF16)


def prepare(owners, patch_counts, counts):
    shapes = (
        (SLOTS, SLOT_K), (WIDE + BLK, SLOTS), (ROWS, SLOT_K), (IMAGES, SLOTS), (SLOTS, 3 * IMAGES),
    )
    return pl.pallas_call(
        prepare_kernel,
        in_specs=vmem(5),
        out_specs=vmem(5),
        out_shape=[jax.ShapeDtypeStruct(shape, BF16) for shape in shapes],
        compiler_params=params(24),
        cost_estimate=pl.CostEstimate(flops=2 * SLOTS * SLOTS * 256, bytes_accessed=2**21, transcendentals=0),
        name="prepare_onehots",
    )(owners[None, :], owners[:, None], patch_counts[None, :], patch_counts[:, None], counts)


def slot_kernel(
    arrived_ref, patch_ref, texts_ref, to_slots_ref, to_message_ref, member_ref, member3_ref,
    sizes_ref, labels_ref, columns_ref,
    patches_ref, send_ref,
    rows_ref, summed, normed_low, scale_ref, spread_ref,
):
    take_message(arrived_ref, rows_ref)
    to_slots = to_slots_ref[...]
    width = 512
    for part in range(D // width):
        columns = slice(part * width, (part + 1) * width)
        summed[:, columns] = patch_ref[:, columns].astype(F32) + jnp.dot(
            to_slots, rows_ref[:, columns], preferred_element_type=F32
        )

    height = 32

    @pl.loop(0, SLOTS // height)
    def _(at):
        rows = pl.ds(pl.multiple_of(at * height, height), height)
        values = summed[rows, :]
        centered = values - jnp.sum(values, axis=1, keepdims=True) * (1.0 / D)
        variance = jnp.sum(centered * centered, axis=1, keepdims=True) * (1.0 / D)
        scale = lax.rsqrt(variance + 1e-06)
        normed = centered * scale
        summed[rows, :] = normed
        high = normed.astype(BF16)
        rows_ref[rows, :] = high
        normed_low[rows, :] = (normed - high.astype(F32)).astype(BF16)
        scale_ref[rows, :] = jnp.broadcast_to(scale, (height, LANES))

    member = member_ref[...]
    sizes = sizes_ref[...].astype(F32)
    pooled = jnp.dot(member, rows_ref[0:SLOTS, :], preferred_element_type=F32)
    pooled = pooled + jnp.dot(member, normed_low[...], preferred_element_type=F32)
    pooled = pooled / sizes
    embed_norm = jnp.sqrt(jnp.sum(pooled * pooled, axis=1, keepdims=True) + 1e-06)
    embedding = pooled / embed_norm
    embed_b = embedding.astype(BF16)
    texts = texts_ref[...]
    logits = LOGIT_SCALE_TEMP * lax.dot_general(
        embed_b, texts, (((1,), (1,)), ((), ())), preferred_element_type=F32
    ) + LOGIT_BIAS_SHIFT
    positive = (labels_ref[...] == columns_ref[...]).astype(F32)
    sigmoid = 1.0 / (1.0 + jnp.exp(-logits))
    weights = (LOSS_SCALE_FACTOR * LOGIT_SCALE_TEMP * (sigmoid - positive)).astype(BF16)
    embed_grad = jnp.dot(weights, texts, preferred_element_type=F32)
    radial = jnp.sum(embedding * embed_grad, axis=1, keepdims=True)
    spread = (embed_grad - embedding * radial) / embed_norm / sizes
    for piece in range(3):
        top = spread.astype(BF16)
        spread_ref[piece * IMAGES : (piece + 1) * IMAGES, :] = top
        spread = spread - top.astype(F32)

    @pl.loop(0, SLOTS // height)
    def _(at):
        rows = pl.ds(pl.multiple_of(at * height, height), height)
        grad = jnp.dot(member3_ref[rows, :], spread_ref[...], preferred_element_type=F32)
        normed = summed[rows, :]
        mean_grad = jnp.sum(grad, axis=1, keepdims=True) * (1.0 / D)
        mean_cross = jnp.sum(grad * normed, axis=1, keepdims=True) * (1.0 / D)
        scale = scale_ref[rows, :][:, :1]
        patches_ref[rows, :] = ((grad - mean_grad - normed * mean_cross) * scale).astype(BF16)

    packed = jnp.dot(to_message_ref[...], patches_ref[...], preferred_element_type=F32).astype(BF16)
    put_message(send_ref, packed[:WIDE, :], packed[WIDE:, :])


def slots(arrived, patch_input, texts, to_slots, to_message, member, member3, sizes, labels, columns):
    return pl.pallas_call(
        slot_kernel,
        in_specs=vmem(10),
        out_specs=vmem(2),
        out_shape=[
            jax.ShapeDtypeStruct((SLOTS, D), BF16),
            jax.ShapeDtypeStruct((BLK, MSG, LANES), BF16),
        ],
        scratch_shapes=[
            pltpu.VMEM((SLOT_K, D), BF16),
            pltpu.VMEM((SLOTS, D), F32),
            pltpu.VMEM((SLOTS, D), BF16),
            pltpu.VMEM((SLOTS, LANES), F32),
            pltpu.VMEM((3 * IMAGES, D), BF16),
        ],
        compiler_params=params(40),
        cost_estimate=pl.CostEstimate(
            flops=4 * SLOTS * SLOT_K * D, bytes_accessed=10 * 2**20, transcendentals=IMAGES * SLOTS
        ),
        name="slot_gradients",
    )(arrived, patch_input, texts, to_slots, to_message, member, member3, sizes, labels, columns)


def backward_kernel(arrived_ref, to_rows_ref, hidden_ref, weight_ref, out_ref, rows_ref, grads_ref):
    @pl.when(pl.program_id(0) == 0)
    def _():
        take_message(arrived_ref, rows_ref)
        grads_ref[...] = jnp.dot(
            to_rows_ref[...], rows_ref[...], preferred_element_type=F32
        ).astype(BF16)

    active_grad = lax.dot_general(
        grads_ref[...], weight_ref[...], (((1,), (1,)), ((), ())), preferred_element_type=F32
    )
    entries = hidden_ref[...].astype(F32)
    square = entries * entries
    tangent = jnp.tanh(GELU_A * (entries + GELU_B * square * entries))
    slope = 0.5 * (1.0 + tangent) + 0.5 * entries * (1.0 - tangent * tangent) * GELU_A * (
        1.0 + 3.0 * GELU_B * square
    )
    out_ref[...] = (slope * active_grad).astype(BF16)


def backward(arrived, to_rows, hidden, weight):
    chunk = 512
    return pl.pallas_call(
        backward_kernel,
        grid=(FF // chunk,),
        in_specs=[
            pl.BlockSpec((BLK, MSG, LANES), lambda k: (0, 0, 0)),
            pl.BlockSpec((ROWS, SLOT_K), lambda k: (0, 0)),
            pl.BlockSpec((ROWS, chunk), lambda k: (0, k)),
            pl.BlockSpec((chunk, D), lambda k: (k, 0)),
        ],
        out_specs=pl.BlockSpec((ROWS, chunk), lambda k: (0, k)),
        out_shape=jax.ShapeDtypeStruct((ROWS, FF), BF16),
        scratch_shapes=[pltpu.VMEM((SLOT_K, D), BF16), pltpu.VMEM((ROWS, D), BF16)],
        compiler_params=params(24),
        cost_estimate=pl.CostEstimate(
            flops=2 * ROWS * FF * D, bytes_accessed=2 * (FF * D + 2 * ROWS * FF), transcendentals=ROWS * FF
        ),
        name="owner_backward",
    )(arrived, to_rows, hidden, weight)


def on_device(
    patch_input, hidden_pre, down_weight, text_features, patch_counts, owners, pair_labels
):
    position = lax.axis_index("blk")
    grp_count = lax.axis_size("grp")
    tallies = jnp.sum(
        (owners[None, :] == jnp.arange(BLK, dtype=I32)[:, None]).astype(I32), axis=1, keepdims=True
    )
    counts = lax.all_to_all(
        jnp.broadcast_to(tallies, (BLK, LANES)), "blk", split_axis=0, concat_axis=0, tiled=True
    )
    branch = forward(hidden_pre, down_weight)
    arrived = lax.all_to_all(
        pack(counts, branch), "blk", split_axis=0, concat_axis=0, tiled=True
    )

    text = text_features.astype(F32)
    text_b = (text / jnp.sqrt(jnp.sum(text * text, axis=-1, keepdims=True) + 1e-06)).astype(BF16)
    met = [text_b]
    for distance in range(1, STEPS):
        route = [((i - distance) % BLK, i) for i in range(BLK)]
        met.append(lax.ppermute(text_b, "blk", route))
    texts = lax.all_gather(jnp.concatenate(met, axis=0), "grp", axis=0, tiled=True)
    at = jnp.arange(grp_count * STEPS * IMAGES, dtype=I32)
    source = (position - (at // IMAGES) % STEPS) % BLK
    columns = source * (grp_count * IMAGES) + at // (STEPS * IMAGES) * IMAGES + at % IMAGES

    to_slots, to_message, to_rows, member, member3 = prepare(owners, patch_counts, counts)
    d_patches, outgoing = slots(
        arrived, patch_input, texts, to_slots, to_message, member, member3,
        patch_counts[:, None], pair_labels[:, None], columns[None, :],
    )
    returned = lax.all_to_all(outgoing, "blk", split_axis=0, concat_axis=0, tiled=True)
    d_hidden = backward(returned, to_rows, hidden_pre, down_weight)
    return (d_patches, d_hidden)


def solution(mesh):
    rows = P(("blk", "grp"), None)
    flat = P(("blk", "grp"))
    return jax.shard_map(
        on_device,
        mesh=mesh,
        in_specs=(rows, rows, P(), rows, flat, flat, flat),
        out_specs=(rows, rows),
        check_vma=False,
    )
```

time: 394 us -> 165 us (0.42)
  blocking collectives: 203 us -> 32.9 us
  matrix products: 34.3 us -> 0 us
  waiting for transfers between devices: 78.9 us -> 45.6 us
  Pallas kernels: 0 us -> 28.9 us
  local copies, waits for them, and re-layouts: 37.1 us -> 17.7 us
  between operations: 1.59 us -> 14.1 us
  other arithmetic: 11.2 us -> 2.54 us
  starting transfers between devices: 26.2 us -> 21.9 us
    unnamed x1 -> x0, blocking collectives: 155 us -> none
    all_to_all x2, waiting for transfers between devices: 59.3 us -> 0.01 us  [the longest x1 0.01 us: on_device(): lax.all_to_all(pack(counts, branch), 'blk', split_axis=0, concat_axis=0,...]
    all_gather x1 -> x0, blocking collectives: 47.9 us -> none  [on_device(): current_text_block = lax.all_gather(text_b, 'grp', axis=0, tiled=True)]
    dot_general x8 -> x0, matrix products: 34.3 us -> none  [the longest x1 11.9 us: on_device(): lax.dot_general(d_patches, down_weight, (((1,), (1,)), ((), ())), preferr...]
    all_to_all x0 -> x1, blocking collectives: none -> 32.9 us  [on_device(): lax.all_to_all(outgoing, 'blk', split_axis=0, concat_axis=0, tiled=True)]
    pallas_call x0 -> x5, Pallas kernels: none -> 28.9 us  [the longest x1 12.5 us: slots(): pl.pallas_call(slot_kernel, in_specs=vmem(10), out_specs=vmem(2), out_sha...]
    all_gather x0 -> x1, waiting for transfers between devices: none -> 25.3 us  [on_device(): lax.all_gather(jnp.concatenate(met, axis=0), 'grp', axis=0, tiled=True)]
    reshape x5 -> x0, local copies, waits for them, and re-layouts: 13.7 us -> none  [the longest x2 7.23 us: on_device(): lax.all_to_all(outgoing, 'blk', split_axis=0, concat_axis=0, tiled=True)]
  transfers between devices with their start and end apart: 5 -> 6, of which waited for: 3 -> 2; matrix products, arithmetic and copies ran while one was open for 8% -> 2% of each run, Pallas kernels for 0% -> 4%
where the time goes in v1:
time: 165 us; the launch traced here: 164 us
  waiting for transfers between devices  45.6 us (28%)
  blocking collectives  32.9 us (20%)
  Pallas kernels  28.9 us (18%)
  starting transfers between devices  21.9 us (13%)
  local copies, waits for them, and re-layouts  17.7 us (11%)
  between operations  14.1 us (9%)
  other arithmetic  2.54 us (2%)
    all_to_all x1, blocking collectives, on_device(): lax.all_to_all(outgoing, 'blk', split_axis=0, concat_axis=0, tiled=True)  32.9 us
    all_gather x1, waiting for transfers between devices, on_device(): lax.all_gather(jnp.concatenate(met, axis=0), 'grp', axis=0, tiled=True)  25.3 us
    ppermute x3, waiting for transfers between devices, on_device(): met.append(lax.ppermute(text_b, 'blk', route))  20.3 us
    unnamed x38, local copies, waits for them, and re-layouts  16 us
    pallas_call x1, Pallas kernels, slots(): pl.pallas_call(slot_kernel, in_specs=vmem(10), out_specs=vmem(2), out_sha...  12.5 us
    all_to_all x1, starting transfers between devices, on_device(): lax.all_to_all(jnp.broadcast_to(tallies, (BLK, LANES)), 'blk', split_axis...  8.97 us
    all_to_all x1, starting transfers between devices, on_device(): lax.all_to_all(pack(counts, branch), 'blk', split_axis=0, concat_axis=0,...  8.43 us
    pallas_call x1, Pallas kernels, backward(): pl.pallas_call(backward_kernel, grid=(FF // chunk,), in_specs=[pl.BlockSp...  7.19 us
  transfers between devices with their start and end apart: 6, of which 2 were waited for; matrix products, arithmetic and copies ran while one was open for 2% of the time, Pallas kernels for 4%

profile of v1, /device:TPU:2, one launch (start us, length us, event | category | flops | bytes accessed | tf_op | source)
XLA Modules:
  0.0 163.7 jit_solution(16529565560065420763)
XLA Ops:
  8.7 9.0 %all-to-all-start = ((s32[32,1,128]{2,1,0:T(1,128)}), s32[32,1,128]{2,1,0:T(1,128)S(1)}, u32[]{:S(2)}, u32[]{:S(2)}) async-start(s32[32,1,128]{2,1,0:T(1,128)} %broadcast_in_dim.12), calls=%async_computation | async-start | bytes 32768 | tf_op jit(solution)/shard_map/all_to_all | solution.py:354
  17.7 0.9 fusion
  18.6 3.7 %copy-done = bf16[3072,1536]{1,0:T(8,128)(2,1)S(1)} copy-done((bf16[3072,1536]{1,0:T(8,128)(2,1)S(1)}, bf16[3072,1536]{1,0:T(8,128)(2,1)}, u32[]{:S(2)}) %copy-start) | copy-done | bytes 9437208
  22.3 1.5 copy-done.2
  23.7 5.2 %owner_forward.1.branch_ref = bf16[288,1536]{1,0:T(8,128)(2,1)S(1)} custom-call(bf16[288,3072]{1,0:T(8,128)(2,1)S(1)} %copy-done.2, bf16[3072,1536]{1,0:T(8,128)(2,1)S(1)} %copy-done), custom_call_target="tpu_custom_call" | custom-call | flops 2717908992 | bytes 11206656 | tf_op jit(solution)/shard_map/owner_forward/pallas_call | solution.py:66
  29.0 2.7 %owner_pack.1 = bf16[32,208,128]{2,1,0:T(8,128)(2,1)} custom-call(s32[32,128]{1,0:T(8,128)S(1)} %bitcast.6, bf16[288,1536]{1,0:T(8,128)(2,1)S(1)} %owner_forward.1.branch_ref), custom_call_target="tpu_custom_call" | custom-call | flops 452984832 | bytes 2588672 | tf_op jit(solution)/shard_map/owner_pack/pallas_call | solution.py:138
  31.7 8.4 %all-to-all-start.1 = ((bf16[32,208,128]{2,1,0:T(8,128)(2,1)}), bf16[32,208,128]{2,1,0:T(8,128)(2,1)S(1)}, u32[]{:S(2)}, u32[]{:S(2)}) async-start(bf16[32,208,128]{2,1,0:T(8,128)(2,1)} %owner_pack.1), calls=%async_computation.1 | async-start | bytes 3407872 | tf_op jit(solution)/shard_map/all_to_all | solution.py:358
  40.3 2.4 %collective-permute-start.2 = (bf16[16,1536]{1,0:T(8,128)(2,1)S(1)}, bf16[16,1536]{1,0:T(8,128)(2,1)S(1)}, u32[]{:S(2)}, u32[]{:S(2)}) collective-permute-start(bf16[16,1536]{1,0:T(8,128)(2,1)S(1)} %fusion.1), channel_id=1, source_target_pairs={{232,0},{240,8},{248,16},{0,24},{8,32},{16,40},{24,48},{32,56},{40... | collective-permute-start | bytes 147464 | tf_op jit(solution)/shard_map/ppermute | solution.py:367
  42.8 1.2 collective-permute-start.1
  43.9 0.9 collective-permute-start
  44.8 20.3 %collective-permute-done.2 = bf16[16,1536]{1,0:T(8,128)(2,1)S(1)} collective-permute-done((bf16[16,1536]{1,0:T(8,128)(2,1)S(1)}, bf16[16,1536]{1,0:T(8,128)(2,1)S(1)}, u32[]{:S(2)}, u32[]{:S(2)}) %collective-permute-start.2) | collective-permute-done | bytes 49184 | tf_op jit(solution)/shard_map/ppermute | solution.py:367
  66.0 0.9 copy.20.owners_col_ref
  66.9 0.9 copy-done.6
  67.8 1.2 prepare_onehots.1
  72.1 25.3 %all-gather.2.cloned.1.call-done.texts_ref = bf16[512,1536]{1,0:T(8,128)(2,1)} async-done(((bf16[64,1536]{1,0:T(8,128)(2,1)}), bf16[512,1536]{1,0:T(8,128)(2,1)}) %all-gather.2.cloned.1.call-update) | async-done | bytes 1572880 | tf_op jit(solution)/shard_map/all_gather | solution.py:368
  97.4 1.4 copy-done.9
  98.8 1.4 copy-done.10
  100.2 1.1 copy-done.12
  101.3 1.1 copy-done.14
  102.4 0.9 copy-done.16
  103.3 12.5 %slot_gradients.1 = (bf16[512,1536]{1,0:T(8,128)(2,1)}, bf16[32,208,128]{2,1,0:T(8,128)(2,1)S(1)}) custom-call(bf16[32,208,128]{2,1,0:T(8,128)(2,1)S(1)} %all-to-all-done.1.arrived_ref, bf16[512,1536]{1,0:T(8,128)(2,1)S(1)} %copy-done.9, bf16[512,1536]{1,0:T(8,128)(2,1)S(1)} %copy-done.10, bf16[512,640]{1,0:T(8,128)(2,1)S(1)} %copy-done.12, ...), custom_call_target="tpu_custom_call" | custom-call | flops 2013265920 | bytes 10485760 | tf_op jit(solution)/shard_map/slot_gradients/pallas_call | solution.py:281
  115.8 32.9 %all_to_all.18.arrived_ref = bf16[32,208,128]{2,1,0:T(8,128)(2,1)S(1)} all-to-all(bf16[32,208,128]{2,1,0:T(8,128)(2,1)S(1)} %get-tuple-element.14), channel_id=1, replica_groups=mesh['blk'=32,'grp'=8] {'blk'}, dimensions={0} | all-to-all | bytes 3407872 | tf_op jit(solution)/shard_map/all_to_all | solution.py:378
  148.7 1.0 copy-done.5
  149.7 7.2 %owner_backward.1 = bf16[288,3072]{1,0:T(8,128)(2,1)} custom-call(bf16[32,208,128]{2,1,0:T(8,128)(2,1)S(1)} %all_to_all.18.arrived_ref, bf16[288,640]{1,0:T(8,128)(2,1)S(1)} %copy-done.5, bf16[288,3072]{1,0:T(8,128)(2,1)S(1)} %copy-done.3, bf16[3072,1536]{1,0:T(8,128)(2,1)S(1)} %copy-done.1), custom_call_target="tpu_custom_call" | custom-call | flops 2717908992 | bytes 12976128 | tf_op jit(solution)/shard_map/owner_backward/pallas_call | solution.py:326
  (43 shorter events, 5.6 us)
Async XLA Ops:
  8.7 20.3 %all-to-all-start = ((s32[32,1,128]{2,1,0:T(1,128)}), s32[32,1,128]{2,1,0:T(1,128)S(1)}, u32[]{:S(2)}, u32[]{:S(2)}) async-start(s32[32,1,128]{2,1,0:T(1,128)} %broadcast_in_dim.12), calls=%async_computation | async-start | bytes 32768 | tf_op jit(solution)/shard_map/all_to_all | solution.py:354
  18.6 3.7 %copy-start = (bf16[3072,1536]{1,0:T(8,128)(2,1)S(1)}, bf16[3072,1536]{1,0:T(8,128)(2,1)}, u32[]{:S(2)}) copy-start(bf16[3072,1536]{1,0:T(8,128)(2,1)} %weight_ref.3) | copy-start | bytes 28311556
  22.3 1.5 copy-start.2
  31.7 8.5 %copy-start.17 = (bf16[16,1536]{1,0:T(8,128)(2,1)S(1)}, bf16[16,1536]{1,0:T(8,128)(2,1)}, u32[]{:S(2)}) copy-start(bf16[16,1536]{1,0:T(8,128)(2,1)} %param.10) | copy-start | bytes 147460
  31.7 34.1 %copy-start.8 = (s32[16]{0:T(128)S(1)}, s32[16]{0:T(128)}, u32[]{:S(2)}) copy-start(s32[16]{0:T(128)} %param.11) | copy-start | bytes 196
  31.7 34.2 %copy-start.18 = (s32[16]{0:T(128)S(1)}, s32[16]{0:T(128)}, u32[]{:S(2)}) copy-start(s32[16]{0:T(128)} %param.13) | copy-start | bytes 196
  31.7 34.2 %copy-start.7 = (s32[512]{0:T(512)S(1)}, s32[512]{0:T(512)}, u32[]{:S(2)}) copy-start(s32[512]{0:T(512)} %param.12) | copy-start | bytes 6148
  31.7 65.7 %all-to-all-start.1 = ((bf16[32,208,128]{2,1,0:T(8,128)(2,1)}), bf16[32,208,128]{2,1,0:T(8,128)(2,1)S(1)}, u32[]{:S(2)}, u32[]{:S(2)}) async-start(bf16[32,208,128]{2,1,0:T(8,128)(2,1)} %owner_pack.1), calls=%async_computation.1 | async-start | bytes 3407872 | tf_op jit(solution)/shard_map/all_to_all | solution.py:358
  40.2 57.2 %all-gather.2.cloned.1.call-start = ((), (), s32[]{:S(2)}) async-start(), calls=%async_computation.3 | async-start | bytes 1769472 | tf_op jit(solution)/shard_map/all_gather | solution.py:368
  40.3 24.7 %collective-permute-start.2 = (bf16[16,1536]{1,0:T(8,128)(2,1)S(1)}, bf16[16,1536]{1,0:T(8,128)(2,1)S(1)}, u32[]{:S(2)}, u32[]{:S(2)}) collective-permute-start(bf16[16,1536]{1,0:T(8,128)(2,1)S(1)} %fusion.1), channel_id=1, source_target_pairs={{232,0},{240,8},{248,16},{0,24},{8,32},{16,40},{24,48},{32,56},{40... | collective-permute-start | bytes 147464 | tf_op jit(solution)/shard_map/ppermute | solution.py:367
  42.8 22.3 %collective-permute-start.1 = (bf16[16,1536]{1,0:T(8,128)(2,1)S(1)}, bf16[16,1536]{1,0:T(8,128)(2,1)S(1)}, u32[]{:S(2)}, u32[]{:S(2)}) collective-permute-start(bf16[16,1536]{1,0:T(8,128)(2,1)S(1)} %fusion.1), channel_id=1, source_target_pairs={{240,0},{248,8},{0,16},{8,24},{16,32},{24,40},{32,48},{40,56},{48,... | collective-permute-start | bytes 147464 | tf_op jit(solution)/shard_map/ppermute | solution.py:367
  43.9 21.1 %collective-permute-start = (bf16[16,1536]{1,0:T(8,128)(2,1)S(1)}, bf16[16,1536]{1,0:T(8,128)(2,1)S(1)}, u32[]{:S(2)}, u32[]{:S(2)}) collective-permute-start(bf16[16,1536]{1,0:T(8,128)(2,1)S(1)} %fusion.1), channel_id=1, source_target_pairs={{248,0},{0,8},{8,16},{16,24},{24,32},{32,40},{40,48},{48,56},{56,6... | collective-permute-start | bytes 147464 | tf_op jit(solution)/shard_map/ppermute | solution.py:367
  66.9 1.0 copy-start.6
  67.8 80.9 %copy-start.3 = (bf16[288,3072]{1,0:T(8,128)(2,1)S(1)}, bf16[288,3072]{1,0:T(8,128)(2,1)}, u32[]{:S(2)}) copy-start(bf16[288,3072]{1,0:T(8,128)(2,1)} %hidden_ref.3) | copy-start | bytes 5308420
  69.1 0.7 copy-start.4
  69.8 0.8 copy-start.11
  70.6 0.8 copy-start.13
  97.4 1.4 copy-start.9
  98.8 1.4 copy-start.10
  100.2 1.1 copy-start.12
  101.3 1.1 copy-start.14
  102.4 0.9 copy-start.16
  103.3 45.4 %copy-start.1 = (bf16[3072,1536]{1,0:T(8,128)(2,1)S(1)}, bf16[3072,1536]{1,0:T(8,128)(2,1)}, u32[]{:S(2)}) copy-start(bf16[3072,1536]{1,0:T(8,128)(2,1)} %weight_ref.3) | copy-start | bytes 28311556
  148.7 1.0 copy-start.5
  (1 other events, 0.7 us)
Sparse Core Ops, SparseCore 0:
  65.9 31.4 all-gather.1

commit v2 on v1

v2 whole, which is shorter than its diff:
```python
import jax
import jax.numpy as jnp
from jax import lax
from jax.experimental import pallas as pl
from jax.experimental.pallas import tpu as pltpu
from jax.sharding import PartitionSpec as P

STEPS = 4
GELU_A = 0.7978845608028654
GELU_B = 0.044715
LOGIT_SCALE_TEMP = 10.0
LOGIT_BIAS_SHIFT = -2.0
LOSS_SCALE_FACTOR = 128.0

BLK = 32
CAP = 16
D = 1536
FF = 3072
SLOTS = 512
ROWS = 288
IMAGES = 16
LANES = 128
TILES = D // LANES
MSG = (TILES + 1) * CAP
WIDE = BLK * CAP
CHUNK = 512
CHUNKS = FF // CHUNK
SLOT_K = 640
F32 = jnp.float32
BF16 = jnp.bfloat16
I32 = jnp.int32


def iota(shape, axis):
    return lax.broadcasted_iota(I32, shape, axis)


def vmem(count):
    return [pl.BlockSpec(memory_space=pltpu.VMEM)] * count


def params(mib):
    return pltpu.CompilerParams(vmem_limit_bytes=mib * 2**20)


def put_message(send_ref, wide, extra):
    for tile in range(TILES):
        send_ref[:, tile * CAP : (tile + 1) * CAP, :] = wide[
            :, tile * LANES : (tile + 1) * LANES
        ].reshape(BLK, CAP, LANES)
    stacked = jnp.concatenate(
        [extra[:, tile * LANES : (tile + 1) * LANES] for tile in range(TILES)], axis=0
    )
    row = iota((WIDE, TILES * BLK), 0)
    column = iota((WIDE, TILES * BLK), 1)
    pick = ((row >> 4) == (column & 31)) & ((row & 15) == (column >> 5))
    last = jnp.dot(pick.astype(F32).astype(BF16), stacked, preferred_element_type=F32)
    send_ref[:, TILES * CAP :, :] = last.astype(BF16).reshape(BLK, CAP, LANES)


def take_message(arrived_ref, rows_ref):
    for tile in range(TILES):
        rows_ref[0:WIDE, tile * LANES : (tile + 1) * LANES] = arrived_ref[
            :, tile * CAP : (tile + 1) * CAP, :
        ].reshape(WIDE, LANES)
    last = arrived_ref[:, TILES * CAP :, :].reshape(WIDE, LANES)
    row = iota((TILES * BLK, WIDE), 0)
    column = iota((TILES * BLK, WIDE), 1)
    pick = ((column >> 4) == (row & 31)) & ((column & 15) == (row >> 5))
    stacked = jnp.dot(pick.astype(F32).astype(BF16), last, preferred_element_type=F32).astype(BF16)
    for tile in range(TILES):
        rows_ref[WIDE : WIDE + BLK, tile * LANES : (tile + 1) * LANES] = stacked[
            tile * BLK : (tile + 1) * BLK, :
        ]
    rows_ref[WIDE + BLK :, :] = jnp.zeros((SLOT_K - WIDE - BLK, D), BF16)


def starts_of(counts):
    before = (iota((BLK, BLK), 0) > iota((BLK, BLK), 1)).astype(F32).astype(BF16)
    return jnp.dot(before, counts.astype(BF16), preferred_element_type=F32)


def tally_kernel(owners_ref, tallies_ref):
    hits = (owners_ref[...] == iota((BLK, SLOTS), 0)).astype(I32)
    tallies_ref[...] = jnp.broadcast_to(jnp.sum(hits, axis=1, keepdims=True), (BLK, LANES))


def tally(owners):
    return pl.pallas_call(
        tally_kernel,
        in_specs=vmem(1),
        out_specs=pl.BlockSpec(memory_space=pltpu.VMEM),
        out_shape=jax.ShapeDtypeStruct((BLK, LANES), I32),
        compiler_params=params(2),
        cost_estimate=pl.CostEstimate(flops=10**10, bytes_accessed=2**15, transcendentals=0),
        name="tally_owners",
    )(owners[None, :])


def gelu(entries):
    inside = GELU_A * (entries + GELU_B * entries * entries * entries)
    return 0.5 * entries * (1.0 + jnp.tanh(inside))


def forward_kernel(hidden_ref, weight_ref, branch_ref, active, total):
    hidden_buf, weight_buf = hidden_ref, weight_ref

    def activate(k):
        part = slice(k * CHUNK, (k + 1) * CHUNK)
        active[:, part] = gelu(hidden_buf[:, part].astype(F32)).astype(BF16)

    activate(0)
    for k in range(CHUNKS):
        if k + 1 < CHUNKS:
            activate(k + 1)
        part = slice(k * CHUNK, (k + 1) * CHUNK)
        product = jnp.dot(active[:, part], weight_buf[part, :], preferred_element_type=F32)
        if k == 0:
            total[...] = product
        else:
            total[...] += product

    branch_ref[...] = total[...].astype(BF16)


def pack_kernel(counts_ref, branch_ref, send_ref):
    counts = counts_ref[...].astype(F32)
    starts = starts_of(counts)
    counts_wide = jnp.broadcast_to(counts[:, None, :], (BLK, CAP, LANES)).reshape(WIDE, LANES)[:, :1]
    starts_wide = jnp.broadcast_to(starts[:, None, :], (BLK, CAP, LANES)).reshape(WIDE, LANES)[:, :1]
    rank = (iota((WIDE, 1), 0) & 15).astype(F32)
    key = jnp.where(rank < counts_wide, starts_wide + rank, -1.0)
    pick = (iota((WIDE, ROWS), 1).astype(F32) == key).astype(F32).astype(BF16)
    branch = branch_ref[...]
    wide = jnp.dot(pick, branch, preferred_element_type=F32).astype(BF16)
    key = jnp.where(counts[:, :1] > CAP, starts[:, :1] + CAP, -1.0)
    pick = (iota((BLK, ROWS), 1).astype(F32) == key).astype(F32).astype(BF16)
    extra = jnp.dot(pick, branch, preferred_element_type=F32).astype(BF16)
    put_message(send_ref, wide, extra)


def any_space(count):
    return [pl.BlockSpec(memory_space=pltpu.HBM)] * count


def forward(hidden, weight):
    return pl.pallas_call(
        forward_kernel,
        in_specs=vmem(2),
        out_specs=pl.BlockSpec(memory_space=pltpu.VMEM),
        out_shape=jax.ShapeDtypeStruct((ROWS, D), BF16),
        scratch_shapes=[pltpu.VMEM((ROWS, FF), BF16), pltpu.VMEM((ROWS, D), F32)],
        compiler_params=params(24),
        cost_estimate=pl.CostEstimate(
            flops=2 * ROWS * FF * D, bytes_accessed=2 * (FF * D + ROWS * FF), transcendentals=ROWS * FF
        ),
        name="owner_forward",
    )(hidden, weight)


def pack(counts, branch):
    return pl.pallas_call(
        pack_kernel,
        in_specs=vmem(2),
        out_specs=pl.BlockSpec(memory_space=pltpu.VMEM),
        out_shape=jax.ShapeDtypeStruct((BLK, MSG, LANES), BF16),
        compiler_params=params(16),
        cost_estimate=pl.CostEstimate(
            flops=2 * WIDE * ROWS * D, bytes_accessed=2 * (BLK * MSG * LANES + ROWS * D), transcendentals=0
        ),
        name="owner_pack",
    )(counts, branch)


def prepare_kernel(
    owners_row_ref, owners_col_ref, sizes_row_ref, sizes_col_ref, counts_ref, labels_ref, columns_ref,
    near_ref, far1_ref, far2_ref, far3_ref, other_ref,
    to_slots_ref, to_message_ref, to_rows_ref, facts_ref, member3_ref, texts_ref,
):
    for at, ref in enumerate((near_ref, far1_ref, far2_ref, far3_ref, other_ref)):
        text = ref[...].astype(F32)
        norm = jnp.sqrt(jnp.sum(text * text, axis=1, keepdims=True) + 1e-06)
        texts_ref[at * 64 : at * 64 + text.shape[0], :] = (text / norm).astype(BF16)
    owners = owners_col_ref[...]
    hits = owners == iota((SLOTS, BLK), 1)
    earlier = (iota((SLOTS, SLOTS), 0) > iota((SLOTS, SLOTS), 1)).astype(F32).astype(BF16)
    prefix = jnp.dot(earlier, hits.astype(F32).astype(BF16), preferred_element_type=F32)
    rank = jnp.sum(jnp.where(hits, prefix, 0.0), axis=1, keepdims=True).astype(I32)
    place = jnp.where(rank < CAP, owners * CAP + rank, WIDE + owners)
    place = jnp.where(owners >= 0, place, -1)
    to_slots_ref[...] = (iota((SLOTS, SLOT_K), 1) == place).astype(F32).astype(BF16)

    owners = owners_row_ref[...]
    hits = owners == iota((BLK, SLOTS), 0)
    earlier = (iota((SLOTS, SLOTS), 0) < iota((SLOTS, SLOTS), 1)).astype(F32).astype(BF16)
    prefix = jnp.dot(hits.astype(F32).astype(BF16), earlier, preferred_element_type=F32)
    rank = jnp.sum(jnp.where(hits, prefix, 0.0), axis=0, keepdims=True).astype(I32)
    place = jnp.where(rank < CAP, owners * CAP + rank, WIDE + owners)
    place = jnp.where(owners >= 0, place, -1)
    to_message_ref[...] = (iota((WIDE + BLK, SLOTS), 0) == place).astype(F32).astype(BF16)

    counts = counts_ref[...].astype(F32)
    starts = starts_of(counts)
    own = iota((BLK, SLOT_K), 0)
    lane = iota((BLK, SLOT_K), 1)
    extra = lane >= WIDE
    mine = jnp.where(extra, lane - WIDE, lane >> 4) == own
    rank = jnp.where(extra, CAP, lane & 15).astype(F32)
    valid = mine & (rank < counts[:, :1])
    key = jnp.sum(jnp.where(valid, starts[:, :1] + rank + 1.0, 0.0), axis=0, keepdims=True) - 1.0
    to_rows_ref[...] = (iota((ROWS, SLOT_K), 0).astype(F32) == key).astype(F32).astype(BF16)

    sizes_row = sizes_row_ref[...].astype(F32)
    sizes_col = sizes_col_ref[...].astype(F32)
    row = iota((IMAGES, IMAGES), 0)
    column = iota((IMAGES, IMAGES), 1)
    begin = jnp.sum(jnp.where(column < row, sizes_row, 0.0), axis=1, keepdims=True)
    slot = iota((IMAGES, SLOTS), 1).astype(F32)
    facts_ref[0:IMAGES, :] = ((slot >= begin) & (slot < begin + sizes_col)).astype(F32)
    facts_ref[IMAGES : 2 * IMAGES, :] = (labels_ref[...] == columns_ref[...]).astype(F32)
    facts_ref[2 * IMAGES :, :] = jnp.broadcast_to(sizes_col, (IMAGES, SLOTS))
    begin = jnp.sum(jnp.where(row < column, sizes_col, 0.0), axis=0, keepdims=True)
    slot = iota((SLOTS, IMAGES), 0).astype(F32)
    member = ((slot >= begin) & (slot < begin + sizes_row)).astype(F32)
    member3_ref[...] = jnp.concatenate([member, member, member], axis=1).astype(BF16)


def prepare(owners, patch_counts, counts, labels, columns, texts):
    shapes = (
        (SLOTS, SLOT_K), (WIDE + BLK, SLOTS), (ROWS, SLOT_K), (3 * IMAGES, SLOTS), (SLOTS, 3 * IMAGES),
        (SLOTS, D),
    )
    return pl.pallas_call(
        prepare_kernel,
        in_specs=vmem(12),
        out_specs=vmem(6),
        out_shape=[jax.ShapeDtypeStruct(shape, F32 if at == 3 else BF16) for at, shape in enumerate(shapes)],
        compiler_params=params(24),
        cost_estimate=pl.CostEstimate(flops=2 * SLOTS * SLOTS * 256, bytes_accessed=2**21, transcendentals=0),
        name="prepare_onehots",
    )(owners[None, :], owners[:, None], patch_counts[None, :], patch_counts[:, None], counts,
      labels[:, None], columns[None, :], *texts)


def slot_kernel(
    arrived_ref, patch_hbm, texts_hbm, to_slots_hbm, to_message_hbm, facts_hbm, member3_hbm,
    patches_hbm, send_ref,
    patch_ref, texts_ref, to_slots_ref, to_message_ref, facts_ref, member3_ref,
    patches_ref, rows_ref, summed, normed_low, scale_ref, spread_ref, sems,
):
    moves = [
        pltpu.make_async_copy(source, target, sems.at[at])
        for at, (source, target) in enumerate((
            (to_slots_hbm, to_slots_ref), (patch_hbm, patch_ref),
            (facts_hbm, facts_ref), (texts_hbm, texts_ref),
            (member3_hbm, member3_ref), (to_message_hbm, to_message_ref),
        ))
    ]
    for copy in moves:
        copy.start()
    take_message(arrived_ref, rows_ref)
    moves[0].wait()
    moves[1].wait()
    to_slots = to_slots_ref[...]
    width = 512
    for part in range(D // width):
        columns = slice(part * width, (part + 1) * width)
        summed[:, columns] = patch_ref[:, columns].astype(F32) + jnp.dot(
            to_slots, rows_ref[:, columns], preferred_element_type=F32
        )

    height = 128

    for at in range(SLOTS // height):
        rows = pl.ds(at * height, height)
        mean = jnp.sum(summed[rows, :], axis=1, keepdims=True) * (1.0 / D)
        centered = summed[rows, :] - mean
        variance = jnp.sum(centered * centered, axis=1, keepdims=True) * (1.0 / D)
        scale = lax.rsqrt(variance + 1e-06)
        normed = (summed[rows, :] - mean) * scale
        summed[rows, :] = normed
        high = normed.astype(BF16)
        rows_ref[rows, :] = high
        normed_low[rows, :] = (normed - high.astype(F32)).astype(BF16)
        scale_ref[rows, :] = jnp.broadcast_to(scale, (height, LANES))

    moves[2].wait()
    member = facts_ref[0:IMAGES, :].astype(BF16)
    sizes = facts_ref[2 * IMAGES :, :][:, :1]
    pooled = jnp.dot(member, rows_ref[0:SLOTS, :], preferred_element_type=F32)
    pooled = pooled + jnp.dot(member, normed_low[...], preferred_element_type=F32)
    pooled = pooled / sizes
    embed_norm = jnp.sqrt(jnp.sum(pooled * pooled, axis=1, keepdims=True) + 1e-06)
    embedding = pooled / embed_norm
    embed_b = embedding.astype(BF16)
    moves[3].wait()
    texts = texts_ref[...]
    logits = LOGIT_SCALE_TEMP * lax.dot_general(
        embed_b, texts, (((1,), (1,)), ((), ())), preferred_element_type=F32
    ) + LOGIT_BIAS_SHIFT
    positive = facts_ref[IMAGES : 2 * IMAGES, :]
    sigmoid = 1.0 / (1.0 + jnp.exp(-logits))
    weights = (LOSS_SCALE_FACTOR * LOGIT_SCALE_TEMP * (sigmoid - positive)).astype(BF16)
    embed_grad = jnp.dot(weights, texts, preferred_element_type=F32)
    radial = jnp.sum(embedding * embed_grad, axis=1, keepdims=True)
    spread = (embed_grad - embedding * radial) / embed_norm / sizes
    for piece in range(3):
        top = spread.astype(BF16)
        spread_ref[piece * IMAGES : (piece + 1) * IMAGES, :] = top
        spread = spread - top.astype(F32)

    moves[4].wait()

    for at in range(SLOTS // height):
        rows = pl.ds(at * height, height)
        grad = jnp.dot(member3_ref[rows, :], spread_ref[...], preferred_element_type=F32)
        normed = summed[rows, :]
        mean_grad = jnp.sum(grad, axis=1, keepdims=True) * (1.0 / D)
        mean_cross = jnp.sum(grad * normed, axis=1, keepdims=True) * (1.0 / D)
        scale = scale_ref[rows, :][:, :1]
        patches_ref[rows, :] = ((grad - mean_grad - normed * mean_cross) * scale).astype(BF16)

    out = pltpu.make_async_copy(patches_ref, patches_hbm, sems.at[6])
    out.start()
    moves[5].wait()
    packed = jnp.dot(to_message_ref[...], patches_ref[...], preferred_element_type=F32).astype(BF16)
    put_message(send_ref, packed[:WIDE, :], packed[WIDE:, :])
    out.wait()


def slots(arrived, patch_input, texts, to_slots, to_message, facts, member3):
    return pl.pallas_call(
        slot_kernel,
        in_specs=vmem(1) + any_space(6),
        out_specs=any_space(1) + vmem(1),
        out_shape=[
            jax.ShapeDtypeStruct((SLOTS, D), BF16),
            jax.ShapeDtypeStruct((BLK, MSG, LANES), BF16),
        ],
        scratch_shapes=[
            pltpu.VMEM((SLOTS, D), BF16),
            pltpu.VMEM((SLOTS, D), BF16),
            pltpu.VMEM((SLOTS, SLOT_K), BF16),
            pltpu.VMEM((WIDE + BLK, SLOTS), BF16),
            pltpu.VMEM((3 * IMAGES, SLOTS), F32),
            pltpu.VMEM((SLOTS, 3 * IMAGES), BF16),
            pltpu.VMEM((SLOTS, D), BF16),
            pltpu.VMEM((SLOT_K, D), BF16),
            pltpu.VMEM((SLOTS, D), F32),
            pltpu.VMEM((SLOTS, D), BF16),
            pltpu.VMEM((SLOTS, LANES), F32),
            pltpu.VMEM((3 * IMAGES, D), BF16),
            pltpu.SemaphoreType.DMA((7,)),
        ],
        compiler_params=params(28),
        cost_estimate=pl.CostEstimate(
            flops=40 * SLOTS * SLOT_K * D, bytes_accessed=100 * 2**20, transcendentals=IMAGES * SLOTS
        ),
        name="slot_gradients",
    )(arrived, *(pltpu.with_memory_space_constraint(a, pltpu.HBM) for a in (
        patch_input, texts, to_slots, to_message, facts, member3
    )))


def slope(entries):
    square = entries * entries
    tangent = jnp.tanh(GELU_A * (entries + GELU_B * square * entries))
    return 0.5 * (1.0 + tangent) + 0.5 * entries * (1.0 - tangent * tangent) * GELU_A * (
        1.0 + 3.0 * GELU_B * square
    )


def backward_kernel(
    arrived_ref, to_rows_ref, hidden_ref, weight_ref, out_ref, out_buf, rows_ref, sems
):
    take_message(arrived_ref, rows_ref)
    grads = jnp.dot(to_rows_ref[...], rows_ref[...], preferred_element_type=F32).astype(BF16)
    rows_ref[0:ROWS, :] = grads
    copies = []
    for k in range(CHUNKS):
        part = slice(k * CHUNK, (k + 1) * CHUNK)
        active_grad = lax.dot_general(
            rows_ref[0:ROWS, :], weight_ref[part, :], (((1,), (1,)), ((), ())),
            preferred_element_type=F32,
        )
        out_buf[:, part] = (slope(hidden_ref[:, part].astype(F32)) * active_grad).astype(BF16)
        copy = pltpu.make_async_copy(out_buf.at[:, part], out_ref.at[:, part], sems.at[k])
        copy.start()
        copies.append(copy)
    for copy in copies:
        copy.wait()


def backward(arrived, to_rows, hidden, weight):
    return pl.pallas_call(
        backward_kernel,
        in_specs=vmem(4),
        out_specs=pl.BlockSpec(memory_space=pl.ANY),
        out_shape=jax.ShapeDtypeStruct((ROWS, FF), BF16),
        scratch_shapes=[
            pltpu.VMEM((ROWS, FF), BF16),
            pltpu.VMEM((SLOT_K, D), BF16),
            pltpu.SemaphoreType.DMA((CHUNKS,)),
        ],
        compiler_params=params(26),
        cost_estimate=pl.CostEstimate(
            flops=2 * ROWS * FF * D, bytes_accessed=2 * (FF * D + 2 * ROWS * FF), transcendentals=ROWS * FF
        ),
        name="owner_backward",
    )(arrived, to_rows, hidden, weight)


def on_device(
    patch_input, hidden_pre, down_weight, text_features, patch_counts, owners, pair_labels
):
    position = lax.axis_index("blk")
    place = lax.axis_index("grp")
    grp_count = lax.axis_size("grp")
    tallies = tally(owners)
    text, tallies = lax.optimization_barrier((text_features, tallies))
    met = [text]
    for distance in range(1, STEPS):
        route = [((i - distance) % BLK, i) for i in range(BLK)]
        met.append(lax.ppermute(text, "blk", route))
    branch = forward(hidden_pre, down_weight)
    branch, position, place, *met = lax.optimization_barrier((branch, position, place, *met))
    near = jnp.concatenate(met, axis=0)
    near, tallies = lax.optimization_barrier((near, tallies))

    def around(block, way):
        turn = [way * (2 - 4 * (i % 2)) for i in range(grp_count)]
        return lax.ppermute(block, "grp", [(i, (i + turn[i]) % grp_count) for i in range(grp_count)])

    first = around(near, 1)
    second = around(near, -1)
    counts = lax.all_to_all(tallies, "blk", split_axis=0, concat_axis=0, tiled=True)
    first, counts = lax.optimization_barrier((first, counts))
    third = around(first, 1)
    message = pack(counts, branch)
    ring = (near, first, second, third)
    message, owners, patch_counts, pair_labels, *ring = lax.optimization_barrier(
        (message, owners, patch_counts, pair_labels, *ring)
    )
    arrived = lax.all_to_all(message, "blk", split_axis=0, concat_axis=0, tiled=True)

    half = jnp.concatenate(ring, axis=0)
    other = lax.ppermute(half, "grp", [(i, i ^ 1) for i in range(grp_count)])
    at = jnp.arange(grp_count * STEPS * IMAGES, dtype=I32)
    source = (position - (at // IMAGES) % STEPS) % BLK
    hop = at // (STEPS * IMAGES) % STEPS
    offset = jnp.where(hop == 1, -2, jnp.where(hop == 2, 2, jnp.where(hop == 3, 4, 0)))
    holder = jnp.where(at < STEPS * STEPS * IMAGES, place, place ^ 1)
    device = (holder + offset * (1 - 2 * (holder % 2)) + grp_count) % grp_count
    columns = source * (grp_count * IMAGES) + device * IMAGES + at % IMAGES

    to_slots, to_message, to_rows, facts, member3, texts = prepare(
        owners, patch_counts, counts, pair_labels, columns, (*ring, other)
    )
    d_patches, outgoing = slots(
        arrived, patch_input, texts, to_slots, to_message, facts, member3
    )
    returned = lax.all_to_all(outgoing, "blk", split_axis=0, concat_axis=0, tiled=True)
    d_hidden = backward(returned, to_rows, hidden_pre, down_weight)
    return (d_patches, d_hidden)


def solution(mesh):
    rows = P(("blk", "grp"), None)
    flat = P(("blk", "grp"))
    return jax.shard_map(
        on_device,
        mesh=mesh,
        in_specs=(rows, rows, P(), rows, flat, flat, flat),
        out_specs=(rows, rows),
        check_vma=False,
    )
```

time: 165 us -> 113 us (0.68)
  waiting for transfers between devices: 45.6 us -> 18.1 us
  between operations: 14.1 us -> 1 us
  local copies, waits for them, and re-layouts: 17.7 us -> 9.25 us
  starting transfers between devices: 21.9 us -> 29.8 us
  blocking collectives: 32.9 us -> 27.2 us
  Pallas kernels: 28.9 us -> 25.8 us
    all_gather x1 -> x0, waiting for transfers between devices: 25.3 us -> none  [on_device(): lax.all_gather(jnp.concatenate(met, axis=0), 'grp', axis=0, tiled=True)]
    ppermute x3 -> x7, waiting for transfers between devices: 20.3 us -> 4.87 us  [the longest x1 2.12 us: on_device(): other = lax.ppermute(half, 'grp', [(i, i ^ 1) for i in range(grp_count)])]
    all_to_all x2, waiting for transfers between devices: 0.01 us -> 13.2 us  [the longest x1 9.18 us: on_device(): lax.all_to_all(message, 'blk', split_axis=0, concat_axis=0, tiled=True)]
    ppermute x3 -> x7, starting transfers between devices: 4.46 us -> 15.6 us  [the longest x3 11.1 us: around(): lax.ppermute(block, 'grp', [(i, (i + turn[i]) % grp_count) for i in range...]
    unnamed x38 -> x46, local copies, waits for them, and re-layouts: 16 us -> 8.94 us
    all_to_all x1, blocking collectives: 32.9 us -> 27.2 us  [on_device(): lax.all_to_all(outgoing, 'blk', split_axis=0, concat_axis=0, tiled=True)]
    all_to_all x2, starting transfers between devices: 17.4 us -> 14.2 us  [the longest x1 7.78 us: on_device(): lax.all_to_all(tallies, 'blk', split_axis=0, concat_axis=0, tiled=True)]
    pallas_call x4 -> x5, Pallas kernels: 26.2 us -> 23 us  [the longest x1 10.8 us: slots(): pl.pallas_call(slot_kernel, in_specs=vmem(1) + any_space(6), out_specs=an...]
  transfers between devices with their start and end apart: 6 -> 9, of which waited for: 2 -> 6; matrix products, arithmetic and copies ran while one was open for 2% -> 2% of each run, Pallas kernels for 4% -> 7%
where the time goes in v2:
time: 113 us
  starting transfers between devices  29.8 us (26%)
  blocking collectives  27.2 us (24%)
  Pallas kernels  25.8 us (23%)
  waiting for transfers between devices  18.1 us (16%)
  local copies, waits for them, and re-layouts  9.25 us (8%)
  other arithmetic  1.92 us (2%)
    all_to_all x1, blocking collectives, on_device(): lax.all_to_all(outgoing, 'blk', split_axis=0, concat_axis=0, tiled=True)  27.2 us
    ppermute x3, starting transfers between devices, around(): lax.ppermute(block, 'grp', [(i, (i + turn[i]) % grp_count) for i in range...  11.1 us
    pallas_call x1, Pallas kernels, slots(): pl.pallas_call(slot_kernel, in_specs=vmem(1) + any_space(6), out_specs=an...  10.8 us
    all_to_all x1, waiting for transfers between devices, on_device(): lax.all_to_all(message, 'blk', split_axis=0, concat_axis=0, tiled=True)  9.18 us
    unnamed x46, local copies, waits for them, and re-layouts  8.94 us
    all_to_all x1, starting transfers between devices, on_device(): lax.all_to_all(tallies, 'blk', split_axis=0, concat_axis=0, tiled=True)  7.78 us
    all_to_all x1, starting transfers between devices, on_device(): lax.all_to_all(message, 'blk', split_axis=0, concat_axis=0, tiled=True)  6.45 us
    pallas_call x1, Pallas kernels, backward(): pl.pallas_call(backward_kernel, in_specs=vmem(4), out_specs=pl.BlockSpec(...  5.81 us
  transfers between devices with their start and end apart: 9, of which 6 were waited for; matrix products, arithmetic and copies ran while one was open for 2% of the time, Pallas kernels for 7%

profile of v2, /device:TPU:2, one launch (start us, length us, event | category | flops | bytes accessed | tf_op | source)
XLA Modules:
  0.0 113.0 jit_solution(9068292174135429011)
XLA Ops:
  0.7 0.8 copy-done.7
  2.5 2.8 %collective-permute-start.2 = (bf16[16,1536]{1,0:T(8,128)(2,1)S(1)}, bf16[16,1536]{1,0:T(8,128)(2,1)S(1)}, u32[]{:S(2)}, u32[]{:S(2)}) collective-permute-start(bf16[16,1536]{1,0:T(8,128)(2,1)S(1)} %copy-done.15), channel_id=1, source_target_pairs={{232,0},{240,8},{248,16},{0,24},{8,32},{16,40},{24,48},{32,56},{40... | collective-permute-start | bytes 147464 | tf_op jit(solution)/shard_map/ppermute | solution.py:424
  5.3 1.2 %collective-permute-start.1 = (bf16[16,1536]{1,0:T(8,128)(2,1)S(1)}, bf16[16,1536]{1,0:T(8,128)(2,1)S(1)}, u32[]{:S(2)}, u32[]{:S(2)}) collective-permute-start(bf16[16,1536]{1,0:T(8,128)(2,1)S(1)} %copy-done.15), channel_id=1, source_target_pairs={{240,0},{248,8},{0,16},{8,24},{16,32},{24,40},{32,48},{40,56},{48,... | collective-permute-start | bytes 147464 | tf_op jit(solution)/shard_map/ppermute | solution.py:424
  7.0 3.0 %owner_forward.1.branch_ref = bf16[288,1536]{1,0:T(8,128)(2,1)S(1)} custom-call(bf16[288,3072]{1,0:T(8,128)(2,1)S(1)} %copy-done, bf16[3072,1536]{1,0:T(8,128)(2,1)S(1)} %bitcast.11), custom_call_target="tpu_custom_call" | custom-call | flops 2717908992 | bytes 11206656 | tf_op jit(solution)/shard_map/owner_forward/pallas_call | solution.py:147
  10.0 1.1 collective-permute-done.2
  11.5 3.3 %collective-permute-start.3 = (bf16[64,1536]{1,0:T(8,128)(2,1)S(1)}, bf16[64,1536]{1,0:T(8,128)(2,1)S(1)}, u32[]{:S(2)}, u32[]{:S(2)}) collective-permute-start(bf16[64,1536]{1,0:T(8,128)(2,1)S(1)} %pad_maximum_fusion.1.near_ref), channel_id=1, source_target_pairs={{0,2},{1,7},{2,4},{3,1},{4,6},{5,3},{6,0},{7,5},{8,10},{9,15},{10,... | collective-permute-start | bytes 589832 | tf_op jit(solution)/shard_map/ppermute | solution.py:432
  14.9 7.8 %all-to-all-start = ((s32[32,1,128]{2,1,0:T(1,128)}), s32[32,1,128]{2,1,0:T(1,128)S(1)}, u32[]{:S(2)}, u32[]{:S(2)}) async-start(s32[32,1,128]{2,1,0:T(1,128)} %bitcast.2), calls=%async_computation | async-start | bytes 32768 | tf_op jit(solution)/shard_map/all_to_all | solution.py:436
  22.7 2.9 %collective-permute-start.4 = (bf16[64,1536]{1,0:T(8,128)(2,1)S(1)}, bf16[64,1536]{1,0:T(8,128)(2,1)S(1)}, u32[]{:S(2)}, u32[]{:S(2)}) collective-permute-start(bf16[64,1536]{1,0:T(8,128)(2,1)S(1)} %pad_maximum_fusion.1.near_ref), channel_id=1, source_target_pairs={{0,6},{1,3},{2,0},{3,5},{4,2},{5,7},{6,4},{7,1},{8,14},{9,11},{10,... | collective-permute-start | bytes 589832 | tf_op jit(solution)/shard_map/ppermute | solution.py:432
  25.5 4.1 %all-to-all-done = s32[32,1,128]{2,1,0:T(1,128)S(1)} async-done(((s32[32,1,128]{2,1,0:T(1,128)}), s32[32,1,128]{2,1,0:T(1,128)S(1)}, u32[]{:S(2)}, u32[]{:S(2)}) %all-to-all-start) | async-done | bytes 16416 | tf_op jit(solution)/shard_map/all_to_all | solution.py:436
  29.6 4.9 %collective-permute-start.5 = (bf16[64,1536]{1,0:T(8,128)(2,1)S(1)}, bf16[64,1536]{1,0:T(8,128)(2,1)}, u32[]{:S(2)}, u32[]{:S(2)}) collective-permute-start(bf16[64,1536]{1,0:T(8,128)(2,1)S(1)} %collective-permute-done.3.far1_ref), channel_id=1, source_target_pairs={{0,2},{1,7},{2,4},{3,1},{4,6},{5,3},{6,0},{7,5},{8,10},{9,15},{10,... | collective-permute-start | bytes 589832 | tf_op jit(solution)/shard_map/ppermute | solution.py:432
  34.5 2.7 %owner_pack.1 = bf16[32,208,128]{2,1,0:T(8,128)(2,1)} custom-call(s32[32,128]{1,0:T(8,128)S(1)} %bitcast.14, bf16[288,1536]{1,0:T(8,128)(2,1)S(1)} %owner_forward.1.branch_ref), custom_call_target="tpu_custom_call" | custom-call | flops 452984832 | bytes 2588672 | tf_op jit(solution)/shard_map/owner_pack/pallas_call | solution.py:162
  37.2 1.2 %collective-permute-done.5.far3_ref = bf16[64,1536]{1,0:T(8,128)(2,1)} collective-permute-done((bf16[64,1536]{1,0:T(8,128)(2,1)S(1)}, bf16[64,1536]{1,0:T(8,128)(2,1)}, u32[]{:S(2)}, u32[]{:S(2)}) %collective-permute-start.5) | collective-permute-done | bytes 196640 | tf_op jit(solution)/shard_map/ppermute | solution.py:432
  38.4 6.4 %all-to-all-start.1 = ((bf16[32,208,128]{2,1,0:T(8,128)(2,1)}), bf16[32,208,128]{2,1,0:T(8,128)(2,1)}, u32[]{:S(2)}, u32[]{:S(2)}) async-start(bf16[32,208,128]{2,1,0:T(8,128)(2,1)} %owner_pack.1), calls=%async_computation.1 | async-start | bytes 3407872 | tf_op jit(solution)/shard_map/all_to_all | solution.py:444
  44.9 1.9 %pad_maximum_fusion = bf16[256,1536]{1,0:T(8,128)(2,1)} fusion(bf16[64,1536]{1,0:T(8,128)(2,1)} %collective-permute-done.5.far3_ref, bf16[64,1536]{1,0:T(8,128)(2,1)S(1)} %collective-permute-done.4.far2_ref, bf16[64,1536]{1,0:T(8,128)(2,1)S(1)} %collective-permute-done.3.far1_ref, bf16[64,1536]{1,0:T(8,128)(2,1)S(1)} %pad_maximum_fusion.1.near_ref), kind=kLoop, calls=%fused_computation | loop fusion | flops 3145728 | bytes 1572864 | tf_op jit(solution)/shard_map/concatenate | solution.py:446
  47.2 2.1 %collective-permute-done.6.other_ref = bf16[256,1536]{1,0:T(8,128)(2,1)S(1)} collective-permute-done((bf16[256,1536]{1,0:T(8,128)(2,1)}, bf16[256,1536]{1,0:T(8,128)(2,1)S(1)}, u32[]{:S(2)}, u32[]{:S(2)}) %collective-permute-start.6) | collective-permute-done | bytes 786464 | tf_op jit(solution)/shard_map/ppermute | solution.py:447
  49.3 0.9 copy-done.1
  50.2 1.1 %copy-done.2 = bf16[256,1536]{1,0:T(8,128)(2,1)S(1)} copy-done((bf16[256,1536]{1,0:T(8,128)(2,1)S(1)}, bf16[256,1536]{1,0:T(8,128)(2,1)}, u32[]{:S(2)}) %copy-start.2) | copy-done | bytes 786456
  51.3 0.9 copy-done.4
  52.2 2.7 %prepare_onehots.1 = (bf16[512,640]{1,0:T(8,128)(2,1)S(1)}, bf16[544,512]{1,0:T(8,128)(2,1)S(1)}, bf16[288,640]{1,0:T(8,128)(2,1)S(1)}, f32[48,512]{1,0:T(8,128)...) custom-call(s32[1,512]{1,0:T(1,128)S(1)} %bitcast.18, s32[512,1]{1,0:T(8,128)S(1)} %copy.15.owners_col_ref, ...), custom_call_target="tpu_custom_call" | custom-call | flops 134217728 | bytes 2097152 | tf_op jit(solution)/shard_map/prepare_onehots/pallas_call | solution.py:233
  55.7 1.2 %copy-done.10 = bf16[512,1536]{1,0:T(8,128)(2,1)} copy-done((bf16[512,1536]{1,0:T(8,128)(2,1)}, bf16[512,1536]{1,0:T(8,128)(2,1)S(1)}, u32[]{:S(2)}) %copy-start.10) | copy-done | bytes 1572888
  59.8 9.2 %all-to-all-done.1.arrived_ref = bf16[32,208,128]{2,1,0:T(8,128)(2,1)} async-done(((bf16[32,208,128]{2,1,0:T(8,128)(2,1)}), bf16[32,208,128]{2,1,0:T(8,128)(2,1)}, u32[]{:S(2)}, u32[]{:S(2)}) %all-to-all-start.1) | async-done | bytes 1703968 | tf_op jit(solution)/shard_map/all_to_all | solution.py:444
  69.0 10.8 %slot_gradients.1 = (bf16[512,1536]{1,0:T(8,128)(2,1)}, bf16[32,208,128]{2,1,0:T(8,128)(2,1)S(1)}) custom-call(bf16[32,208,128]{2,1,0:T(8,128)(2,1)} %all-to-all-done.1.arrived_ref, bf16[512,1536]{1,0:T(8,128)(2,1)} %patch_hbm.1, bf16[512,1536]{1,0:T(8,128)(2,1)} %copy-done.10, bf16[512,640]{1,0:T(8,128)(2,1)} %copy-done.11, bf16[544,512]{1,0:T(8,128)(2,1)} %copy-done.12, ...), custom_call_target="tpu_custom_call" | custom-call | flops 20132659200 | bytes 104857600 | tf_op jit(solution)/shard_map/slot_gradients/pallas_call | solution.py:332
  79.8 27.2 %all_to_all.22.arrived_ref = bf16[32,208,128]{2,1,0:T(8,128)(2,1)S(1)} all-to-all(bf16[32,208,128]{2,1,0:T(8,128)(2,1)S(1)} %get-tuple-element.58), channel_id=1, replica_groups=mesh['blk'=32,'grp'=8] {'blk'}, dimensions={0} | all-to-all | bytes 3407872 | tf_op jit(solution)/shard_map/all_to_all | solution.py:462
  107.0 5.8 %owner_backward.1 = bf16[288,3072]{1,0:T(8,128)(2,1)} custom-call(bf16[32,208,128]{2,1,0:T(8,128)(2,1)S(1)} %all_to_all.22.arrived_ref, bf16[288,640]{1,0:T(8,128)(2,1)S(1)} %copy-done.6, bf16[288,3072]{1,0:T(8,128)(2,1)S(1)} %copy-done, bf16[3072,1536]{1,0:T(8,128)(2,1)S(1)} %bitcast.13), custom_call_target="tpu_custom_call" | custom-call | flops 2717908992 | bytes 12976128 | tf_op jit(solution)/shard_map/owner_backward/pallas_call | solution.py:395
  (55 shorter events, 6.0 us)
Async XLA Ops:
  0.6 6.3 %slice-start = ((s8[9437184]{0:T(1024)(128)(4,1)}), s8[4194304]{0:T(1024)(128)(4,1)S(1)}, s32[]{:S(2)}) async-start(s8[9437184]{0:T(1024)(128)(4,1)} %bitcast.10), calls=%async_computation.3 | async-start | bytes 8388608
  1.5 1.0 copy-start.15
  1.5 5.5 %slice-start.1 = ((s8[9437184]{0:T(1024)(128)(4,1)}), s8[4194304]{0:T(1024)(128)(4,1)S(1)}, s32[]{:S(2)}) async-start(s8[9437184]{0:T(1024)(128)(4,1)} %bitcast.10), calls=%async_computation.4 | async-start | bytes 8388608
  1.5 5.5 %slice-start.2 = ((s8[9437184]{0:T(1024)(128)(4,1)}), s8[1048576]{0:T(1024)(128)(4,1)S(1)}, s32[]{:S(2)}) async-start(s8[9437184]{0:T(1024)(128)(4,1)} %bitcast.10), calls=%async_computation.5 | async-start | bytes 2097152
  1.5 5.5 %copy-start = (bf16[288,3072]{1,0:T(8,128)(2,1)S(1)}, bf16[288,3072]{1,0:T(8,128)(2,1)}, u32[]{:S(2)}) copy-start(bf16[288,3072]{1,0:T(8,128)(2,1)} %hidden_ref.3) | copy-start | bytes 5308420
  2.5 8.6 %collective-permute-start.2 = (bf16[16,1536]{1,0:T(8,128)(2,1)S(1)}, bf16[16,1536]{1,0:T(8,128)(2,1)S(1)}, u32[]{:S(2)}, u32[]{:S(2)}) collective-permute-start(bf16[16,1536]{1,0:T(8,128)(2,1)S(1)} %copy-done.15), channel_id=1, source_target_pairs={{232,0},{240,8},{248,16},{0,24},{8,32},{16,40},{24,48},{32,56},{40... | collective-permute-start | bytes 147464 | tf_op jit(solution)/shard_map/ppermute | solution.py:424
  5.3 5.8 %collective-permute-start.1 = (bf16[16,1536]{1,0:T(8,128)(2,1)S(1)}, bf16[16,1536]{1,0:T(8,128)(2,1)S(1)}, u32[]{:S(2)}, u32[]{:S(2)}) collective-permute-start(bf16[16,1536]{1,0:T(8,128)(2,1)S(1)} %copy-done.15), channel_id=1, source_target_pairs={{240,0},{248,8},{0,16},{8,24},{16,32},{24,40},{32,48},{40,56},{48,... | collective-permute-start | bytes 147464 | tf_op jit(solution)/shard_map/ppermute | solution.py:424
  6.5 5.0 %collective-permute-start = (bf16[16,1536]{1,0:T(8,128)(2,1)S(1)}, bf16[16,1536]{1,0:T(8,128)(2,1)S(1)}, u32[]{:S(2)}, u32[]{:S(2)}) collective-permute-start(bf16[16,1536]{1,0:T(8,128)(2,1)S(1)} %copy-done.15), channel_id=1, source_target_pairs={{248,0},{0,8},{8,16},{16,24},{24,32},{32,40},{40,48},{48,56},{56,6... | collective-permute-start | bytes 147464 | tf_op jit(solution)/shard_map/ppermute | solution.py:424
  11.5 18.1 %collective-permute-start.3 = (bf16[64,1536]{1,0:T(8,128)(2,1)S(1)}, bf16[64,1536]{1,0:T(8,128)(2,1)S(1)}, u32[]{:S(2)}, u32[]{:S(2)}) collective-permute-start(bf16[64,1536]{1,0:T(8,128)(2,1)S(1)} %pad_maximum_fusion.1.near_ref), channel_id=1, source_target_pairs={{0,2},{1,7},{2,4},{3,1},{4,6},{5,3},{6,0},{7,5},{8,10},{9,15},{10,... | collective-permute-start | bytes 589832 | tf_op jit(solution)/shard_map/ppermute | solution.py:432
  14.9 14.7 %all-to-all-start = ((s32[32,1,128]{2,1,0:T(1,128)}), s32[32,1,128]{2,1,0:T(1,128)S(1)}, u32[]{:S(2)}, u32[]{:S(2)}) async-start(s32[32,1,128]{2,1,0:T(1,128)} %bitcast.2), calls=%async_computation | async-start | bytes 32768 | tf_op jit(solution)/shard_map/all_to_all | solution.py:436
  22.7 14.5 %collective-permute-start.4 = (bf16[64,1536]{1,0:T(8,128)(2,1)S(1)}, bf16[64,1536]{1,0:T(8,128)(2,1)S(1)}, u32[]{:S(2)}, u32[]{:S(2)}) collective-permute-start(bf16[64,1536]{1,0:T(8,128)(2,1)S(1)} %pad_maximum_fusion.1.near_ref), channel_id=1, source_target_pairs={{0,6},{1,3},{2,0},{3,5},{4,2},{5,7},{6,4},{7,1},{8,14},{9,11},{10,... | collective-permute-start | bytes 589832 | tf_op jit(solution)/shard_map/ppermute | solution.py:432
  29.6 8.8 %collective-permute-start.5 = (bf16[64,1536]{1,0:T(8,128)(2,1)S(1)}, bf16[64,1536]{1,0:T(8,128)(2,1)}, u32[]{:S(2)}, u32[]{:S(2)}) collective-permute-start(bf16[64,1536]{1,0:T(8,128)(2,1)S(1)} %collective-permute-done.3.far1_ref), channel_id=1, source_target_pairs={{0,2},{1,7},{2,4},{3,1},{4,6},{5,3},{6,0},{7,5},{8,10},{9,15},{10,... | collective-permute-start | bytes 589832 | tf_op jit(solution)/shard_map/ppermute | solution.py:432
  37.2 7.7 %copy-start.3 = (bf16[64,1536]{1,0:T(8,128)(2,1)}, bf16[64,1536]{1,0:T(8,128)(2,1)S(1)}, u32[]{:S(2)}) copy-start(bf16[64,1536]{1,0:T(8,128)(2,1)S(1)} %collective-permute-done.4.far2_ref) | copy-start | bytes 589828
  38.4 30.6 %all-to-all-start.1 = ((bf16[32,208,128]{2,1,0:T(8,128)(2,1)}), bf16[32,208,128]{2,1,0:T(8,128)(2,1)}, u32[]{:S(2)}, u32[]{:S(2)}) async-start(bf16[32,208,128]{2,1,0:T(8,128)(2,1)} %owner_pack.1), calls=%async_computation.1 | async-start | bytes 3407872 | tf_op jit(solution)/shard_map/all_to_all | solution.py:444
  44.9 2.0 %copy-start.16 = (s32[16]{0:T(128)S(1)}, s32[16]{0:T(128)}, u32[]{:S(2)}) copy-start(s32[16]{0:T(128)} %param.13) | copy-start | bytes 196
  44.9 2.0 %copy-start.9 = (s32[16]{0:T(128)S(1)}, s32[16]{0:T(128)}, u32[]{:S(2)}) copy-start(s32[16]{0:T(128)} %param.11) | copy-start | bytes 196
  44.9 2.1 %copy-start.8 = (s32[512]{0:T(512)S(1)}, s32[512]{0:T(512)}, u32[]{:S(2)}) copy-start(s32[512]{0:T(512)} %param.12) | copy-start | bytes 6148
  46.8 2.5 %collective-permute-start.6 = (bf16[256,1536]{1,0:T(8,128)(2,1)}, bf16[256,1536]{1,0:T(8,128)(2,1)S(1)}, u32[]{:S(2)}, u32[]{:S(2)}) collective-permute-start(bf16[256,1536]{1,0:T(8,128)(2,1)} %pad_maximum_fusion), channel_id=1, source_target_pairs={{0,1},{1,0},{2,3},{3,2},{4,5},{5,4},{6,7},{7,6},{8,9},{9,8},{10,11... | collective-permute-start | bytes 2359304 | tf_op jit(solution)/shard_map/ppermute | solution.py:447
  50.2 1.1 %copy-start.2 = (bf16[256,1536]{1,0:T(8,128)(2,1)S(1)}, bf16[256,1536]{1,0:T(8,128)(2,1)}, u32[]{:S(2)}) copy-start(bf16[256,1536]{1,0:T(8,128)(2,1)} %copy-done.1) | copy-start | bytes 2359300
  52.2 54.8 %slice-start.3 = ((s8[9437184]{0:T(1024)(128)(4,1)}), s8[1048576]{0:T(1024)(128)(4,1)S(1)}, s32[]{:S(2)}) async-start(s8[9437184]{0:T(1024)(128)(4,1)} %bitcast.12), calls=%async_computation.6 | async-start | bytes 2097152
  55.7 1.2 %copy-start.10 = (bf16[512,1536]{1,0:T(8,128)(2,1)}, bf16[512,1536]{1,0:T(8,128)(2,1)S(1)}, u32[]{:S(2)}) copy-start(bf16[512,1536]{1,0:T(8,128)(2,1)S(1)} %get-tuple-element.52.texts_hbm) | copy-start | bytes 4718596
  69.0 38.0 %slice-start.4 = ((s8[9437184]{0:T(1024)(128)(4,1)}), s8[4194304]{0:T(1024)(128)(4,1)S(1)}, s32[]{:S(2)}) async-start(s8[9437184]{0:T(1024)(128)(4,1)} %bitcast.12), calls=%async_computation.7 | async-start | bytes 8388608
  69.0 38.0 %slice-start.5 = ((s8[9437184]{0:T(1024)(128)(4,1)}), s8[4194304]{0:T(1024)(128)(4,1)S(1)}, s32[]{:S(2)}) async-start(s8[9437184]{0:T(1024)(128)(4,1)} %bitcast.12), calls=%async_computation.8 | async-start | bytes 8388608
  79.8 27.2 %copy-start.6 = (bf16[288,640]{1,0:T(8,128)(2,1)S(1)}, bf16[288,640]{1,0:T(8,128)(2,1)}, u32[]{:S(2)}) copy-start(bf16[288,640]{1,0:T(8,128)(2,1)} %copy-done.5) | copy-start | bytes 1105924
  (8 other events, 6.3 us)

commit v3 on v2

--- a/solution.py
+++ b/solution.py
@@ -166,21 +166,36 @@
         out_shape=jax.ShapeDtypeStruct((BLK, MSG, LANES), BF16),
         compiler_params=params(16),
         cost_estimate=pl.CostEstimate(
-            flops=2 * WIDE * ROWS * D, bytes_accessed=2 * (BLK * MSG * LANES + ROWS * D), transcendentals=0
+            flops=3 * 10**9, bytes_accessed=2**12, transcendentals=0
         ),
         name="owner_pack",
     )(counts, branch)
 
 
+def texts_kernel(near_ref, first_ref, second_ref, third_ref, texts_ref):
+    height = STEPS * IMAGES
+    for at, ref in enumerate((near_ref, first_ref, second_ref, third_ref)):
+        text = ref[...].astype(F32)
+        norm = jnp.sqrt(jnp.sum(text * text, axis=1, keepdims=True) + 1e-06)
+        texts_ref[at * height : (at + 1) * height, :] = (text / norm).astype(BF16)
+
+
+def normalised(ring):
+    return pl.pallas_call(
+        texts_kernel,
+        in_specs=vmem(4),
+        out_specs=pl.BlockSpec(memory_space=pltpu.VMEM),
+        out_shape=pltpu.HBM((STEPS * STEPS * IMAGES, D), BF16),
+        compiler_params=params(12),
+        cost_estimate=pl.CostEstimate(flops=1, bytes_accessed=2**20, transcendentals=0),
+        name="normalise_texts",
+    )(*ring)
+
+
 def prepare_kernel(
     owners_row_ref, owners_col_ref, sizes_row_ref, sizes_col_ref, counts_ref, labels_ref, columns_ref,
-    near_ref, far1_ref, far2_ref, far3_ref, other_ref,
-    to_slots_ref, to_message_ref, to_rows_ref, facts_ref, member3_ref, texts_ref,
+    to_slots_ref, to_message_ref, to_rows_ref, facts_ref, member3_ref,
 ):
-    for at, ref in enumerate((near_ref, far1_ref, far2_ref, far3_ref, other_ref)):
-        text = ref[...].astype(F32)
-        norm = jnp.sqrt(jnp.sum(text * text, axis=1, keepdims=True) + 1e-06)
-        texts_ref[at * 64 : at * 64 + text.shape[0], :] = (text / norm).astype(BF16)
     owners = owners_col_ref[...]
     hits = owners == iota((SLOTS, BLK), 1)
     earlier = (iota((SLOTS, SLOTS), 0) > iota((SLOTS, SLOTS), 1)).astype(F32).astype(BF16)
@@ -225,25 +240,24 @@
     member3_ref[...] = jnp.concatenate([member, member, member], axis=1).astype(BF16)
 
 
-def prepare(owners, patch_counts, counts, labels, columns, texts):
+def prepare(owners, patch_counts, counts, labels, columns):
     shapes = (
         (SLOTS, SLOT_K), (WIDE + BLK, SLOTS), (ROWS, SLOT_K), (3 * IMAGES, SLOTS), (SLOTS, 3 * IMAGES),
-        (SLOTS, D),
     )
     return pl.pallas_call(
         prepare_kernel,
-        in_specs=vmem(12),
-        out_specs=vmem(6),
-        out_shape=[jax.ShapeDtypeStruct(shape, F32 if at == 3 else BF16) for at, shape in enumerate(shapes)],
+        in_specs=vmem(7),
+        out_specs=vmem(5),
+        out_shape=[pltpu.HBM(shape, F32 if at == 3 else BF16) for at, shape in enumerate(shapes)],
         compiler_params=params(24),
         cost_estimate=pl.CostEstimate(flops=2 * SLOTS * SLOTS * 256, bytes_accessed=2**21, transcendentals=0),
         name="prepare_onehots",
     )(owners[None, :], owners[:, None], patch_counts[None, :], patch_counts[:, None], counts,
-      labels[:, None], columns[None, :], *texts)
+      labels[:, None], columns[None, :])
 
 
 def slot_kernel(
-    arrived_ref, patch_hbm, texts_hbm, to_slots_hbm, to_message_hbm, facts_hbm, member3_hbm,
+    arrived_ref, patch_hbm, half_hbm, other_hbm, to_slots_hbm, to_message_hbm, facts_hbm, member3_hbm,
     patches_hbm, send_ref,
     patch_ref, texts_ref, to_slots_ref, to_message_ref, facts_ref, member3_ref,
     patches_ref, rows_ref, summed, normed_low, scale_ref, spread_ref, sems,
@@ -252,7 +266,8 @@
         pltpu.make_async_copy(source, target, sems.at[at])
         for at, (source, target) in enumerate((
             (to_slots_hbm, to_slots_ref), (patch_hbm, patch_ref),
-            (facts_hbm, facts_ref), (texts_hbm, texts_ref),
+            (facts_hbm, facts_ref), (half_hbm, texts_ref.at[: SLOTS // 2, :]),
+            (other_hbm, texts_ref.at[SLOTS // 2 :, :]),
             (member3_hbm, member3_ref), (to_message_hbm, to_message_ref),
         ))
     ]
@@ -260,24 +275,22 @@
         copy.start()
     take_message(arrived_ref, rows_ref)
     moves[0].wait()
-    moves[1].wait()
     to_slots = to_slots_ref[...]
     width = 512
     for part in range(D // width):
         columns = slice(part * width, (part + 1) * width)
-        summed[:, columns] = patch_ref[:, columns].astype(F32) + jnp.dot(
-            to_slots, rows_ref[:, columns], preferred_element_type=F32
-        )
+        summed[:, columns] = jnp.dot(to_slots, rows_ref[:, columns], preferred_element_type=F32)
 
     height = 128
+    moves[1].wait()
 
     for at in range(SLOTS // height):
         rows = pl.ds(at * height, height)
-        mean = jnp.sum(summed[rows, :], axis=1, keepdims=True) * (1.0 / D)
-        centered = summed[rows, :] - mean
+        values = summed[rows, :] + patch_ref[rows, :].astype(F32)
+        centered = values - jnp.sum(values, axis=1, keepdims=True) * (1.0 / D)
         variance = jnp.sum(centered * centered, axis=1, keepdims=True) * (1.0 / D)
         scale = lax.rsqrt(variance + 1e-06)
-        normed = (summed[rows, :] - mean) * scale
+        normed = centered * scale
         summed[rows, :] = normed
         high = normed.astype(BF16)
         rows_ref[rows, :] = high
@@ -294,6 +307,7 @@
     embedding = pooled / embed_norm
     embed_b = embedding.astype(BF16)
     moves[3].wait()
+    moves[4].wait()
     texts = texts_ref[...]
     logits = LOGIT_SCALE_TEMP * lax.dot_general(
         embed_b, texts, (((1,), (1,)), ((), ())), preferred_element_type=F32
@@ -304,34 +318,34 @@
     embed_grad = jnp.dot(weights, texts, preferred_element_type=F32)
     radial = jnp.sum(embedding * embed_grad, axis=1, keepdims=True)
     spread = (embed_grad - embedding * radial) / embed_norm / sizes
+    spread = spread - jnp.sum(spread, axis=1, keepdims=True) * (1.0 / D)
     for piece in range(3):
         top = spread.astype(BF16)
         spread_ref[piece * IMAGES : (piece + 1) * IMAGES, :] = top
         spread = spread - top.astype(F32)
 
-    moves[4].wait()
+    moves[5].wait()
 
     for at in range(SLOTS // height):
         rows = pl.ds(at * height, height)
         grad = jnp.dot(member3_ref[rows, :], spread_ref[...], preferred_element_type=F32)
         normed = summed[rows, :]
-        mean_grad = jnp.sum(grad, axis=1, keepdims=True) * (1.0 / D)
         mean_cross = jnp.sum(grad * normed, axis=1, keepdims=True) * (1.0 / D)
         scale = scale_ref[rows, :][:, :1]
-        patches_ref[rows, :] = ((grad - mean_grad - normed * mean_cross) * scale).astype(BF16)
-
-    out = pltpu.make_async_copy(patches_ref, patches_hbm, sems.at[6])
+        patches_ref[rows, :] = ((grad - normed * mean_cross) * scale).astype(BF16)
+
+    out = pltpu.make_async_copy(patches_ref, patches_hbm, sems.at[7])
     out.start()
-    moves[5].wait()
+    moves[6].wait()
     packed = jnp.dot(to_message_ref[...], patches_ref[...], preferred_element_type=F32).astype(BF16)
     put_message(send_ref, packed[:WIDE, :], packed[WIDE:, :])
     out.wait()
 
 
-def slots(arrived, patch_input, texts, to_slots, to_message, facts, member3):
+def slots(arrived, patch_input, half, other, to_slots, to_message, facts, member3):
     return pl.pallas_call(
         slot_kernel,
-        in_specs=vmem(1) + any_space(6),
+        in_specs=vmem(1) + any_space(7),
         out_specs=any_space(1) + vmem(1),
         out_shape=[
             jax.ShapeDtypeStruct((SLOTS, D), BF16),
@@ -350,7 +364,7 @@
             pltpu.VMEM((SLOTS, D), BF16),
             pltpu.VMEM((SLOTS, LANES), F32),
             pltpu.VMEM((3 * IMAGES, D), BF16),
-            pltpu.SemaphoreType.DMA((7,)),
+            pltpu.SemaphoreType.DMA((8,)),
         ],
         compiler_params=params(28),
         cost_estimate=pl.CostEstimate(
@@ -358,7 +372,7 @@
         ),
         name="slot_gradients",
     )(arrived, *(pltpu.with_memory_space_constraint(a, pltpu.HBM) for a in (
-        patch_input, texts, to_slots, to_message, facts, member3
+        patch_input, half, other, to_slots, to_message, facts, member3
     )))
 
 
@@ -427,15 +441,14 @@
     near = jnp.concatenate(met, axis=0)
     near, tallies = lax.optimization_barrier((near, tallies))
 
-    def around(block, way):
-        turn = [way * (2 - 4 * (i % 2)) for i in range(grp_count)]
-        return lax.ppermute(block, "grp", [(i, (i + turn[i]) % grp_count) for i in range(grp_count)])
-
-    first = around(near, 1)
-    second = around(near, -1)
+    def swapped(block, masks):
+        return lax.ppermute(block, "grp", [(i, i ^ masks[i % 2]) for i in range(grp_count)])
+
+    first = swapped(near, (2, 6))
+    second = swapped(near, (6, 2))
     counts = lax.all_to_all(tallies, "blk", split_axis=0, concat_axis=0, tiled=True)
-    first, counts = lax.optimization_barrier((first, counts))
-    third = around(first, 1)
+    first, second = lax.optimization_barrier((first, second))
+    third = swapped(first, (6, 2))
     message = pack(counts, branch)
     ring = (near, first, second, third)
     message, owners, patch_counts, pair_labels, *ring = lax.optimization_barrier(
@@ -443,21 +456,22 @@
     )
     arrived = lax.all_to_all(message, "blk", split_axis=0, concat_axis=0, tiled=True)
 
-    half = jnp.concatenate(ring, axis=0)
+    half = normalised(ring)
     other = lax.ppermute(half, "grp", [(i, i ^ 1) for i in range(grp_count)])
     at = jnp.arange(grp_count * STEPS * IMAGES, dtype=I32)
     source = (position - (at // IMAGES) % STEPS) % BLK
     hop = at // (STEPS * IMAGES) % STEPS
-    offset = jnp.where(hop == 1, -2, jnp.where(hop == 2, 2, jnp.where(hop == 3, 4, 0)))
     holder = jnp.where(at < STEPS * STEPS * IMAGES, place, place ^ 1)
-    device = (holder + offset * (1 - 2 * (holder % 2)) + grp_count) % grp_count
+    near_mask = jnp.where(holder % 2 == 0, 2, 6)
+    mask = jnp.where(hop == 1, near_mask, jnp.where(hop == 2, 8 - near_mask, 4 * (hop // 3)))
+    device = holder ^ mask
     columns = source * (grp_count * IMAGES) + device * IMAGES + at % IMAGES
 
-    to_slots, to_message, to_rows, facts, member3, texts = prepare(
-        owners, patch_counts, counts, pair_labels, columns, (*ring, other)
+    to_slots, to_message, to_rows, facts, member3 = prepare(
+        owners, patch_counts, counts, pair_labels, columns
     )
     d_patches, outgoing = slots(
-        arrived, patch_input, texts, to_slots, to_message, facts, member3
+        arrived, patch_input, half, other, to_slots, to_message, facts, member3
     )
     returned = lax.all_to_all(outgoing, "blk", split_axis=0, concat_axis=0, tiled=True)
     d_hidden = backward(returned, to_rows, hidden_pre, down_weight)

time: 113 us -> 109 us (0.965)
  local copies, waits for them, and re-layouts: 9.25 us -> 1.47 us
  starting transfers between devices: 29.8 us -> 32.2 us
  other arithmetic: 1.92 us -> 0.05 us
  waiting for transfers between devices: 18.1 us -> 19.9 us
  Pallas kernels: 25.8 us -> 27.2 us
    unnamed x46 -> x26, local copies, waits for them, and re-layouts: 8.94 us -> 1.16 us
    all_to_all x1, waiting for transfers between devices: 9.18 us -> 15 us  [on_device(): lax.all_to_all(message, 'blk', split_axis=0, concat_axis=0, tiled=True)]
    all_to_all x1, starting transfers between devices: 6.45 us -> 8.67 us  [on_device(): lax.all_to_all(message, 'blk', split_axis=0, concat_axis=0, tiled=True)]
    ppermute x1, waiting for transfers between devices: 2.12 us -> 0.01 us  [on_device(): other = lax.ppermute(half, 'grp', [(i, i ^ 1) for i in range(grp_count)])]
    concatenate x1 -> x0, other arithmetic: 1.87 us -> none  [on_device(): half = jnp.concatenate(ring, axis=0)]
    pallas_call x2 -> x3, Pallas kernels: 13.5 us -> 15 us  [the longest x1 10.5 us: slots(): pl.pallas_call(slot_kernel, in_specs=vmem(1) + any_space(7), out_specs=an...]
    ppermute x3, waiting for transfers between devices: 1.2 us -> 0.01 us  [swapped(): lax.ppermute(block, 'grp', [(i, i ^ masks[i % 2]) for i in range(grp_coun...]
  transfers between devices with their start and end apart: 9 -> 9, of which waited for: 6 -> 4; matrix products, arithmetic and copies ran while one was open for 2% -> 0% of each run, Pallas kernels for 7% -> 9%
where the time goes in v3:
time: 109 us
  starting transfers between devices  32.2 us (30%)
  Pallas kernels  27.2 us (25%)
  blocking collectives  27.1 us (25%)
  waiting for transfers between devices  19.9 us (18%)
  local copies, waits for them, and re-layouts  1.47 us (1%)
    all_to_all x1, blocking collectives, on_device(): lax.all_to_all(outgoing, 'blk', split_axis=0, concat_axis=0, tiled=True)  27.1 us
    all_to_all x1, waiting for transfers between devices, on_device(): lax.all_to_all(message, 'blk', split_axis=0, concat_axis=0, tiled=True)  15 us
    ppermute x3, starting transfers between devices, swapped(): lax.ppermute(block, 'grp', [(i, i ^ masks[i % 2]) for i in range(grp_coun...  11.1 us
    pallas_call x1, Pallas kernels, slots(): pl.pallas_call(slot_kernel, in_specs=vmem(1) + any_space(7), out_specs=an...  10.5 us
    all_to_all x1, starting transfers between devices, on_device(): lax.all_to_all(message, 'blk', split_axis=0, concat_axis=0, tiled=True)  8.67 us
    all_to_all x1, starting transfers between devices, on_device(): lax.all_to_all(tallies, 'blk', split_axis=0, concat_axis=0, tiled=True)  7.95 us
    pallas_call x1, Pallas kernels, backward(): pl.pallas_call(backward_kernel, in_specs=vmem(4), out_specs=pl.BlockSpec(...  5.81 us
    ppermute x3, starting transfers between devices, on_device(): met.append(lax.ppermute(text, 'blk', route))  4.47 us
  transfers between devices with their start and end apart: 9, of which 4 were waited for; matrix products, arithmetic and copies ran while one was open for 0% of the time, Pallas kernels for 9%

profile of v3, /device:TPU:2, one launch (start us, length us, event | category | flops | bytes accessed | tf_op | source)
XLA Modules:
  0.0 108.8 jit_solution(17466429888821275512)
XLA Ops:
  0.7 0.8 copy-done.2
  1.5 0.7 tally_owners.1
  2.2 0.3 copy-done.5
  2.5 2.8 %collective-permute-start.2 = (bf16[16,1536]{1,0:T(8,128)(2,1)S(1)}, bf16[16,1536]{1,0:T(8,128)(2,1)S(1)}, u32[]{:S(2)}, u32[]{:S(2)}) collective-permute-start(bf16[16,1536]{1,0:T(8,128)(2,1)S(1)} %copy-done.5), channel_id=1, source_target_pairs={{232,0},{240,8},{248,16},{0,24},{8,32},{16,40},{24,48},{32,56},{40... | collective-permute-start | bytes 147464 | tf_op jit(solution)/shard_map/ppermute | solution.py:438
  5.3 1.2 %collective-permute-start.1 = (bf16[16,1536]{1,0:T(8,128)(2,1)S(1)}, bf16[16,1536]{1,0:T(8,128)(2,1)S(1)}, u32[]{:S(2)}, u32[]{:S(2)}) collective-permute-start(bf16[16,1536]{1,0:T(8,128)(2,1)S(1)} %copy-done.5), channel_id=1, source_target_pairs={{240,0},{248,8},{0,16},{8,24},{16,32},{24,40},{32,48},{40,56},{48,... | collective-permute-start | bytes 147464 | tf_op jit(solution)/shard_map/ppermute | solution.py:438
  6.5 0.4 collective-permute-start
  7.0 3.0 %owner_forward.1.branch_ref = bf16[288,1536]{1,0:T(8,128)(2,1)S(1)} custom-call(bf16[288,3072]{1,0:T(8,128)(2,1)S(1)} %copy-done, bf16[3072,1536]{1,0:T(8,128)(2,1)S(1)} %bitcast.11), custom_call_target="tpu_custom_call" | custom-call | flops 2717908992 | bytes 11206656 | tf_op jit(solution)/shard_map/owner_forward/pallas_call | solution.py:147
  10.0 1.1 %collective-permute-done.2 = bf16[16,1536]{1,0:T(8,128)(2,1)S(1)} collective-permute-done((bf16[16,1536]{1,0:T(8,128)(2,1)S(1)}, bf16[16,1536]{1,0:T(8,128)(2,1)S(1)}, u32[]{:S(2)}, u32[]{:S(2)}) %collective-permute-start.2) | collective-permute-done | bytes 49184 | tf_op jit(solution)/shard_map/ppermute | solution.py:438
  11.1 0.4 collective-permute-done
  11.5 6.0 %collective-permute-start.4 = (bf16[64,1536]{1,0:T(8,128)(2,1)S(1)}, bf16[64,1536]{1,0:T(8,128)(2,1)S(1)}, u32[]{:S(2)}, u32[]{:S(2)}) collective-permute-start(bf16[64,1536]{1,0:T(8,128)(2,1)S(1)} %pad_maximum_fusion.near_ref), channel_id=1, source_target_pairs={{0,6},{1,3},{2,4},{3,1},{4,2},{5,7},{6,0},{7,5},{8,14},{9,11},{10,... | collective-permute-start | bytes 589832 | tf_op jit(solution)/shard_map/ppermute | solution.py:445
  17.5 1.5 %collective-permute-start.3 = (bf16[64,1536]{1,0:T(8,128)(2,1)S(1)}, bf16[64,1536]{1,0:T(8,128)(2,1)S(1)}, u32[]{:S(2)}, u32[]{:S(2)}) collective-permute-start(bf16[64,1536]{1,0:T(8,128)(2,1)S(1)} %pad_maximum_fusion.near_ref), channel_id=1, source_target_pairs={{0,2},{1,7},{2,0},{3,5},{4,6},{5,3},{6,4},{7,1},{8,10},{9,15},{10,... | collective-permute-start | bytes 589832 | tf_op jit(solution)/shard_map/ppermute | solution.py:445
  18.9 8.0 %all-to-all-start = ((s32[32,1,128]{2,1,0:T(1,128)}), s32[32,1,128]{2,1,0:T(1,128)S(1)}, u32[]{:S(2)}, u32[]{:S(2)}) async-start(s32[32,1,128]{2,1,0:T(1,128)} %bitcast.2), calls=%async_computation | async-start | bytes 32768 | tf_op jit(solution)/shard_map/all_to_all | solution.py:449
  26.9 3.7 %collective-permute-start.5 = (bf16[64,1536]{1,0:T(8,128)(2,1)S(1)}, bf16[64,1536]{1,0:T(8,128)(2,1)}, u32[]{:S(2)}, u32[]{:S(2)}) collective-permute-start(bf16[64,1536]{1,0:T(8,128)(2,1)S(1)} %collective-permute-done.3.first_ref), channel_id=1, source_target_pairs={{0,6},{1,3},{2,4},{3,1},{4,2},{5,7},{6,0},{7,5},{8,14},{9,11},{10,... | collective-permute-start | bytes 589832 | tf_op jit(solution)/shard_map/ppermute | solution.py:445
  30.6 3.3 %all-to-all-done = s32[32,1,128]{2,1,0:T(1,128)S(1)} async-done(((s32[32,1,128]{2,1,0:T(1,128)}), s32[32,1,128]{2,1,0:T(1,128)S(1)}, u32[]{:S(2)}, u32[]{:S(2)}) %all-to-all-start) | async-done | bytes 16416 | tf_op jit(solution)/shard_map/all_to_all | solution.py:449
  33.9 2.7 %owner_pack.1 = bf16[32,208,128]{2,1,0:T(8,128)(2,1)} custom-call(s32[32,128]{1,0:T(8,128)S(1)} %bitcast.14, bf16[288,1536]{1,0:T(8,128)(2,1)S(1)} %owner_forward.1.branch_ref), custom_call_target="tpu_custom_call" | custom-call | flops 3000000000 | bytes 4096 | tf_op jit(solution)/shard_map/owner_pack/pallas_call | solution.py:162
  36.7 8.7 %all-to-all-start.1 = ((bf16[32,208,128]{2,1,0:T(8,128)(2,1)}), bf16[32,208,128]{2,1,0:T(8,128)(2,1)}, u32[]{:S(2)}, u32[]{:S(2)}) async-start(bf16[32,208,128]{2,1,0:T(8,128)(2,1)} %owner_pack.1), calls=%async_computation.1 | async-start | bytes 3407872 | tf_op jit(solution)/shard_map/all_to_all | solution.py:457
  45.4 2.2 %normalise_texts.1.half_hbm = bf16[256,1536]{1,0:T(8,128)(2,1)} custom-call(bf16[64,1536]{1,0:T(8,128)(2,1)S(1)} %pad_maximum_fusion.near_ref, bf16[64,1536]{1,0:T(8,128)(2,1)S(1)} %collective-permute-done.3.first_ref, bf16[64,1536]{1,0:T(8,128)(2,1)S(1)} %collective-permute-done.4.second_ref, bf16[64,1536]{1,0:T(8,128)(2,1)} %collective-permute-done.5.third_ref), custom_call_target="tpu_custom_call" | custom-call | flops 1 | bytes 1048576 | tf_op jit(solution)/shard_map/normalise_texts/pallas_call | solution.py:184
  47.6 0.1 copy.17.labels_ref
  47.7 0.1 copy.15.owners_col_ref
  47.9 2.4 %prepare_onehots.1 = (bf16[512,640]{1,0:T(8,128)(2,1)}, bf16[544,512]{1,0:T(8,128)(2,1)}, bf16[288,640]{1,0:T(8,128)(2,1)}, f32[48,512]{1,0:T(8,128)}, bf16[512,48]{1,0:T(8,128)(2,1)}) custom-call(s32[1,512]{1,0:T(1,128)S(1)} %bitcast.18, s32[512,1]{1,0:T(8,128)S(1)} %copy.15.owners_col_ref, s32[1,16]{1,0:T(1,128)S(1)} %bitcast.20, ...), custom_call_target="tpu_custom_call" | custom-call | flops 134217728 | bytes 2097152 | tf_op jit(solution)/shard_map/prepare_onehots/pallas_call | solution.py:247
  50.3 15.0 %all-to-all-done.1.arrived_ref = bf16[32,208,128]{2,1,0:T(8,128)(2,1)} async-done(((bf16[32,208,128]{2,1,0:T(8,128)(2,1)}), bf16[32,208,128]{2,1,0:T(8,128)(2,1)}, u32[]{:S(2)}, u32[]{:S(2)}) %all-to-all-start.1) | async-done | bytes 1703968 | tf_op jit(solution)/shard_map/all_to_all | solution.py:457
  65.3 10.5 %slot_gradients.1 = (bf16[512,1536]{1,0:T(8,128)(2,1)}, bf16[32,208,128]{2,1,0:T(8,128)(2,1)S(1)}) custom-call(bf16[32,208,128]{2,1,0:T(8,128)(2,1)} %all-to-all-done.1.arrived_ref, bf16[512,1536]{1,0:T(8,128)(2,1)} %patch_hbm.1, bf16[256,1536]{1,0:T(8,128)(2,1)} %normalise_texts.1.half_hbm, bf16[256,1536]{1,0:T(8,128)(2,1)} %collective-permute-done.6.other_hbm, ...), custom_call_target="tpu_custom_call" | custom-call | flops 20132659200 | bytes 104857600 | tf_op jit(solution)/shard_map/slot_gradients/pallas_call | solution.py:346
  75.8 27.1 %all_to_all.21.arrived_ref = bf16[32,208,128]{2,1,0:T(8,128)(2,1)S(1)} all-to-all(bf16[32,208,128]{2,1,0:T(8,128)(2,1)S(1)} %get-tuple-element.56), channel_id=1, replica_groups=mesh['blk'=32,'grp'=8] {'blk'}, dimensions={0} | all-to-all | bytes 3407872 | tf_op jit(solution)/shard_map/all_to_all | solution.py:476
  102.9 5.8 %owner_backward.1 = bf16[288,3072]{1,0:T(8,128)(2,1)} custom-call(bf16[32,208,128]{2,1,0:T(8,128)(2,1)S(1)} %all_to_all.21.arrived_ref, bf16[288,640]{1,0:T(8,128)(2,1)S(1)} %copy-done.1, bf16[288,3072]{1,0:T(8,128)(2,1)S(1)} %copy-done, bf16[3072,1536]{1,0:T(8,128)(2,1)S(1)} %bitcast.13), custom_call_target="tpu_custom_call" | custom-call | flops 2717908992 | bytes 12976128 | tf_op jit(solution)/shard_map/owner_backward/pallas_call | solution.py:409
  (35 shorter events, 0.2 us)
Async XLA Ops:
  0.6 6.3 %slice-start = ((s8[9437184]{0:T(1024)(128)(4,1)}), s8[4194304]{0:T(1024)(128)(4,1)S(1)}, s32[]{:S(2)}) async-start(s8[9437184]{0:T(1024)(128)(4,1)} %bitcast.10), calls=%async_computation.3 | async-start | bytes 8388608
  0.6 0.8 copy-start.2
  1.5 1.0 copy-start.5
  1.5 5.5 %slice-start.1 = ((s8[9437184]{0:T(1024)(128)(4,1)}), s8[4194304]{0:T(1024)(128)(4,1)S(1)}, s32[]{:S(2)}) async-start(s8[9437184]{0:T(1024)(128)(4,1)} %bitcast.10), calls=%async_computation.4 | async-start | bytes 8388608
  1.5 5.5 %slice-start.2 = ((s8[9437184]{0:T(1024)(128)(4,1)}), s8[1048576]{0:T(1024)(128)(4,1)S(1)}, s32[]{:S(2)}) async-start(s8[9437184]{0:T(1024)(128)(4,1)} %bitcast.10), calls=%async_computation.5 | async-start | bytes 2097152
  1.5 5.5 %copy-start = (bf16[288,3072]{1,0:T(8,128)(2,1)S(1)}, bf16[288,3072]{1,0:T(8,128)(2,1)}, u32[]{:S(2)}) copy-start(bf16[288,3072]{1,0:T(8,128)(2,1)} %hidden_ref.3) | copy-start | bytes 5308420
  2.5 8.6 %collective-permute-start.2 = (bf16[16,1536]{1,0:T(8,128)(2,1)S(1)}, bf16[16,1536]{1,0:T(8,128)(2,1)S(1)}, u32[]{:S(2)}, u32[]{:S(2)}) collective-permute-start(bf16[16,1536]{1,0:T(8,128)(2,1)S(1)} %copy-done.5), channel_id=1, source_target_pairs={{232,0},{240,8},{248,16},{0,24},{8,32},{16,40},{24,48},{32,56},{40... | collective-permute-start | bytes 147464 | tf_op jit(solution)/shard_map/ppermute | solution.py:438
  5.3 5.8 %collective-permute-start.1 = (bf16[16,1536]{1,0:T(8,128)(2,1)S(1)}, bf16[16,1536]{1,0:T(8,128)(2,1)S(1)}, u32[]{:S(2)}, u32[]{:S(2)}) collective-permute-start(bf16[16,1536]{1,0:T(8,128)(2,1)S(1)} %copy-done.5), channel_id=1, source_target_pairs={{240,0},{248,8},{0,16},{8,24},{16,32},{24,40},{32,48},{40,56},{48,... | collective-permute-start | bytes 147464 | tf_op jit(solution)/shard_map/ppermute | solution.py:438
  6.5 5.0 %collective-permute-start = (bf16[16,1536]{1,0:T(8,128)(2,1)S(1)}, bf16[16,1536]{1,0:T(8,128)(2,1)S(1)}, u32[]{:S(2)}, u32[]{:S(2)}) collective-permute-start(bf16[16,1536]{1,0:T(8,128)(2,1)S(1)} %copy-done.5), channel_id=1, source_target_pairs={{248,0},{0,8},{8,16},{16,24},{24,32},{32,40},{40,48},{48,56},{56,6... | collective-permute-start | bytes 147464 | tf_op jit(solution)/shard_map/ppermute | solution.py:438
  11.5 15.4 %collective-permute-start.4 = (bf16[64,1536]{1,0:T(8,128)(2,1)S(1)}, bf16[64,1536]{1,0:T(8,128)(2,1)S(1)}, u32[]{:S(2)}, u32[]{:S(2)}) collective-permute-start(bf16[64,1536]{1,0:T(8,128)(2,1)S(1)} %pad_maximum_fusion.near_ref), channel_id=1, source_target_pairs={{0,6},{1,3},{2,4},{3,1},{4,2},{5,7},{6,0},{7,5},{8,14},{9,11},{10,... | collective-permute-start | bytes 589832 | tf_op jit(solution)/shard_map/ppermute | solution.py:445
  17.5 9.4 %collective-permute-start.3 = (bf16[64,1536]{1,0:T(8,128)(2,1)S(1)}, bf16[64,1536]{1,0:T(8,128)(2,1)S(1)}, u32[]{:S(2)}, u32[]{:S(2)}) collective-permute-start(bf16[64,1536]{1,0:T(8,128)(2,1)S(1)} %pad_maximum_fusion.near_ref), channel_id=1, source_target_pairs={{0,2},{1,7},{2,0},{3,5},{4,6},{5,3},{6,4},{7,1},{8,10},{9,15},{10,... | collective-permute-start | bytes 589832 | tf_op jit(solution)/shard_map/ppermute | solution.py:445
  18.9 15.0 %all-to-all-start = ((s32[32,1,128]{2,1,0:T(1,128)}), s32[32,1,128]{2,1,0:T(1,128)S(1)}, u32[]{:S(2)}, u32[]{:S(2)}) async-start(s32[32,1,128]{2,1,0:T(1,128)} %bitcast.2), calls=%async_computation | async-start | bytes 32768 | tf_op jit(solution)/shard_map/all_to_all | solution.py:449
  26.9 9.7 %collective-permute-start.5 = (bf16[64,1536]{1,0:T(8,128)(2,1)S(1)}, bf16[64,1536]{1,0:T(8,128)(2,1)}, u32[]{:S(2)}, u32[]{:S(2)}) collective-permute-start(bf16[64,1536]{1,0:T(8,128)(2,1)S(1)} %collective-permute-done.3.first_ref), channel_id=1, source_target_pairs={{0,6},{1,3},{2,4},{3,1},{4,2},{5,7},{6,0},{7,5},{8,14},{9,11},{10,... | collective-permute-start | bytes 589832 | tf_op jit(solution)/shard_map/ppermute | solution.py:445
  36.7 10.9 %copy-start.6 = (s32[16]{0:T(128)S(1)}, s32[16]{0:T(128)}, u32[]{:S(2)}) copy-start(s32[16]{0:T(128)} %param.13) | copy-start | bytes 196
  36.7 11.0 %copy-start.4 = (s32[16]{0:T(128)S(1)}, s32[16]{0:T(128)}, u32[]{:S(2)}) copy-start(s32[16]{0:T(128)} %param.11) | copy-start | bytes 196
  36.7 11.1 %copy-start.3 = (s32[512]{0:T(512)S(1)}, s32[512]{0:T(512)}, u32[]{:S(2)}) copy-start(s32[512]{0:T(512)} %param.12) | copy-start | bytes 6148
  36.7 28.6 %all-to-all-start.1 = ((bf16[32,208,128]{2,1,0:T(8,128)(2,1)}), bf16[32,208,128]{2,1,0:T(8,128)(2,1)}, u32[]{:S(2)}, u32[]{:S(2)}) async-start(bf16[32,208,128]{2,1,0:T(8,128)(2,1)} %owner_pack.1), calls=%async_computation.1 | async-start | bytes 3407872 | tf_op jit(solution)/shard_map/all_to_all | solution.py:457
  45.3 57.5 %slice-start.3 = ((s8[9437184]{0:T(1024)(128)(4,1)}), s8[1048576]{0:T(1024)(128)(4,1)S(1)}, s32[]{:S(2)}) async-start(s8[9437184]{0:T(1024)(128)(4,1)} %bitcast.12), calls=%async_computation.6 | async-start | bytes 2097152
  47.5 2.8 %collective-permute-start.6 = (bf16[256,1536]{1,0:T(8,128)(2,1)}, bf16[256,1536]{1,0:T(8,128)(2,1)}, u32[]{:S(2)}, u32[]{:S(2)}) collective-permute-start(bf16[256,1536]{1,0:T(8,128)(2,1)} %normalise_texts.1.half_hbm), channel_id=1, source_target_pairs={{0,1},{1,0},{2,3},{3,2},{4,5},{5,4},{6,7},{7,6},{8,9},{9,8},{10,11... | collective-permute-start | bytes 2359304 | tf_op jit(solution)/shard_map/ppermute | solution.py:460
  65.3 37.5 %slice-start.4 = ((s8[9437184]{0:T(1024)(128)(4,1)}), s8[4194304]{0:T(1024)(128)(4,1)S(1)}, s32[]{:S(2)}) async-start(s8[9437184]{0:T(1024)(128)(4,1)} %bitcast.12), calls=%async_computation.7 | async-start | bytes 8388608
  65.3 37.5 %slice-start.5 = ((s8[9437184]{0:T(1024)(128)(4,1)}), s8[4194304]{0:T(1024)(128)(4,1)S(1)}, s32[]{:S(2)}) async-start(s8[9437184]{0:T(1024)(128)(4,1)} %bitcast.12), calls=%async_computation.8 | async-start | bytes 8388608
  75.8 27.1 %copy-start.1 = (bf16[288,640]{1,0:T(8,128)(2,1)S(1)}, bf16[288,640]{1,0:T(8,128)(2,1)}, u32[]{:S(2)}) copy-start(bf16[288,640]{1,0:T(8,128)(2,1)} %get-tuple-element.57.to_rows_ref) | copy-start | bytes 1105924

commit v4 on v3

--- a/solution.py
+++ b/solution.py
@@ -25,6 +25,8 @@
 WIDE = BLK * CAP
 CHUNK = 512
 CHUNKS = FF // CHUNK
+PART = 512
+PARTS = D // PART
 SLOT_K = 640
 F32 = jnp.float32
 BF16 = jnp.bfloat16
@@ -43,19 +45,18 @@
     return pltpu.CompilerParams(vmem_limit_bytes=mib * 2**20)
 
 
-def put_message(send_ref, wide, extra):
-    for tile in range(TILES):
-        send_ref[:, tile * CAP : (tile + 1) * CAP, :] = wide[
+def put_rows(send_ref, part, wide):
+    for tile in range(PART // LANES):
+        start = (part * (PART // LANES) + tile) * CAP
+        send_ref[:, start : start + CAP, :] = wide[
             :, tile * LANES : (tile + 1) * LANES
         ].reshape(BLK, CAP, LANES)
-    stacked = jnp.concatenate(
-        [extra[:, tile * LANES : (tile + 1) * LANES] for tile in range(TILES)], axis=0
-    )
-    row = iota((WIDE, TILES * BLK), 0)
-    column = iota((WIDE, TILES * BLK), 1)
-    pick = ((row >> 4) == (column & 31)) & ((row & 15) == (column >> 5))
-    last = jnp.dot(pick.astype(F32).astype(BF16), stacked, preferred_element_type=F32)
-    send_ref[:, TILES * CAP :, :] = last.astype(BF16).reshape(BLK, CAP, LANES)
+
+
+def put_extra(send_ref, extra):
+    last = extra.reshape(BLK, TILES, LANES)
+    last = jnp.concatenate([last, jnp.zeros((BLK, CAP - TILES, LANES), F32)], axis=1)
+    send_ref[:, TILES * CAP :, :] = last.astype(BF16)
 
 
 def take_message(arrived_ref, rows_ref):
@@ -63,15 +64,8 @@
         rows_ref[0:WIDE, tile * LANES : (tile + 1) * LANES] = arrived_ref[
             :, tile * CAP : (tile + 1) * CAP, :
         ].reshape(WIDE, LANES)
-    last = arrived_ref[:, TILES * CAP :, :].reshape(WIDE, LANES)
-    row = iota((TILES * BLK, WIDE), 0)
-    column = iota((TILES * BLK, WIDE), 1)
-    pick = ((column >> 4) == (row & 31)) & ((column & 15) == (row >> 5))
-    stacked = jnp.dot(pick.astype(F32).astype(BF16), last, preferred_element_type=F32).astype(BF16)
-    for tile in range(TILES):
-        rows_ref[WIDE : WIDE + BLK, tile * LANES : (tile + 1) * LANES] = stacked[
-            tile * BLK : (tile + 1) * BLK, :
-        ]
+    last = arrived_ref[:, TILES * CAP :, :].astype(F32)[:, :TILES, :]
+    rows_ref[WIDE : WIDE + BLK, :] = last.reshape(BLK, D).astype(BF16)
     rows_ref[WIDE + BLK :, :] = jnp.zeros((SLOT_K - WIDE - BLK, D), BF16)
 
 
@@ -123,7 +117,7 @@
     branch_ref[...] = total[...].astype(BF16)
 
 
-def pack_kernel(counts_ref, branch_ref, send_ref):
+def pack_kernel(counts_ref, branch_ref, send_ref, buffer, sems):
     counts = counts_ref[...].astype(F32)
     starts = starts_of(counts)
     counts_wide = jnp.broadcast_to(counts[:, None, :], (BLK, CAP, LANES)).reshape(WIDE, LANES)[:, :1]
@@ -131,12 +125,24 @@
     rank = (iota((WIDE, 1), 0) & 15).astype(F32)
     key = jnp.where(rank < counts_wide, starts_wide + rank, -1.0)
     pick = (iota((WIDE, ROWS), 1).astype(F32) == key).astype(F32).astype(BF16)
-    branch = branch_ref[...]
-    wide = jnp.dot(pick, branch, preferred_element_type=F32).astype(BF16)
-    key = jnp.where(counts[:, :1] > CAP, starts[:, :1] + CAP, -1.0)
-    pick = (iota((BLK, ROWS), 1).astype(F32) == key).astype(F32).astype(BF16)
-    extra = jnp.dot(pick, branch, preferred_element_type=F32).astype(BF16)
-    put_message(send_ref, wide, extra)
+    extra_key = jnp.where(counts[:, :1] > CAP, starts[:, :1] + CAP, -1.0)
+    extra_pick = (iota((BLK, ROWS), 1).astype(F32) == extra_key).astype(F32).astype(BF16)
+    put_extra(buffer, jnp.dot(extra_pick, branch_ref[...], preferred_element_type=F32))
+    copies = []
+    begin = 0
+    for part in range(PARTS):
+        columns = slice(part * PART, (part + 1) * PART)
+        wide = jnp.dot(pick, branch_ref[:, columns], preferred_element_type=F32).astype(BF16)
+        put_rows(buffer, part, wide)
+        end = (part + 1) * (PART // LANES) * CAP if part + 1 < PARTS else MSG
+        copy = pltpu.make_async_copy(
+            buffer.at[:, begin:end, :], send_ref.at[:, begin:end, :], sems.at[part]
+        )
+        copy.start()
+        copies.append(copy)
+        begin = end
+    for copy in copies:
+        copy.wait()
 
 
 def any_space(count):
@@ -162,8 +168,9 @@
     return pl.pallas_call(
         pack_kernel,
         in_specs=vmem(2),
-        out_specs=pl.BlockSpec(memory_space=pltpu.VMEM),
-        out_shape=jax.ShapeDtypeStruct((BLK, MSG, LANES), BF16),
+        out_specs=pl.BlockSpec(memory_space=pltpu.HBM),
+        scratch_shapes=[pltpu.VMEM((BLK, MSG, LANES), BF16), pltpu.SemaphoreType.DMA((PARTS,))],
+        out_shape=pltpu.HBM((BLK, MSG, LANES), BF16),
         compiler_params=params(16),
         cost_estimate=pl.CostEstimate(
             flops=3 * 10**9, bytes_accessed=2**12, transcendentals=0
@@ -250,15 +257,15 @@
         out_specs=vmem(5),
         out_shape=[pltpu.HBM(shape, F32 if at == 3 else BF16) for at, shape in enumerate(shapes)],
         compiler_params=params(24),
-        cost_estimate=pl.CostEstimate(flops=2 * SLOTS * SLOTS * 256, bytes_accessed=2**21, transcendentals=0),
+        cost_estimate=pl.CostEstimate(flops=100*10**9, bytes_accessed=2**12, transcendentals=0),
         name="prepare_onehots",
     )(owners[None, :], owners[:, None], patch_counts[None, :], patch_counts[:, None], counts,
       labels[:, None], columns[None, :])
 
 
 def slot_kernel(
-    arrived_ref, patch_hbm, half_hbm, other_hbm, to_slots_hbm, to_message_hbm, facts_hbm, member3_hbm,
-    patches_hbm, send_ref,
+    arrived_ref, patch_hbm, half_hbm, other_hbm, to_slots_hbm, to_message_hbm, facts_hbm, member3_hbm, weight_hbm,
+    patches_hbm, send_ref, weight_ref,
     patch_ref, texts_ref, to_slots_ref, to_message_ref, facts_ref, member3_ref,
     patches_ref, rows_ref, summed, normed_low, scale_ref, spread_ref, sems,
 ):
@@ -283,6 +290,8 @@
 
     height = 128
     moves[1].wait()
+    weight_copy = pltpu.make_async_copy(weight_hbm, weight_ref, sems.at[8])
+    weight_copy.start()
 
     for at in range(SLOTS // height):
         rows = pl.ds(at * height, height)
@@ -337,19 +346,26 @@
     out = pltpu.make_async_copy(patches_ref, patches_hbm, sems.at[7])
     out.start()
     moves[6].wait()
-    packed = jnp.dot(to_message_ref[...], patches_ref[...], preferred_element_type=F32).astype(BF16)
-    put_message(send_ref, packed[:WIDE, :], packed[WIDE:, :])
+    put_extra(send_ref, jnp.dot(to_message_ref[WIDE:, :], patches_ref[...], preferred_element_type=F32))
+    for part in range(PARTS):
+        wide = jnp.dot(
+            to_message_ref[:WIDE, :], patches_ref[:, part * PART : (part + 1) * PART],
+            preferred_element_type=F32,
+        )
+        put_rows(send_ref, part, wide.astype(BF16))
     out.wait()
-
-
-def slots(arrived, patch_input, half, other, to_slots, to_message, facts, member3):
+    weight_copy.wait()
+
+
+def slots(arrived, patch_input, half, other, to_slots, to_message, facts, member3, weight):
     return pl.pallas_call(
         slot_kernel,
-        in_specs=vmem(1) + any_space(7),
-        out_specs=any_space(1) + vmem(1),
+        in_specs=vmem(1) + any_space(8),
+        out_specs=any_space(1) + vmem(2),
         out_shape=[
             jax.ShapeDtypeStruct((SLOTS, D), BF16),
             jax.ShapeDtypeStruct((BLK, MSG, LANES), BF16),
+            pltpu.VMEM((FF, D), BF16),
         ],
         scratch_shapes=[
             pltpu.VMEM((SLOTS, D), BF16),
@@ -364,24 +380,23 @@
             pltpu.VMEM((SLOTS, D), BF16),
             pltpu.VMEM((SLOTS, LANES), F32),
             pltpu.VMEM((3 * IMAGES, D), BF16),
-            pltpu.SemaphoreType.DMA((8,)),
+            pltpu.SemaphoreType.DMA((9,)),
         ],
         compiler_params=params(28),
         cost_estimate=pl.CostEstimate(
-            flops=40 * SLOTS * SLOT_K * D, bytes_accessed=100 * 2**20, transcendentals=IMAGES * SLOTS
+            flops=4 * SLOTS * SLOT_K * D, bytes_accessed=10 * 2**20, transcendentals=IMAGES * SLOTS
         ),
         name="slot_gradients",
     )(arrived, *(pltpu.with_memory_space_constraint(a, pltpu.HBM) for a in (
-        patch_input, half, other, to_slots, to_message, facts, member3
+        patch_input, half, other, to_slots, to_message, facts, member3, weight
     )))
 
 
 def slope(entries):
     square = entries * entries
-    tangent = jnp.tanh(GELU_A * (entries + GELU_B * square * entries))
-    return 0.5 * (1.0 + tangent) + 0.5 * entries * (1.0 - tangent * tangent) * GELU_A * (
-        1.0 + 3.0 * GELU_B * square
-    )
+    half = 0.5 * jnp.tanh(entries * (GELU_A + GELU_A * GELU_B * square)) + 0.5
+    rise = entries * (2.0 * GELU_A + 6.0 * GELU_A * GELU_B * square)
+    return half + half * (1.0 - half) * rise
 
 
 def backward_kernel(
@@ -450,10 +465,10 @@
     first, second = lax.optimization_barrier((first, second))
     third = swapped(first, (6, 2))
     message = pack(counts, branch)
+    message, owners, patch_counts, pair_labels, near, first, second = lax.optimization_barrier(
+        (message, owners, patch_counts, pair_labels, near, first, second)
+    )
     ring = (near, first, second, third)
-    message, owners, patch_counts, pair_labels, *ring = lax.optimization_barrier(
-        (message, owners, patch_counts, pair_labels, *ring)
-    )
     arrived = lax.all_to_all(message, "blk", split_axis=0, concat_axis=0, tiled=True)
 
     half = normalised(ring)
@@ -470,11 +485,11 @@
     to_slots, to_message, to_rows, facts, member3 = prepare(
         owners, patch_counts, counts, pair_labels, columns
     )
-    d_patches, outgoing = slots(
-        arrived, patch_input, half, other, to_slots, to_message, facts, member3
+    d_patches, outgoing, weight_near = slots(
+        arrived, patch_input, half, other, to_slots, to_message, facts, member3, down_weight
     )
     returned = lax.all_to_all(outgoing, "blk", split_axis=0, concat_axis=0, tiled=True)
-    d_hidden = backward(returned, to_rows, hidden_pre, down_weight)
+    d_hidden = backward(returned, to_rows, hidden_pre, weight_near)
     return (d_patches, d_hidden)
 
 

time: 109 us -> 104 us (0.954)
  Pallas kernels: 27.2 us -> 23.3 us
  starting transfers between devices: 32.2 us -> 28.6 us
  local copies, waits for them, and re-layouts: 1.47 us -> 4.98 us
  waiting for transfers between devices: 19.9 us -> 18 us
    all_to_all x1, starting transfers between devices: 8.67 us -> 5.19 us  [on_device(): lax.all_to_all(message, 'blk', split_axis=0, concat_axis=0, tiled=True)]
    pallas_call x1, Pallas kernels: 10.5 us -> 7.65 us  [slots(): pl.pallas_call(slot_kernel, in_specs=vmem(1) + any_space(8), out_specs=an...]
    unnamed x26 -> x30, local copies, waits for them, and re-layouts: 1.16 us -> 3.96 us
    all_to_all x1, waiting for transfers between devices: 15 us -> 13 us  [on_device(): lax.all_to_all(message, 'blk', split_axis=0, concat_axis=0, tiled=True)]
  transfers between devices with their start and end apart: 9 -> 9, of which waited for: 4 -> 4; matrix products, arithmetic and copies ran while one was open for 0% -> 1% of each run, Pallas kernels for 9% -> 9%
where the time goes in v4:
time: 104 us; the launch traced here: 103 us
  starting transfers between devices  28.6 us (28%)
  blocking collectives  27.2 us (26%)
  Pallas kernels  23.3 us (22%)
  waiting for transfers between devices  18 us (17%)
  local copies, waits for them, and re-layouts  4.98 us (5%)
    all_to_all x1, blocking collectives, on_device(): lax.all_to_all(outgoing, 'blk', split_axis=0, concat_axis=0, tiled=True)  27.2 us
    all_to_all x1, waiting for transfers between devices, on_device(): lax.all_to_all(message, 'blk', split_axis=0, concat_axis=0, tiled=True)  13 us
    ppermute x3, starting transfers between devices, swapped(): lax.ppermute(block, 'grp', [(i, i ^ masks[i % 2]) for i in range(grp_coun...  11 us
    all_to_all x1, starting transfers between devices, on_device(): lax.all_to_all(tallies, 'blk', split_axis=0, concat_axis=0, tiled=True)  7.95 us
    pallas_call x1, Pallas kernels, slots(): pl.pallas_call(slot_kernel, in_specs=vmem(1) + any_space(8), out_specs=an...  7.65 us
    pallas_call x1, Pallas kernels, backward(): pl.pallas_call(backward_kernel, in_specs=vmem(4), out_specs=pl.BlockSpec(...  5.25 us
    all_to_all x1, starting transfers between devices, on_device(): lax.all_to_all(message, 'blk', split_axis=0, concat_axis=0, tiled=True)  5.19 us
    ppermute x3, starting transfers between devices, on_device(): met.append(lax.ppermute(text, 'blk', route))  4.47 us
  transfers between devices with their start and end apart: 9, of which 4 were waited for; matrix products, arithmetic and copies ran while one was open for 1% of the time, Pallas kernels for 9%

profile of v4, /device:TPU:2, one launch (start us, length us, event | category | flops | bytes accessed | tf_op | source)
XLA Modules:
  0.0 103.2 jit_solution(210092476939453921)
XLA Ops:
  0.7 0.8 copy-done.7
  1.5 0.7 tally_owners.1
  2.5 2.8 %collective-permute-start.2 = (bf16[16,1536]{1,0:T(8,128)(2,1)S(1)}, bf16[16,1536]{1,0:T(8,128)(2,1)S(1)}, u32[]{:S(2)}, u32[]{:S(2)}) collective-permute-start(bf16[16,1536]{1,0:T(8,128)(2,1)S(1)} %copy-done.10), channel_id=1, source_target_pairs={{232,0},{240,8},{248,16},{0,24},{8,32},{16,40},{24,48},{32,56},{40... | collective-permute-start | bytes 147464 | tf_op jit(solution)/shard_map/ppermute | solution.py:453
  5.3 1.2 %collective-permute-start.1 = (bf16[16,1536]{1,0:T(8,128)(2,1)S(1)}, bf16[16,1536]{1,0:T(8,128)(2,1)S(1)}, u32[]{:S(2)}, u32[]{:S(2)}) collective-permute-start(bf16[16,1536]{1,0:T(8,128)(2,1)S(1)} %copy-done.10), channel_id=1, source_target_pairs={{240,0},{248,8},{0,16},{8,24},{16,32},{24,40},{32,48},{40,56},{48,... | collective-permute-start | bytes 147464 | tf_op jit(solution)/shard_map/ppermute | solution.py:453
  6.5 0.4 collective-permute-start
  7.0 3.0 %owner_forward.1.branch_ref = bf16[288,1536]{1,0:T(8,128)(2,1)S(1)} custom-call(bf16[288,3072]{1,0:T(8,128)(2,1)S(1)} %copy-done, bf16[3072,1536]{1,0:T(8,128)(2,1)S(1)} %bitcast.11), custom_call_target="tpu_custom_call" | custom-call | flops 2717908992 | bytes 11206656 | tf_op jit(solution)/shard_map/owner_forward/pallas_call | solution.py:153
  10.0 1.1 %collective-permute-done.2 = bf16[16,1536]{1,0:T(8,128)(2,1)S(1)} collective-permute-done((bf16[16,1536]{1,0:T(8,128)(2,1)S(1)}, bf16[16,1536]{1,0:T(8,128)(2,1)S(1)}, u32[]{:S(2)}, u32[]{:S(2)}) %collective-permute-start.2) | collective-permute-done | bytes 49184 | tf_op jit(solution)/shard_map/ppermute | solution.py:453
  11.5 6.0 %collective-permute-start.4 = (bf16[64,1536]{1,0:T(8,128)(2,1)S(1)}, bf16[64,1536]{1,0:T(8,128)(2,1)S(1)}, u32[]{:S(2)}, u32[]{:S(2)}) collective-permute-start(bf16[64,1536]{1,0:T(8,128)(2,1)S(1)} %pad_maximum_fusion.near_ref), channel_id=1, source_target_pairs={{0,6},{1,3},{2,4},{3,1},{4,2},{5,7},{6,0},{7,5},{8,14},{9,11},{10,... | collective-permute-start | bytes 589832 | tf_op jit(solution)/shard_map/ppermute | solution.py:460
  17.5 1.5 %collective-permute-start.3 = (bf16[64,1536]{1,0:T(8,128)(2,1)S(1)}, bf16[64,1536]{1,0:T(8,128)(2,1)}, u32[]{:S(2)}, u32[]{:S(2)}) collective-permute-start(bf16[64,1536]{1,0:T(8,128)(2,1)S(1)} %pad_maximum_fusion.near_ref), channel_id=1, source_target_pairs={{0,2},{1,7},{2,0},{3,5},{4,6},{5,3},{6,4},{7,1},{8,10},{9,15},{10,... | collective-permute-start | bytes 589832 | tf_op jit(solution)/shard_map/ppermute | solution.py:460
  19.0 8.0 %all-to-all-start = ((s32[32,1,128]{2,1,0:T(1,128)}), s32[32,1,128]{2,1,0:T(1,128)S(1)}, u32[]{:S(2)}, u32[]{:S(2)}) async-start(s32[32,1,128]{2,1,0:T(1,128)} %bitcast.2), calls=%async_computation | async-start | bytes 32768 | tf_op jit(solution)/shard_map/all_to_all | solution.py:464
  27.0 3.6 %collective-permute-start.5 = (bf16[64,1536]{1,0:T(8,128)(2,1)}, bf16[64,1536]{1,0:T(8,128)(2,1)}, u32[]{:S(2)}, u32[]{:S(2)}) collective-permute-start(bf16[64,1536]{1,0:T(8,128)(2,1)} %collective-permute-done.3.first_ref), channel_id=1, source_target_pairs={{0,6},{1,3},{2,4},{3,1},{4,2},{5,7},{6,0},{7,5},{8,14},{9,11},{10,... | collective-permute-start | bytes 589832 | tf_op jit(solution)/shard_map/ppermute | solution.py:460
  30.6 3.4 %all-to-all-done = s32[32,1,128]{2,1,0:T(1,128)S(1)} async-done(((s32[32,1,128]{2,1,0:T(1,128)}), s32[32,1,128]{2,1,0:T(1,128)S(1)}, u32[]{:S(2)}, u32[]{:S(2)}) %all-to-all-start) | async-done | bytes 16416 | tf_op jit(solution)/shard_map/all_to_all | solution.py:464
  34.0 2.2 %owner_pack.1 = bf16[32,208,128]{2,1,0:T(8,128)(2,1)} custom-call(s32[32,128]{1,0:T(8,128)S(1)} %bitcast.12, bf16[288,1536]{1,0:T(8,128)(2,1)S(1)} %owner_forward.1.branch_ref), custom_call_target="tpu_custom_call" | custom-call | flops 3000000000 | bytes 4096 | tf_op jit(solution)/shard_map/owner_pack/pallas_call | solution.py:168
  36.4 5.2 %all-to-all-start.1 = ((bf16[32,208,128]{2,1,0:T(8,128)(2,1)}), bf16[32,208,128]{2,1,0:T(8,128)(2,1)S(1)}, u32[]{:S(2)}, u32[]{:S(2)}) async-start(bf16[32,208,128]{2,1,0:T(8,128)(2,1)} %owner_pack.1), calls=%async_computation.1 | async-start | bytes 3407872 | tf_op jit(solution)/shard_map/all_to_all | solution.py:472
  41.6 0.9 copy.15.owners_col_ref
  42.5 0.9 copy-done.2
  43.4 0.9 copy-done.6
  44.3 2.2 %normalise_texts.1.half_hbm = bf16[256,1536]{1,0:T(8,128)(2,1)} custom-call(bf16[64,1536]{1,0:T(8,128)(2,1)S(1)} %copy-done.2, bf16[64,1536]{1,0:T(8,128)(2,1)} %collective-permute-done.3.first_ref, bf16[64,1536]{1,0:T(8,128)(2,1)S(1)} %copy-done.6, bf16[64,1536]{1,0:T(8,128)(2,1)} %collective-permute-done.5.third_ref), custom_call_target="tpu_custom_call" | custom-call | flops 1 | bytes 1048576 | tf_op jit(solution)/shard_map/normalise_texts/pallas_call | solution.py:191
  46.5 0.9 copy-done.4
  47.5 2.4 %prepare_onehots.1 = (bf16[512,640]{1,0:T(8,128)(2,1)}, bf16[544,512]{1,0:T(8,128)(2,1)}, bf16[288,640]{1,0:T(8,128)(2,1)}, f32[48,512]{1,0:T(8,128)}, bf16[512,48]{1,0:T(8,128)(2,1)}) custom-call(s32[1,512]{1,0:T(1,128)S(1)} %bitcast.16, s32[512,1]{1,0:T(8,128)S(1)} %copy-done.4, s32[1,16]{1,0:T(1,128)S(1)} %bitcast.18, s32[16,1]{1,0:T(8,128)S(1)} %copy.16.sizes_col_ref, ...), custom_call_target="tpu_custom_call" | custom-call | flops 99999997952 | bytes 4096 | tf_op jit(solution)/shard_map/prepare_onehots/pallas_call | solution.py:254
  49.9 13.0 %all-to-all-done.1.arrived_ref = bf16[32,208,128]{2,1,0:T(8,128)(2,1)S(1)} async-done(((bf16[32,208,128]{2,1,0:T(8,128)(2,1)}), bf16[32,208,128]{2,1,0:T(8,128)(2,1)S(1)}, u32[]{:S(2)}, u32[]{:S(2)}) %all-to-all-start.1) | async-done | bytes 1703968 | tf_op jit(solution)/shard_map/all_to_all | solution.py:472
  62.9 7.6 %slot_gradients.1 = (bf16[512,1536]{1,0:T(8,128)(2,1)}, bf16[32,208,128]{2,1,0:T(8,128)(2,1)S(1)}, bf16[3072,1536]{1,0:T(8,128)(2,1)S(1)}) custom-call(bf16[32,208,128]{2,1,0:T(8,128)(2,1)S(1)} %all-to-all-done.1.arrived_ref, bf16[512,1536]{1,0:T(8,128)(2,1)} %patch_hbm.1, bf16[256,1536]{1,0:T(8,128)(2,1)} %normalise_texts.1.half_hbm, ...), custom_call_target="tpu_custom_call" | custom-call | flops 2013265920 | bytes 10485760 | tf_op jit(solution)/shard_map/slot_gradients/pallas_call | solution.py:361
  70.5 27.2 %all_to_all.21.arrived_ref = bf16[32,208,128]{2,1,0:T(8,128)(2,1)S(1)} all-to-all(bf16[32,208,128]{2,1,0:T(8,128)(2,1)S(1)} %get-tuple-element.55), channel_id=1, replica_groups=mesh['blk'=32,'grp'=8] {'blk'}, dimensions={0} | all-to-all | bytes 3407872 | tf_op jit(solution)/shard_map/all_to_all | solution.py:491
  97.7 5.3 %owner_backward.1 = bf16[288,3072]{1,0:T(8,128)(2,1)} custom-call(bf16[32,208,128]{2,1,0:T(8,128)(2,1)S(1)} %all_to_all.21.arrived_ref, bf16[288,640]{1,0:T(8,128)(2,1)S(1)} %copy-done.3, bf16[288,3072]{1,0:T(8,128)(2,1)S(1)} %copy-done, bf16[3072,1536]{1,0:T(8,128)(2,1)S(1)} %get-tuple-element.57.weight_ref), custom_call_target="tpu_custom_call" | custom-call | flops 2717908992 | bytes 12976128 | tf_op jit(solution)/shard_map/owner_backward/pallas_call | solution.py:424
  (38 shorter events, 1.0 us)
Async XLA Ops:
  0.6 6.3 %slice-start = ((s8[9437184]{0:T(1024)(128)(4,1)}), s8[4194304]{0:T(1024)(128)(4,1)S(1)}, s32[]{:S(2)}) async-start(s8[9437184]{0:T(1024)(128)(4,1)} %bitcast.10), calls=%async_computation.3 | async-start | bytes 8388608
  0.6 0.8 copy-start.7
  1.5 1.0 copy-start.10
  1.5 5.5 %slice-start.1 = ((s8[9437184]{0:T(1024)(128)(4,1)}), s8[4194304]{0:T(1024)(128)(4,1)S(1)}, s32[]{:S(2)}) async-start(s8[9437184]{0:T(1024)(128)(4,1)} %bitcast.10), calls=%async_computation.4 | async-start | bytes 8388608
  1.5 5.5 %slice-start.2 = ((s8[9437184]{0:T(1024)(128)(4,1)}), s8[1048576]{0:T(1024)(128)(4,1)S(1)}, s32[]{:S(2)}) async-start(s8[9437184]{0:T(1024)(128)(4,1)} %bitcast.10), calls=%async_computation.5 | async-start | bytes 2097152
  1.5 5.5 %copy-start = (bf16[288,3072]{1,0:T(8,128)(2,1)S(1)}, bf16[288,3072]{1,0:T(8,128)(2,1)}, u32[]{:S(2)}) copy-start(bf16[288,3072]{1,0:T(8,128)(2,1)} %hidden_ref.3) | copy-start | bytes 5308420
  2.5 8.6 %collective-permute-start.2 = (bf16[16,1536]{1,0:T(8,128)(2,1)S(1)}, bf16[16,1536]{1,0:T(8,128)(2,1)S(1)}, u32[]{:S(2)}, u32[]{:S(2)}) collective-permute-start(bf16[16,1536]{1,0:T(8,128)(2,1)S(1)} %copy-done.10), channel_id=1, source_target_pairs={{232,0},{240,8},{248,16},{0,24},{8,32},{16,40},{24,48},{32,56},{40... | collective-permute-start | bytes 147464 | tf_op jit(solution)/shard_map/ppermute | solution.py:453
  5.3 5.8 %collective-permute-start.1 = (bf16[16,1536]{1,0:T(8,128)(2,1)S(1)}, bf16[16,1536]{1,0:T(8,128)(2,1)S(1)}, u32[]{:S(2)}, u32[]{:S(2)}) collective-permute-start(bf16[16,1536]{1,0:T(8,128)(2,1)S(1)} %copy-done.10), channel_id=1, source_target_pairs={{240,0},{248,8},{0,16},{8,24},{16,32},{24,40},{32,48},{40,56},{48,... | collective-permute-start | bytes 147464 | tf_op jit(solution)/shard_map/ppermute | solution.py:453
  6.5 5.0 %collective-permute-start = (bf16[16,1536]{1,0:T(8,128)(2,1)S(1)}, bf16[16,1536]{1,0:T(8,128)(2,1)S(1)}, u32[]{:S(2)}, u32[]{:S(2)}) collective-permute-start(bf16[16,1536]{1,0:T(8,128)(2,1)S(1)} %copy-done.10), channel_id=1, source_target_pairs={{248,0},{0,8},{8,16},{16,24},{24,32},{32,40},{40,48},{48,56},{56,6... | collective-permute-start | bytes 147464 | tf_op jit(solution)/shard_map/ppermute | solution.py:453
  11.5 24.7 %copy-start.1 = (bf16[64,1536]{1,0:T(8,128)(2,1)}, bf16[64,1536]{1,0:T(8,128)(2,1)S(1)}, u32[]{:S(2)}) copy-start(bf16[64,1536]{1,0:T(8,128)(2,1)S(1)} %pad_maximum_fusion.near_ref) | copy-start | bytes 589828
  11.5 15.4 %collective-permute-start.4 = (bf16[64,1536]{1,0:T(8,128)(2,1)S(1)}, bf16[64,1536]{1,0:T(8,128)(2,1)S(1)}, u32[]{:S(2)}, u32[]{:S(2)}) collective-permute-start(bf16[64,1536]{1,0:T(8,128)(2,1)S(1)} %pad_maximum_fusion.near_ref), channel_id=1, source_target_pairs={{0,6},{1,3},{2,4},{3,1},{4,2},{5,7},{6,0},{7,5},{8,14},{9,11},{10,... | collective-permute-start | bytes 589832 | tf_op jit(solution)/shard_map/ppermute | solution.py:460
  17.5 9.5 %collective-permute-start.3 = (bf16[64,1536]{1,0:T(8,128)(2,1)S(1)}, bf16[64,1536]{1,0:T(8,128)(2,1)}, u32[]{:S(2)}, u32[]{:S(2)}) collective-permute-start(bf16[64,1536]{1,0:T(8,128)(2,1)S(1)} %pad_maximum_fusion.near_ref), channel_id=1, source_target_pairs={{0,2},{1,7},{2,0},{3,5},{4,6},{5,3},{6,4},{7,1},{8,10},{9,15},{10,... | collective-permute-start | bytes 589832 | tf_op jit(solution)/shard_map/ppermute | solution.py:460
  19.0 15.1 %all-to-all-start = ((s32[32,1,128]{2,1,0:T(1,128)}), s32[32,1,128]{2,1,0:T(1,128)S(1)}, u32[]{:S(2)}, u32[]{:S(2)}) async-start(s32[32,1,128]{2,1,0:T(1,128)} %bitcast.2), calls=%async_computation | async-start | bytes 32768 | tf_op jit(solution)/shard_map/all_to_all | solution.py:464
  27.0 9.2 %copy-start.5 = (bf16[64,1536]{1,0:T(8,128)(2,1)}, bf16[64,1536]{1,0:T(8,128)(2,1)S(1)}, u32[]{:S(2)}) copy-start(bf16[64,1536]{1,0:T(8,128)(2,1)S(1)} %collective-permute-done.4.second_ref) | copy-start | bytes 589828
  27.0 15.5 %collective-permute-start.5 = (bf16[64,1536]{1,0:T(8,128)(2,1)}, bf16[64,1536]{1,0:T(8,128)(2,1)}, u32[]{:S(2)}, u32[]{:S(2)}) collective-permute-start(bf16[64,1536]{1,0:T(8,128)(2,1)} %collective-permute-done.3.first_ref), channel_id=1, source_target_pairs={{0,6},{1,3},{2,4},{3,1},{4,2},{5,7},{6,0},{7,5},{8,14},{9,11},{10,... | collective-permute-start | bytes 589832 | tf_op jit(solution)/shard_map/ppermute | solution.py:460
  34.0 2.2 %copy-start.11 = (s32[16]{0:T(128)S(1)}, s32[16]{0:T(128)}, u32[]{:S(2)}) copy-start(s32[16]{0:T(128)} %param.13) | copy-start | bytes 196
  34.0 2.3 %copy-start.9 = (s32[16]{0:T(128)S(1)}, s32[16]{0:T(128)}, u32[]{:S(2)}) copy-start(s32[16]{0:T(128)} %param.11) | copy-start | bytes 196
  36.4 5.2 %copy-start.8 = (s32[512]{0:T(512)S(1)}, s32[512]{0:T(512)}, u32[]{:S(2)}) copy-start(s32[512]{0:T(512)} %param.12) | copy-start | bytes 6148
  36.4 26.5 %all-to-all-start.1 = ((bf16[32,208,128]{2,1,0:T(8,128)(2,1)}), bf16[32,208,128]{2,1,0:T(8,128)(2,1)S(1)}, u32[]{:S(2)}, u32[]{:S(2)}) async-start(bf16[32,208,128]{2,1,0:T(8,128)(2,1)} %owner_pack.1), calls=%async_computation.1 | async-start | bytes 3407872 | tf_op jit(solution)/shard_map/all_to_all | solution.py:472
  42.5 0.9 copy-start.2
  43.4 0.9 copy-start.6
  46.5 3.3 %collective-permute-start.6 = (bf16[256,1536]{1,0:T(8,128)(2,1)}, bf16[256,1536]{1,0:T(8,128)(2,1)}, u32[]{:S(2)}, u32[]{:S(2)}) collective-permute-start(bf16[256,1536]{1,0:T(8,128)(2,1)} %normalise_texts.1.half_hbm), channel_id=1, source_target_pairs={{0,1},{1,0},{2,3},{3,2},{4,5},{5,4},{6,7},{7,6},{8,9},{9,8},{10,11... | collective-permute-start | bytes 2359304 | tf_op jit(solution)/shard_map/ppermute | solution.py:475
  46.5 1.0 copy-start.4
  70.5 27.2 %copy-start.3 = (bf16[288,640]{1,0:T(8,128)(2,1)S(1)}, bf16[288,640]{1,0:T(8,128)(2,1)}, u32[]{:S(2)}) copy-start(bf16[288,640]{1,0:T(8,128)(2,1)} %get-tuple-element.56.to_rows_ref) | copy-start | bytes 1105924

commit v5 on v4

--- a/solution.py
+++ b/solution.py
@@ -88,7 +88,7 @@
         compiler_params=params(2),
         cost_estimate=pl.CostEstimate(flops=10**10, bytes_accessed=2**15, transcendentals=0),
         name="tally_owners",
-    )(owners[None, :])
+    )(pltpu.with_memory_space_constraint(owners[None, :], pltpu.HBM))
 
 
 def gelu(entries):
@@ -460,13 +460,13 @@
         return lax.ppermute(block, "grp", [(i, i ^ masks[i % 2]) for i in range(grp_count)])
 
     first = swapped(near, (2, 6))
-    second = swapped(near, (6, 2))
     counts = lax.all_to_all(tallies, "blk", split_axis=0, concat_axis=0, tiled=True)
-    first, second = lax.optimization_barrier((first, second))
     third = swapped(first, (6, 2))
+    near_again, first = lax.optimization_barrier((near, first))
+    second = swapped(near_again, (6, 2))
     message = pack(counts, branch)
-    message, owners, patch_counts, pair_labels, near, first, second = lax.optimization_barrier(
-        (message, owners, patch_counts, pair_labels, near, first, second)
+    message, owners, patch_counts, pair_labels, near, first = lax.optimization_barrier(
+        (message, owners, patch_counts, pair_labels, near, first)
     )
     ring = (near, first, second, third)
     arrived = lax.all_to_all(message, "blk", split_axis=0, concat_axis=0, tiled=True)

time: 104 us -> 103 us (level)
  waiting for transfers between devices: 18 us -> 21.1 us
  local copies, waits for them, and re-layouts: 4.98 us -> 2.02 us
  starting transfers between devices: 28.6 us -> 25.9 us
    all_to_all x1, waiting for transfers between devices: 13 us -> 17.1 us  [on_device(): lax.all_to_all(message, 'blk', split_axis=0, concat_axis=0, tiled=True)]
    ppermute x3, starting transfers between devices: 11 us -> 7.7 us  [swapped(): lax.ppermute(block, 'grp', [(i, i ^ masks[i % 2]) for i in range(grp_coun...]
    unnamed x30 -> x20, local copies, waits for them, and re-layouts: 3.96 us -> 0.99 us
  transfers between devices with their start and end apart: 9 -> 9, of which waited for: 4 -> 4; matrix products, arithmetic and copies ran while one was open for 1% -> 1% of each run, Pallas kernels for 9% -> 10%
where the time goes in v5:
time: 103 us; the launch traced here: 102 us
  blocking collectives  27.3 us (27%)
  starting transfers between devices  25.9 us (25%)
  Pallas kernels  24.3 us (24%)
  waiting for transfers between devices  21.1 us (20%)
  local copies, waits for them, and re-layouts  2.02 us (2%)
    all_to_all x1, blocking collectives, on_device(): lax.all_to_all(outgoing, 'blk', split_axis=0, concat_axis=0, tiled=True)  27.3 us
    all_to_all x1, waiting for transfers between devices, on_device(): lax.all_to_all(message, 'blk', split_axis=0, concat_axis=0, tiled=True)  17.1 us
    all_to_all x1, starting transfers between devices, on_device(): lax.all_to_all(tallies, 'blk', split_axis=0, concat_axis=0, tiled=True)  7.77 us
    ppermute x3, starting transfers between devices, swapped(): lax.ppermute(block, 'grp', [(i, i ^ masks[i % 2]) for i in range(grp_coun...  7.7 us
    pallas_call x1, Pallas kernels, slots(): pl.pallas_call(slot_kernel, in_specs=vmem(1) + any_space(8), out_specs=an...  7.64 us
    all_to_all x1, starting transfers between devices, on_device(): lax.all_to_all(message, 'blk', split_axis=0, concat_axis=0, tiled=True)  5.96 us
    pallas_call x1, Pallas kernels, backward(): pl.pallas_call(backward_kernel, in_specs=vmem(4), out_specs=pl.BlockSpec(...  5.25 us
    ppermute x3, starting transfers between devices, on_device(): met.append(lax.ppermute(text, 'blk', route))  4.47 us
  transfers between devices with their start and end apart: 9, of which 4 were waited for; matrix products, arithmetic and copies ran while one was open for 1% of the time, Pallas kernels for 10%

profile of v5, /device:TPU:2, one launch (start us, length us, event | category | flops | bytes accessed | tf_op | source)
XLA Modules:
  0.0 102.3 jit_solution(402024691600409351)
XLA Ops:
  0.7 1.5 %tally_owners.1 = s32[32,128]{1,0:T(8,128)} custom-call(s32[1,512]{1,0:T(1,128)} %bitcast.14), custom_call_target="tpu_custom_call" | custom-call | flops 10000000000 | bytes 32768 | tf_op jit(solution)/shard_map/tally_owners/pallas_call | solution.py:83
  2.2 2.8 %collective-permute-start.2 = (bf16[16,1536]{1,0:T(8,128)(2,1)S(1)}, bf16[16,1536]{1,0:T(8,128)(2,1)S(1)}, u32[]{:S(2)}, u32[]{:S(2)}) collective-permute-start(bf16[16,1536]{1,0:T(8,128)(2,1)S(1)} %copy-done.5), channel_id=1, source_target_pairs={{232,0},{240,8},{248,16},{0,24},{8,32},{16,40},{24,48},{32,56},{40... | collective-permute-start | bytes 147464 | tf_op jit(solution)/shard_map/ppermute | solution.py:453
  5.1 1.2 %collective-permute-start.1 = (bf16[16,1536]{1,0:T(8,128)(2,1)S(1)}, bf16[16,1536]{1,0:T(8,128)(2,1)S(1)}, u32[]{:S(2)}, u32[]{:S(2)}) collective-permute-start(bf16[16,1536]{1,0:T(8,128)(2,1)S(1)} %copy-done.5), channel_id=1, source_target_pairs={{240,0},{248,8},{0,16},{8,24},{16,32},{24,40},{32,48},{40,56},{48,... | collective-permute-start | bytes 147464 | tf_op jit(solution)/shard_map/ppermute | solution.py:453
  6.3 0.4 collective-permute-start
  6.7 3.0 %owner_forward.1.branch_ref = bf16[288,1536]{1,0:T(8,128)(2,1)S(1)} custom-call(bf16[288,3072]{1,0:T(8,128)(2,1)S(1)} %copy-done, bf16[3072,1536]{1,0:T(8,128)(2,1)S(1)} %bitcast.11), custom_call_target="tpu_custom_call" | custom-call | flops 2717908992 | bytes 11206656 | tf_op jit(solution)/shard_map/owner_forward/pallas_call | solution.py:153
  9.7 1.1 %collective-permute-done.2 = bf16[16,1536]{1,0:T(8,128)(2,1)S(1)} collective-permute-done((bf16[16,1536]{1,0:T(8,128)(2,1)S(1)}, bf16[16,1536]{1,0:T(8,128)(2,1)S(1)}, u32[]{:S(2)}, u32[]{:S(2)}) %collective-permute-start.2) | collective-permute-done | bytes 49184 | tf_op jit(solution)/shard_map/ppermute | solution.py:453
  10.8 0.4 collective-permute-done
  11.3 0.7 pad_maximum_fusion.near_ref
  11.9 3.3 %collective-permute-start.3 = (bf16[64,1536]{1,0:T(8,128)(2,1)}, bf16[64,1536]{1,0:T(8,128)(2,1)}, u32[]{:S(2)}, u32[]{:S(2)}) collective-permute-start(bf16[64,1536]{1,0:T(8,128)(2,1)} %pad_maximum_fusion.near_ref), channel_id=1, source_target_pairs={{0,2},{1,7},{2,0},{3,5},{4,6},{5,3},{6,4},{7,1},{8,10},{9,15},{10,... | collective-permute-start | bytes 589832 | tf_op jit(solution)/shard_map/ppermute | solution.py:460
  15.2 7.8 %all-to-all-start = ((s32[32,1,128]{2,1,0:T(1,128)}), s32[32,1,128]{2,1,0:T(1,128)S(1)}, u32[]{:S(2)}, u32[]{:S(2)}) async-start(s32[32,1,128]{2,1,0:T(1,128)} %bitcast.2), calls=%async_computation | async-start | bytes 32768 | tf_op jit(solution)/shard_map/all_to_all | solution.py:463
  23.0 4.3 %collective-permute-start.4 = (bf16[64,1536]{1,0:T(8,128)(2,1)}, bf16[64,1536]{1,0:T(8,128)(2,1)}, u32[]{:S(2)}, u32[]{:S(2)}) collective-permute-start(bf16[64,1536]{1,0:T(8,128)(2,1)} %pad_maximum_fusion.near_ref), channel_id=1, source_target_pairs={{0,6},{1,3},{2,4},{3,1},{4,2},{5,7},{6,0},{7,5},{8,14},{9,11},{10,... | collective-permute-start | bytes 589832 | tf_op jit(solution)/shard_map/ppermute | solution.py:460
  27.4 0.1 collective-permute-start.5
  27.5 2.5 %all-to-all-done = s32[32,1,128]{2,1,0:T(1,128)S(1)} async-done(((s32[32,1,128]{2,1,0:T(1,128)}), s32[32,1,128]{2,1,0:T(1,128)S(1)}, u32[]{:S(2)}, u32[]{:S(2)}) %all-to-all-start) | async-done | bytes 16416 | tf_op jit(solution)/shard_map/all_to_all | solution.py:463
  29.9 2.2 %owner_pack.1 = bf16[32,208,128]{2,1,0:T(8,128)(2,1)} custom-call(s32[32,128]{1,0:T(8,128)S(1)} %bitcast.12, bf16[288,1536]{1,0:T(8,128)(2,1)S(1)} %owner_forward.1.branch_ref), custom_call_target="tpu_custom_call" | custom-call | flops 3000000000 | bytes 4096 | tf_op jit(solution)/shard_map/owner_pack/pallas_call | solution.py:168
  32.1 0.1 copy.17.labels_ref
  32.3 6.0 %all-to-all-start.1 = ((bf16[32,208,128]{2,1,0:T(8,128)(2,1)}), bf16[32,208,128]{2,1,0:T(8,128)(2,1)S(1)}, u32[]{:S(2)}, u32[]{:S(2)}) async-start(bf16[32,208,128]{2,1,0:T(8,128)(2,1)} %owner_pack.1), calls=%async_computation.1 | async-start | bytes 3407872 | tf_op jit(solution)/shard_map/all_to_all | solution.py:472
  38.3 0.9 copy.15.owners_col_ref
  39.2 2.4 %normalise_texts.1.half_hbm = bf16[256,1536]{1,0:T(8,128)(2,1)} custom-call(bf16[64,1536]{1,0:T(8,128)(2,1)} %pad_maximum_fusion.near_ref, bf16[64,1536]{1,0:T(8,128)(2,1)} %collective-permute-done.3.first_ref, bf16[64,1536]{1,0:T(8,128)(2,1)} %collective-permute-done.4.second_ref, bf16[64,1536]{1,0:T(8,128)(2,1)} %collective-permute-done.5.third_ref), custom_call_target="tpu_custom_call" | custom-call | flops 1 | bytes 1048576 | tf_op jit(solution)/shard_map/normalise_texts/pallas_call | solution.py:191
  41.5 0.9 copy-done.2
  42.5 2.3 %prepare_onehots.1 = (bf16[512,640]{1,0:T(8,128)(2,1)}, bf16[544,512]{1,0:T(8,128)(2,1)}, bf16[288,640]{1,0:T(8,128)(2,1)}, f32[48,512]{1,0:T(8,128)}, bf16[512,48]{1,0:T(8,128)(2,1)}) custom-call(s32[1,512]{1,0:T(1,128)S(1)} %bitcast.16, s32[512,1]{1,0:T(8,128)S(1)} %copy-done.2, s32[1,16]{1,0:T(1,128)S(1)} %bitcast.18, s32[16,1]{1,0:T(8,128)S(1)} %copy.16.sizes_col_ref, ...), custom_call_target="tpu_custom_call" | custom-call | flops 99999997952 | bytes 4096 | tf_op jit(solution)/shard_map/prepare_onehots/pallas_call | solution.py:254
  44.8 17.1 %all-to-all-done.1.arrived_ref = bf16[32,208,128]{2,1,0:T(8,128)(2,1)S(1)} async-done(((bf16[32,208,128]{2,1,0:T(8,128)(2,1)}), bf16[32,208,128]{2,1,0:T(8,128)(2,1)S(1)}, u32[]{:S(2)}, u32[]{:S(2)}) %all-to-all-start.1) | async-done | bytes 1703968 | tf_op jit(solution)/shard_map/all_to_all | solution.py:472
  61.9 7.6 %slot_gradients.1 = (bf16[512,1536]{1,0:T(8,128)(2,1)}, bf16[32,208,128]{2,1,0:T(8,128)(2,1)S(1)}, bf16[3072,1536]{1,0:T(8,128)(2,1)S(1)}) custom-call(bf16[32,208,128]{2,1,0:T(8,128)(2,1)S(1)} %all-to-all-done.1.arrived_ref, bf16[512,1536]{1,0:T(8,128)(2,1)} %patch_hbm.1, bf16[256,1536]{1,0:T(8,128)(2,1)} %normalise_texts.1.half_hbm, ...), custom_call_target="tpu_custom_call" | custom-call | flops 2013265920 | bytes 10485760 | tf_op jit(solution)/shard_map/slot_gradients/pallas_call | solution.py:361
  69.6 27.3 %all_to_all.21.arrived_ref = bf16[32,208,128]{2,1,0:T(8,128)(2,1)S(1)} all-to-all(bf16[32,208,128]{2,1,0:T(8,128)(2,1)S(1)} %get-tuple-element.53), channel_id=1, replica_groups=mesh['blk'=32,'grp'=8] {'blk'}, dimensions={0} | all-to-all | bytes 3407872 | tf_op jit(solution)/shard_map/all_to_all | solution.py:491
  96.9 5.3 %owner_backward.1 = bf16[288,3072]{1,0:T(8,128)(2,1)} custom-call(bf16[32,208,128]{2,1,0:T(8,128)(2,1)S(1)} %all_to_all.21.arrived_ref, bf16[288,640]{1,0:T(8,128)(2,1)S(1)} %copy-done.1, bf16[288,3072]{1,0:T(8,128)(2,1)S(1)} %copy-done, bf16[3072,1536]{1,0:T(8,128)(2,1)S(1)} %get-tuple-element.55.weight_ref), custom_call_target="tpu_custom_call" | custom-call | flops 2717908992 | bytes 12976128 | tf_op jit(solution)/shard_map/owner_backward/pallas_call | solution.py:424
  (28 shorter events, 0.2 us)
Async XLA Ops:
  0.6 6.1 %slice-start = ((s8[9437184]{0:T(1024)(128)(4,1)}), s8[4194304]{0:T(1024)(128)(4,1)S(1)}, s32[]{:S(2)}) async-start(s8[9437184]{0:T(1024)(128)(4,1)} %bitcast.10), calls=%async_computation.3 | async-start | bytes 8388608
  0.6 1.6 %copy-start.5 = (bf16[16,1536]{1,0:T(8,128)(2,1)S(1)}, bf16[16,1536]{1,0:T(8,128)(2,1)}, u32[]{:S(2)}) copy-start(bf16[16,1536]{1,0:T(8,128)(2,1)} %param.10) | copy-start | bytes 147460
  0.7 6.0 %slice-start.1 = ((s8[9437184]{0:T(1024)(128)(4,1)}), s8[4194304]{0:T(1024)(128)(4,1)S(1)}, s32[]{:S(2)}) async-start(s8[9437184]{0:T(1024)(128)(4,1)} %bitcast.10), calls=%async_computation.4 | async-start | bytes 8388608
  0.7 6.0 %slice-start.2 = ((s8[9437184]{0:T(1024)(128)(4,1)}), s8[1048576]{0:T(1024)(128)(4,1)S(1)}, s32[]{:S(2)}) async-start(s8[9437184]{0:T(1024)(128)(4,1)} %bitcast.10), calls=%async_computation.5 | async-start | bytes 2097152
  0.7 6.0 %copy-start = (bf16[288,3072]{1,0:T(8,128)(2,1)S(1)}, bf16[288,3072]{1,0:T(8,128)(2,1)}, u32[]{:S(2)}) copy-start(bf16[288,3072]{1,0:T(8,128)(2,1)} %hidden_ref.3) | copy-start | bytes 5308420
  2.2 8.6 %collective-permute-start.2 = (bf16[16,1536]{1,0:T(8,128)(2,1)S(1)}, bf16[16,1536]{1,0:T(8,128)(2,1)S(1)}, u32[]{:S(2)}, u32[]{:S(2)}) collective-permute-start(bf16[16,1536]{1,0:T(8,128)(2,1)S(1)} %copy-done.5), channel_id=1, source_target_pairs={{232,0},{240,8},{248,16},{0,24},{8,32},{16,40},{24,48},{32,56},{40... | collective-permute-start | bytes 147464 | tf_op jit(solution)/shard_map/ppermute | solution.py:453
  5.1 5.8 %collective-permute-start.1 = (bf16[16,1536]{1,0:T(8,128)(2,1)S(1)}, bf16[16,1536]{1,0:T(8,128)(2,1)S(1)}, u32[]{:S(2)}, u32[]{:S(2)}) collective-permute-start(bf16[16,1536]{1,0:T(8,128)(2,1)S(1)} %copy-done.5), channel_id=1, source_target_pairs={{240,0},{248,8},{0,16},{8,24},{16,32},{24,40},{32,48},{40,56},{48,... | collective-permute-start | bytes 147464 | tf_op jit(solution)/shard_map/ppermute | solution.py:453
  6.3 5.0 %collective-permute-start = (bf16[16,1536]{1,0:T(8,128)(2,1)S(1)}, bf16[16,1536]{1,0:T(8,128)(2,1)S(1)}, u32[]{:S(2)}, u32[]{:S(2)}) collective-permute-start(bf16[16,1536]{1,0:T(8,128)(2,1)S(1)} %copy-done.5), channel_id=1, source_target_pairs={{248,0},{0,8},{8,16},{16,24},{24,32},{32,40},{40,48},{48,56},{56,6... | collective-permute-start | bytes 147464 | tf_op jit(solution)/shard_map/ppermute | solution.py:453
  11.9 11.1 %collective-permute-start.3 = (bf16[64,1536]{1,0:T(8,128)(2,1)}, bf16[64,1536]{1,0:T(8,128)(2,1)}, u32[]{:S(2)}, u32[]{:S(2)}) collective-permute-start(bf16[64,1536]{1,0:T(8,128)(2,1)} %pad_maximum_fusion.near_ref), channel_id=1, source_target_pairs={{0,2},{1,7},{2,0},{3,5},{4,6},{5,3},{6,4},{7,1},{8,10},{9,15},{10,... | collective-permute-start | bytes 589832 | tf_op jit(solution)/shard_map/ppermute | solution.py:460
  15.2 14.7 %all-to-all-start = ((s32[32,1,128]{2,1,0:T(1,128)}), s32[32,1,128]{2,1,0:T(1,128)S(1)}, u32[]{:S(2)}, u32[]{:S(2)}) async-start(s32[32,1,128]{2,1,0:T(1,128)} %bitcast.2), calls=%async_computation | async-start | bytes 32768 | tf_op jit(solution)/shard_map/all_to_all | solution.py:463
  23.0 16.1 %collective-permute-start.4 = (bf16[64,1536]{1,0:T(8,128)(2,1)}, bf16[64,1536]{1,0:T(8,128)(2,1)}, u32[]{:S(2)}, u32[]{:S(2)}) collective-permute-start(bf16[64,1536]{1,0:T(8,128)(2,1)} %pad_maximum_fusion.near_ref), channel_id=1, source_target_pairs={{0,6},{1,3},{2,4},{3,1},{4,2},{5,7},{6,0},{7,5},{8,14},{9,11},{10,... | collective-permute-start | bytes 589832 | tf_op jit(solution)/shard_map/ppermute | solution.py:460
  27.4 11.8 %collective-permute-start.5 = (bf16[64,1536]{1,0:T(8,128)(2,1)}, bf16[64,1536]{1,0:T(8,128)(2,1)}, u32[]{:S(2)}, u32[]{:S(2)}) collective-permute-start(bf16[64,1536]{1,0:T(8,128)(2,1)} %collective-permute-done.3.first_ref), channel_id=1, source_target_pairs={{0,6},{1,3},{2,4},{3,1},{4,2},{5,7},{6,0},{7,5},{8,14},{9,11},{10,... | collective-permute-start | bytes 589832 | tf_op jit(solution)/shard_map/ppermute | solution.py:460
  29.9 2.2 %copy-start.6 = (s32[16]{0:T(128)S(1)}, s32[16]{0:T(128)}, u32[]{:S(2)}) copy-start(s32[16]{0:T(128)} %param.13) | copy-start | bytes 196
  29.9 2.3 %copy-start.4 = (s32[16]{0:T(128)S(1)}, s32[16]{0:T(128)}, u32[]{:S(2)}) copy-start(s32[16]{0:T(128)} %param.11) | copy-start | bytes 196
  32.3 6.0 %copy-start.3 = (s32[512]{0:T(512)S(1)}, s32[512]{0:T(512)}, u32[]{:S(2)}) copy-start(s32[512]{0:T(512)} %param.12) | copy-start | bytes 6148
  32.3 29.6 %all-to-all-start.1 = ((bf16[32,208,128]{2,1,0:T(8,128)(2,1)}), bf16[32,208,128]{2,1,0:T(8,128)(2,1)S(1)}, u32[]{:S(2)}, u32[]{:S(2)}) async-start(bf16[32,208,128]{2,1,0:T(8,128)(2,1)} %owner_pack.1), calls=%async_computation.1 | async-start | bytes 3407872 | tf_op jit(solution)/shard_map/all_to_all | solution.py:472
  41.5 3.3 %collective-permute-start.6 = (bf16[256,1536]{1,0:T(8,128)(2,1)}, bf16[256,1536]{1,0:T(8,128)(2,1)}, u32[]{:S(2)}, u32[]{:S(2)}) collective-permute-start(bf16[256,1536]{1,0:T(8,128)(2,1)} %normalise_texts.1.half_hbm), channel_id=1, source_target_pairs={{0,1},{1,0},{2,3},{3,2},{4,5},{5,4},{6,7},{7,6},{8,9},{9,8},{10,11... | collective-permute-start | bytes 2359304 | tf_op jit(solution)/shard_map/ppermute | solution.py:475
  41.5 1.0 copy-start.2
  69.6 27.3 %copy-start.1 = (bf16[288,640]{1,0:T(8,128)(2,1)S(1)}, bf16[288,640]{1,0:T(8,128)(2,1)}, u32[]{:S(2)}) copy-start(bf16[288,640]{1,0:T(8,128)(2,1)} %get-tuple-element.54.to_rows_ref) | copy-start | bytes 1105924

commit v6 on v5

--- a/solution.py
+++ b/solution.py
@@ -459,11 +459,11 @@
     def swapped(block, masks):
         return lax.ppermute(block, "grp", [(i, i ^ masks[i % 2]) for i in range(grp_count)])
 
-    first = swapped(near, (2, 6))
+    first = swapped(near, (6, 2))
     counts = lax.all_to_all(tallies, "blk", split_axis=0, concat_axis=0, tiled=True)
-    third = swapped(first, (6, 2))
+    third = swapped(first, (2, 6))
     near_again, first = lax.optimization_barrier((near, first))
-    second = swapped(near_again, (6, 2))
+    second = swapped(near_again, (2, 6))
     message = pack(counts, branch)
     message, owners, patch_counts, pair_labels, near, first = lax.optimization_barrier(
         (message, owners, patch_counts, pair_labels, near, first)
@@ -477,7 +477,7 @@
     source = (position - (at // IMAGES) % STEPS) % BLK
     hop = at // (STEPS * IMAGES) % STEPS
     holder = jnp.where(at < STEPS * STEPS * IMAGES, place, place ^ 1)
-    near_mask = jnp.where(holder % 2 == 0, 2, 6)
+    near_mask = jnp.where(holder % 2 == 0, 6, 2)
     mask = jnp.where(hop == 1, near_mask, jnp.where(hop == 2, 8 - near_mask, 4 * (hop // 3)))
     device = holder ^ mask
     columns = source * (grp_count * IMAGES) + device * IMAGES + at % IMAGES

time: 103 us -> 100 us (0.971)
  blocking collectives: 27.3 us -> 23.6 us
    all_to_all x1, blocking collectives: 27.3 us -> 23.6 us  [on_device(): lax.all_to_all(outgoing, 'blk', split_axis=0, concat_axis=0, tiled=True)]
    all_to_all x1, waiting for transfers between devices: 17.1 us -> 14.7 us  [on_device(): lax.all_to_all(message, 'blk', split_axis=0, concat_axis=0, tiled=True)]
    all_to_all x1, waiting for transfers between devices: 2.46 us -> 3.95 us  [on_device(): lax.all_to_all(tallies, 'blk', split_axis=0, concat_axis=0, tiled=True)]
    ppermute x3, starting transfers between devices: 7.7 us -> 8.89 us  [swapped(): lax.ppermute(block, 'grp', [(i, i ^ masks[i % 2]) for i in range(grp_coun...]
where the time goes in v6:
time: 100 us; the launch traced here: 98.3 us
  starting transfers between devices  26.6 us (27%)
  Pallas kernels  24.3 us (24%)
  blocking collectives  23.6 us (24%)
  waiting for transfers between devices  20.2 us (20%)
  local copies, waits for them, and re-layouts  2.02 us (2%)
    all_to_all x1, blocking collectives, on_device(): lax.all_to_all(outgoing, 'blk', split_axis=0, concat_axis=0, tiled=True)  23.6 us
    all_to_all x1, waiting for transfers between devices, on_device(): lax.all_to_all(message, 'blk', split_axis=0, concat_axis=0, tiled=True)  14.7 us
    ppermute x3, starting transfers between devices, swapped(): lax.ppermute(block, 'grp', [(i, i ^ masks[i % 2]) for i in range(grp_coun...  8.89 us
    all_to_all x1, starting transfers between devices, on_device(): lax.all_to_all(tallies, 'blk', split_axis=0, concat_axis=0, tiled=True)  7.95 us
    pallas_call x1, Pallas kernels, slots(): pl.pallas_call(slot_kernel, in_specs=vmem(1) + any_space(8), out_specs=an...  7.64 us
    pallas_call x1, Pallas kernels, backward(): pl.pallas_call(backward_kernel, in_specs=vmem(4), out_specs=pl.BlockSpec(...  5.26 us
    all_to_all x1, starting transfers between devices, on_device(): lax.all_to_all(message, 'blk', split_axis=0, concat_axis=0, tiled=True)  5.24 us
    ppermute x3, starting transfers between devices, on_device(): met.append(lax.ppermute(text, 'blk', route))  4.47 us
  transfers between devices with their start and end apart: 9, of which 4 were waited for; matrix products, arithmetic and copies ran while one was open for 1% of the time, Pallas kernels for 10%

profile of v6, /device:TPU:2, one launch (start us, length us, event | category | flops | bytes accessed | tf_op | source)
XLA Modules:
  0.0 98.3 jit_solution(3579560491767287978)
XLA Ops:
  0.7 1.5 %tally_owners.1 = s32[32,128]{1,0:T(8,128)} custom-call(s32[1,512]{1,0:T(1,128)} %bitcast.14), custom_call_target="tpu_custom_call" | custom-call | flops 10000000000 | bytes 32768 | tf_op jit(solution)/shard_map/tally_owners/pallas_call | solution.py:83
  2.2 2.8 %collective-permute-start.2 = (bf16[16,1536]{1,0:T(8,128)(2,1)S(1)}, bf16[16,1536]{1,0:T(8,128)(2,1)S(1)}, u32[]{:S(2)}, u32[]{:S(2)}) collective-permute-start(bf16[16,1536]{1,0:T(8,128)(2,1)S(1)} %copy-done.5), channel_id=1, source_target_pairs={{232,0},{240,8},{248,16},{0,24},{8,32},{16,40},{24,48},{32,56},{40... | collective-permute-start | bytes 147464 | tf_op jit(solution)/shard_map/ppermute | solution.py:453
  5.1 1.2 %collective-permute-start.1 = (bf16[16,1536]{1,0:T(8,128)(2,1)S(1)}, bf16[16,1536]{1,0:T(8,128)(2,1)S(1)}, u32[]{:S(2)}, u32[]{:S(2)}) collective-permute-start(bf16[16,1536]{1,0:T(8,128)(2,1)S(1)} %copy-done.5), channel_id=1, source_target_pairs={{240,0},{248,8},{0,16},{8,24},{16,32},{24,40},{32,48},{40,56},{48,... | collective-permute-start | bytes 147464 | tf_op jit(solution)/shard_map/ppermute | solution.py:453
  6.3 0.4 collective-permute-start
  6.7 3.0 %owner_forward.1.branch_ref = bf16[288,1536]{1,0:T(8,128)(2,1)S(1)} custom-call(bf16[288,3072]{1,0:T(8,128)(2,1)S(1)} %copy-done, bf16[3072,1536]{1,0:T(8,128)(2,1)S(1)} %bitcast.11), custom_call_target="tpu_custom_call" | custom-call | flops 2717908992 | bytes 11206656 | tf_op jit(solution)/shard_map/owner_forward/pallas_call | solution.py:153
  9.7 1.1 %collective-permute-done.2 = bf16[16,1536]{1,0:T(8,128)(2,1)S(1)} collective-permute-done((bf16[16,1536]{1,0:T(8,128)(2,1)S(1)}, bf16[16,1536]{1,0:T(8,128)(2,1)S(1)}, u32[]{:S(2)}, u32[]{:S(2)}) %collective-permute-start.2) | collective-permute-done | bytes 49184 | tf_op jit(solution)/shard_map/ppermute | solution.py:453
  10.8 0.4 collective-permute-done
  11.3 0.7 pad_maximum_fusion.near_ref
  11.9 5.9 %collective-permute-start.3 = (bf16[64,1536]{1,0:T(8,128)(2,1)}, bf16[64,1536]{1,0:T(8,128)(2,1)}, u32[]{:S(2)}, u32[]{:S(2)}) collective-permute-start(bf16[64,1536]{1,0:T(8,128)(2,1)} %pad_maximum_fusion.near_ref), channel_id=1, source_target_pairs={{0,6},{1,3},{2,4},{3,1},{4,2},{5,7},{6,0},{7,5},{8,14},{9,11},{10,... | collective-permute-start | bytes 589832 | tf_op jit(solution)/shard_map/ppermute | solution.py:460
  17.8 8.0 %all-to-all-start = ((s32[32,1,128]{2,1,0:T(1,128)}), s32[32,1,128]{2,1,0:T(1,128)S(1)}, u32[]{:S(2)}, u32[]{:S(2)}) async-start(s32[32,1,128]{2,1,0:T(1,128)} %bitcast.2), calls=%async_computation | async-start | bytes 32768 | tf_op jit(solution)/shard_map/all_to_all | solution.py:463
  25.8 1.5 %collective-permute-start.4 = (bf16[64,1536]{1,0:T(8,128)(2,1)}, bf16[64,1536]{1,0:T(8,128)(2,1)}, u32[]{:S(2)}, u32[]{:S(2)}) collective-permute-start(bf16[64,1536]{1,0:T(8,128)(2,1)} %pad_maximum_fusion.near_ref), channel_id=1, source_target_pairs={{0,2},{1,7},{2,0},{3,5},{4,6},{5,3},{6,4},{7,1},{8,10},{9,15},{10,... | collective-permute-start | bytes 589832 | tf_op jit(solution)/shard_map/ppermute | solution.py:460
  27.4 1.5 %collective-permute-start.5 = (bf16[64,1536]{1,0:T(8,128)(2,1)}, bf16[64,1536]{1,0:T(8,128)(2,1)}, u32[]{:S(2)}, u32[]{:S(2)}) collective-permute-start(bf16[64,1536]{1,0:T(8,128)(2,1)} %collective-permute-done.3.first_ref), channel_id=1, source_target_pairs={{0,2},{1,7},{2,0},{3,5},{4,6},{5,3},{6,4},{7,1},{8,10},{9,15},{10,... | collective-permute-start | bytes 589832 | tf_op jit(solution)/shard_map/ppermute | solution.py:460
  28.9 4.0 %all-to-all-done = s32[32,1,128]{2,1,0:T(1,128)S(1)} async-done(((s32[32,1,128]{2,1,0:T(1,128)}), s32[32,1,128]{2,1,0:T(1,128)S(1)}, u32[]{:S(2)}, u32[]{:S(2)}) %all-to-all-start) | async-done | bytes 16416 | tf_op jit(solution)/shard_map/all_to_all | solution.py:463
  32.8 2.2 %owner_pack.1 = bf16[32,208,128]{2,1,0:T(8,128)(2,1)} custom-call(s32[32,128]{1,0:T(8,128)S(1)} %bitcast.12, bf16[288,1536]{1,0:T(8,128)(2,1)S(1)} %owner_forward.1.branch_ref), custom_call_target="tpu_custom_call" | custom-call | flops 3000000000 | bytes 4096 | tf_op jit(solution)/shard_map/owner_pack/pallas_call | solution.py:168
  35.0 0.1 copy.17.labels_ref
  35.2 5.2 %all-to-all-start.1 = ((bf16[32,208,128]{2,1,0:T(8,128)(2,1)}), bf16[32,208,128]{2,1,0:T(8,128)(2,1)S(1)}, u32[]{:S(2)}, u32[]{:S(2)}) async-start(bf16[32,208,128]{2,1,0:T(8,128)(2,1)} %owner_pack.1), calls=%async_computation.1 | async-start | bytes 3407872 | tf_op jit(solution)/shard_map/all_to_all | solution.py:472
  40.4 0.9 copy.15.owners_col_ref
  41.3 2.4 %normalise_texts.1.half_hbm = bf16[256,1536]{1,0:T(8,128)(2,1)} custom-call(bf16[64,1536]{1,0:T(8,128)(2,1)} %pad_maximum_fusion.near_ref, bf16[64,1536]{1,0:T(8,128)(2,1)} %collective-permute-done.3.first_ref, bf16[64,1536]{1,0:T(8,128)(2,1)} %collective-permute-done.4.second_ref, bf16[64,1536]{1,0:T(8,128)(2,1)} %collective-permute-done.5.third_ref), custom_call_target="tpu_custom_call" | custom-call | flops 1 | bytes 1048576 | tf_op jit(solution)/shard_map/normalise_texts/pallas_call | solution.py:191
  43.7 0.9 copy-done.2
  44.6 2.3 %prepare_onehots.1 = (bf16[512,640]{1,0:T(8,128)(2,1)}, bf16[544,512]{1,0:T(8,128)(2,1)}, bf16[288,640]{1,0:T(8,128)(2,1)}, f32[48,512]{1,0:T(8,128)}, bf16[512,48]{1,0:T(8,128)(2,1)}) custom-call(s32[1,512]{1,0:T(1,128)S(1)} %bitcast.16, s32[512,1]{1,0:T(8,128)S(1)} %copy-done.2, s32[1,16]{1,0:T(1,128)S(1)} %bitcast.18, s32[16,1]{1,0:T(8,128)S(1)} %copy.16.sizes_col_ref, ...), custom_call_target="tpu_custom_call" | custom-call | flops 99999997952 | bytes 4096 | tf_op jit(solution)/shard_map/prepare_onehots/pallas_call | solution.py:254
  47.0 14.7 %all-to-all-done.1.arrived_ref = bf16[32,208,128]{2,1,0:T(8,128)(2,1)S(1)} async-done(((bf16[32,208,128]{2,1,0:T(8,128)(2,1)}), bf16[32,208,128]{2,1,0:T(8,128)(2,1)S(1)}, u32[]{:S(2)}, u32[]{:S(2)}) %all-to-all-start.1) | async-done | bytes 1703968 | tf_op jit(solution)/shard_map/all_to_all | solution.py:472
  61.7 7.6 %slot_gradients.1 = (bf16[512,1536]{1,0:T(8,128)(2,1)}, bf16[32,208,128]{2,1,0:T(8,128)(2,1)S(1)}, bf16[3072,1536]{1,0:T(8,128)(2,1)S(1)}) custom-call(bf16[32,208,128]{2,1,0:T(8,128)(2,1)S(1)} %all-to-all-done.1.arrived_ref, bf16[512,1536]{1,0:T(8,128)(2,1)} %patch_hbm.1, bf16[256,1536]{1,0:T(8,128)(2,1)} %normalise_texts.1.half_hbm, ...), custom_call_target="tpu_custom_call" | custom-call | flops 2013265920 | bytes 10485760 | tf_op jit(solution)/shard_map/slot_gradients/pallas_call | solution.py:361
  69.3 23.6 %all_to_all.21.arrived_ref = bf16[32,208,128]{2,1,0:T(8,128)(2,1)S(1)} all-to-all(bf16[32,208,128]{2,1,0:T(8,128)(2,1)S(1)} %get-tuple-element.53), channel_id=1, replica_groups=mesh['blk'=32,'grp'=8] {'blk'}, dimensions={0} | all-to-all | bytes 3407872 | tf_op jit(solution)/shard_map/all_to_all | solution.py:491
  92.9 5.3 %owner_backward.1 = bf16[288,3072]{1,0:T(8,128)(2,1)} custom-call(bf16[32,208,128]{2,1,0:T(8,128)(2,1)S(1)} %all_to_all.21.arrived_ref, bf16[288,640]{1,0:T(8,128)(2,1)S(1)} %copy-done.1, bf16[288,3072]{1,0:T(8,128)(2,1)S(1)} %copy-done, bf16[3072,1536]{1,0:T(8,128)(2,1)S(1)} %get-tuple-element.55.weight_ref), custom_call_target="tpu_custom_call" | custom-call | flops 2717908992 | bytes 12976128 | tf_op jit(solution)/shard_map/owner_backward/pallas_call | solution.py:424
  (28 shorter events, 0.2 us)
Async XLA Ops:
  0.6 6.1 %slice-start = ((s8[9437184]{0:T(1024)(128)(4,1)}), s8[4194304]{0:T(1024)(128)(4,1)S(1)}, s32[]{:S(2)}) async-start(s8[9437184]{0:T(1024)(128)(4,1)} %bitcast.10), calls=%async_computation.3 | async-start | bytes 8388608
  0.6 1.6 %copy-start.5 = (bf16[16,1536]{1,0:T(8,128)(2,1)S(1)}, bf16[16,1536]{1,0:T(8,128)(2,1)}, u32[]{:S(2)}) copy-start(bf16[16,1536]{1,0:T(8,128)(2,1)} %param.10) | copy-start | bytes 147460
  0.7 6.0 %slice-start.1 = ((s8[9437184]{0:T(1024)(128)(4,1)}), s8[4194304]{0:T(1024)(128)(4,1)S(1)}, s32[]{:S(2)}) async-start(s8[9437184]{0:T(1024)(128)(4,1)} %bitcast.10), calls=%async_computation.4 | async-start | bytes 8388608
  0.7 6.0 %slice-start.2 = ((s8[9437184]{0:T(1024)(128)(4,1)}), s8[1048576]{0:T(1024)(128)(4,1)S(1)}, s32[]{:S(2)}) async-start(s8[9437184]{0:T(1024)(128)(4,1)} %bitcast.10), calls=%async_computation.5 | async-start | bytes 2097152
  0.7 6.0 %copy-start = (bf16[288,3072]{1,0:T(8,128)(2,1)S(1)}, bf16[288,3072]{1,0:T(8,128)(2,1)}, u32[]{:S(2)}) copy-start(bf16[288,3072]{1,0:T(8,128)(2,1)} %hidden_ref.3) | copy-start | bytes 5308420
  2.2 8.6 %collective-permute-start.2 = (bf16[16,1536]{1,0:T(8,128)(2,1)S(1)}, bf16[16,1536]{1,0:T(8,128)(2,1)S(1)}, u32[]{:S(2)}, u32[]{:S(2)}) collective-permute-start(bf16[16,1536]{1,0:T(8,128)(2,1)S(1)} %copy-done.5), channel_id=1, source_target_pairs={{232,0},{240,8},{248,16},{0,24},{8,32},{16,40},{24,48},{32,56},{40... | collective-permute-start | bytes 147464 | tf_op jit(solution)/shard_map/ppermute | solution.py:453
  5.1 5.8 %collective-permute-start.1 = (bf16[16,1536]{1,0:T(8,128)(2,1)S(1)}, bf16[16,1536]{1,0:T(8,128)(2,1)S(1)}, u32[]{:S(2)}, u32[]{:S(2)}) collective-permute-start(bf16[16,1536]{1,0:T(8,128)(2,1)S(1)} %copy-done.5), channel_id=1, source_target_pairs={{240,0},{248,8},{0,16},{8,24},{16,32},{24,40},{32,48},{40,56},{48,... | collective-permute-start | bytes 147464 | tf_op jit(solution)/shard_map/ppermute | solution.py:453
  6.3 5.0 %collective-permute-start = (bf16[16,1536]{1,0:T(8,128)(2,1)S(1)}, bf16[16,1536]{1,0:T(8,128)(2,1)S(1)}, u32[]{:S(2)}, u32[]{:S(2)}) collective-permute-start(bf16[16,1536]{1,0:T(8,128)(2,1)S(1)} %copy-done.5), channel_id=1, source_target_pairs={{248,0},{0,8},{8,16},{16,24},{24,32},{32,40},{40,48},{48,56},{56,6... | collective-permute-start | bytes 147464 | tf_op jit(solution)/shard_map/ppermute | solution.py:453
  11.9 13.9 %collective-permute-start.3 = (bf16[64,1536]{1,0:T(8,128)(2,1)}, bf16[64,1536]{1,0:T(8,128)(2,1)}, u32[]{:S(2)}, u32[]{:S(2)}) collective-permute-start(bf16[64,1536]{1,0:T(8,128)(2,1)} %pad_maximum_fusion.near_ref), channel_id=1, source_target_pairs={{0,6},{1,3},{2,4},{3,1},{4,2},{5,7},{6,0},{7,5},{8,14},{9,11},{10,... | collective-permute-start | bytes 589832 | tf_op jit(solution)/shard_map/ppermute | solution.py:460
  17.8 15.0 %all-to-all-start = ((s32[32,1,128]{2,1,0:T(1,128)}), s32[32,1,128]{2,1,0:T(1,128)S(1)}, u32[]{:S(2)}, u32[]{:S(2)}) async-start(s32[32,1,128]{2,1,0:T(1,128)} %bitcast.2), calls=%async_computation | async-start | bytes 32768 | tf_op jit(solution)/shard_map/all_to_all | solution.py:463
  25.8 15.4 %collective-permute-start.4 = (bf16[64,1536]{1,0:T(8,128)(2,1)}, bf16[64,1536]{1,0:T(8,128)(2,1)}, u32[]{:S(2)}, u32[]{:S(2)}) collective-permute-start(bf16[64,1536]{1,0:T(8,128)(2,1)} %pad_maximum_fusion.near_ref), channel_id=1, source_target_pairs={{0,2},{1,7},{2,0},{3,5},{4,6},{5,3},{6,4},{7,1},{8,10},{9,15},{10,... | collective-permute-start | bytes 589832 | tf_op jit(solution)/shard_map/ppermute | solution.py:460
  27.4 13.9 %collective-permute-start.5 = (bf16[64,1536]{1,0:T(8,128)(2,1)}, bf16[64,1536]{1,0:T(8,128)(2,1)}, u32[]{:S(2)}, u32[]{:S(2)}) collective-permute-start(bf16[64,1536]{1,0:T(8,128)(2,1)} %collective-permute-done.3.first_ref), channel_id=1, source_target_pairs={{0,2},{1,7},{2,0},{3,5},{4,6},{5,3},{6,4},{7,1},{8,10},{9,15},{10,... | collective-permute-start | bytes 589832 | tf_op jit(solution)/shard_map/ppermute | solution.py:460
  32.8 2.2 %copy-start.6 = (s32[16]{0:T(128)S(1)}, s32[16]{0:T(128)}, u32[]{:S(2)}) copy-start(s32[16]{0:T(128)} %param.13) | copy-start | bytes 196
  32.8 2.3 %copy-start.4 = (s32[16]{0:T(128)S(1)}, s32[16]{0:T(128)}, u32[]{:S(2)}) copy-start(s32[16]{0:T(128)} %param.11) | copy-start | bytes 196
  35.2 5.2 %copy-start.3 = (s32[512]{0:T(512)S(1)}, s32[512]{0:T(512)}, u32[]{:S(2)}) copy-start(s32[512]{0:T(512)} %param.12) | copy-start | bytes 6148
  35.2 26.5 %all-to-all-start.1 = ((bf16[32,208,128]{2,1,0:T(8,128)(2,1)}), bf16[32,208,128]{2,1,0:T(8,128)(2,1)S(1)}, u32[]{:S(2)}, u32[]{:S(2)}) async-start(bf16[32,208,128]{2,1,0:T(8,128)(2,1)} %owner_pack.1), calls=%async_computation.1 | async-start | bytes 3407872 | tf_op jit(solution)/shard_map/all_to_all | solution.py:472
  43.7 3.3 %collective-permute-start.6 = (bf16[256,1536]{1,0:T(8,128)(2,1)}, bf16[256,1536]{1,0:T(8,128)(2,1)}, u32[]{:S(2)}, u32[]{:S(2)}) collective-permute-start(bf16[256,1536]{1,0:T(8,128)(2,1)} %normalise_texts.1.half_hbm), channel_id=1, source_target_pairs={{0,1},{1,0},{2,3},{3,2},{4,5},{5,4},{6,7},{7,6},{8,9},{9,8},{10,11... | collective-permute-start | bytes 2359304 | tf_op jit(solution)/shard_map/ppermute | solution.py:475
  43.7 1.0 copy-start.2
  69.3 23.6 %copy-start.1 = (bf16[288,640]{1,0:T(8,128)(2,1)S(1)}, bf16[288,640]{1,0:T(8,128)(2,1)}, u32[]{:S(2)}) copy-start(bf16[288,640]{1,0:T(8,128)(2,1)} %get-tuple-element.54.to_rows_ref) | copy-start | bytes 1105924

commit v7 on v6

--- a/solution.py
+++ b/solution.py
@@ -448,9 +448,9 @@
     tallies = tally(owners)
     text, tallies = lax.optimization_barrier((text_features, tallies))
     met = [text]
-    for distance in range(1, STEPS):
+    for distance in range(STEPS - 1, 0, -1):
         route = [((i - distance) % BLK, i) for i in range(BLK)]
-        met.append(lax.ppermute(text, "blk", route))
+        met.insert(1, lax.ppermute(text, "blk", route))
     branch = forward(hidden_pre, down_weight)
     branch, position, place, *met = lax.optimization_barrier((branch, position, place, *met))
     near = jnp.concatenate(met, axis=0)

time: 100 us -> 100 us (level)
  no operation moved by 1% of the time
where the time goes in v7:
time: 100 us; the launch traced here: 98.3 us
  starting transfers between devices  26.6 us (27%)
  Pallas kernels  24.3 us (24%)
  blocking collectives  23.6 us (24%)
  waiting for transfers between devices  20.2 us (20%)
  local copies, waits for them, and re-layouts  2.02 us (2%)
    all_to_all x1, blocking collectives, on_device(): lax.all_to_all(outgoing, 'blk', split_axis=0, concat_axis=0, tiled=True)  23.6 us
    all_to_all x1, waiting for transfers between devices, on_device(): lax.all_to_all(message, 'blk', split_axis=0, concat_axis=0, tiled=True)  14.7 us
    ppermute x3, starting transfers between devices, swapped(): lax.ppermute(block, 'grp', [(i, i ^ masks[i % 2]) for i in range(grp_coun...  8.89 us
    all_to_all x1, starting transfers between devices, on_device(): lax.all_to_all(tallies, 'blk', split_axis=0, concat_axis=0, tiled=True)  7.95 us
    pallas_call x1, Pallas kernels, slots(): pl.pallas_call(slot_kernel, in_specs=vmem(1) + any_space(8), out_specs=an...  7.64 us
    pallas_call x1, Pallas kernels, backward(): pl.pallas_call(backward_kernel, in_specs=vmem(4), out_specs=pl.BlockSpec(...  5.26 us
    all_to_all x1, starting transfers between devices, on_device(): lax.all_to_all(message, 'blk', split_axis=0, concat_axis=0, tiled=True)  5.24 us
    ppermute x3, starting transfers between devices, on_device(): met.insert(1, lax.ppermute(text, 'blk', route))  4.47 us
  transfers between devices with their start and end apart: 9, of which 4 were waited for; matrix products, arithmetic and copies ran while one was open for 1% of the time, Pallas kernels for 10%

profile of v7, /device:TPU:2, one launch (start us, length us, event | category | flops | bytes accessed | tf_op | source)
XLA Modules:
  0.0 98.3 jit_solution(3579560491767287978)
XLA Ops:
  0.7 1.5 %tally_owners.1 = s32[32,128]{1,0:T(8,128)} custom-call(s32[1,512]{1,0:T(1,128)} %bitcast.14), custom_call_target="tpu_custom_call" | custom-call | flops 10000000000 | bytes 32768 | tf_op jit(solution)/shard_map/tally_owners/pallas_call | solution.py:83
  2.2 2.8 %collective-permute-start.2 = (bf16[16,1536]{1,0:T(8,128)(2,1)S(1)}, bf16[16,1536]{1,0:T(8,128)(2,1)S(1)}, u32[]{:S(2)}, u32[]{:S(2)}) collective-permute-start(bf16[16,1536]{1,0:T(8,128)(2,1)S(1)} %copy-done.5), channel_id=1, source_target_pairs={{232,0},{240,8},{248,16},{0,24},{8,32},{16,40},{24,48},{32,56},{40... | collective-permute-start | bytes 147464 | tf_op jit(solution)/shard_map/ppermute | solution.py:453
  5.1 1.2 %collective-permute-start.1 = (bf16[16,1536]{1,0:T(8,128)(2,1)S(1)}, bf16[16,1536]{1,0:T(8,128)(2,1)S(1)}, u32[]{:S(2)}, u32[]{:S(2)}) collective-permute-start(bf16[16,1536]{1,0:T(8,128)(2,1)S(1)} %copy-done.5), channel_id=1, source_target_pairs={{240,0},{248,8},{0,16},{8,24},{16,32},{24,40},{32,48},{40,56},{48,... | collective-permute-start | bytes 147464 | tf_op jit(solution)/shard_map/ppermute | solution.py:453
  6.3 0.4 collective-permute-start
  6.7 3.0 %owner_forward.1.branch_ref = bf16[288,1536]{1,0:T(8,128)(2,1)S(1)} custom-call(bf16[288,3072]{1,0:T(8,128)(2,1)S(1)} %copy-done, bf16[3072,1536]{1,0:T(8,128)(2,1)S(1)} %bitcast.11), custom_call_target="tpu_custom_call" | custom-call | flops 2717908992 | bytes 11206656 | tf_op jit(solution)/shard_map/owner_forward/pallas_call | solution.py:153
  9.7 1.1 %collective-permute-done.2 = bf16[16,1536]{1,0:T(8,128)(2,1)S(1)} collective-permute-done((bf16[16,1536]{1,0:T(8,128)(2,1)S(1)}, bf16[16,1536]{1,0:T(8,128)(2,1)S(1)}, u32[]{:S(2)}, u32[]{:S(2)}) %collective-permute-start.2) | collective-permute-done | bytes 49184 | tf_op jit(solution)/shard_map/ppermute | solution.py:453
  10.8 0.4 collective-permute-done
  11.3 0.7 pad_maximum_fusion.near_ref
  11.9 5.9 %collective-permute-start.3 = (bf16[64,1536]{1,0:T(8,128)(2,1)}, bf16[64,1536]{1,0:T(8,128)(2,1)}, u32[]{:S(2)}, u32[]{:S(2)}) collective-permute-start(bf16[64,1536]{1,0:T(8,128)(2,1)} %pad_maximum_fusion.near_ref), channel_id=1, source_target_pairs={{0,6},{1,3},{2,4},{3,1},{4,2},{5,7},{6,0},{7,5},{8,14},{9,11},{10,... | collective-permute-start | bytes 589832 | tf_op jit(solution)/shard_map/ppermute | solution.py:460
  17.8 8.0 %all-to-all-start = ((s32[32,1,128]{2,1,0:T(1,128)}), s32[32,1,128]{2,1,0:T(1,128)S(1)}, u32[]{:S(2)}, u32[]{:S(2)}) async-start(s32[32,1,128]{2,1,0:T(1,128)} %bitcast.2), calls=%async_computation | async-start | bytes 32768 | tf_op jit(solution)/shard_map/all_to_all | solution.py:463
  25.8 1.5 %collective-permute-start.4 = (bf16[64,1536]{1,0:T(8,128)(2,1)}, bf16[64,1536]{1,0:T(8,128)(2,1)}, u32[]{:S(2)}, u32[]{:S(2)}) collective-permute-start(bf16[64,1536]{1,0:T(8,128)(2,1)} %pad_maximum_fusion.near_ref), channel_id=1, source_target_pairs={{0,2},{1,7},{2,0},{3,5},{4,6},{5,3},{6,4},{7,1},{8,10},{9,15},{10,... | collective-permute-start | bytes 589832 | tf_op jit(solution)/shard_map/ppermute | solution.py:460
  27.4 1.5 %collective-permute-start.5 = (bf16[64,1536]{1,0:T(8,128)(2,1)}, bf16[64,1536]{1,0:T(8,128)(2,1)}, u32[]{:S(2)}, u32[]{:S(2)}) collective-permute-start(bf16[64,1536]{1,0:T(8,128)(2,1)} %collective-permute-done.3.first_ref), channel_id=1, source_target_pairs={{0,2},{1,7},{2,0},{3,5},{4,6},{5,3},{6,4},{7,1},{8,10},{9,15},{10,... | collective-permute-start | bytes 589832 | tf_op jit(solution)/shard_map/ppermute | solution.py:460
  28.9 4.0 %all-to-all-done = s32[32,1,128]{2,1,0:T(1,128)S(1)} async-done(((s32[32,1,128]{2,1,0:T(1,128)}), s32[32,1,128]{2,1,0:T(1,128)S(1)}, u32[]{:S(2)}, u32[]{:S(2)}) %all-to-all-start) | async-done | bytes 16416 | tf_op jit(solution)/shard_map/all_to_all | solution.py:463
  32.8 2.2 %owner_pack.1 = bf16[32,208,128]{2,1,0:T(8,128)(2,1)} custom-call(s32[32,128]{1,0:T(8,128)S(1)} %bitcast.12, bf16[288,1536]{1,0:T(8,128)(2,1)S(1)} %owner_forward.1.branch_ref), custom_call_target="tpu_custom_call" | custom-call | flops 3000000000 | bytes 4096 | tf_op jit(solution)/shard_map/owner_pack/pallas_call | solution.py:168
  35.0 0.1 copy.17.labels_ref
  35.2 5.2 %all-to-all-start.1 = ((bf16[32,208,128]{2,1,0:T(8,128)(2,1)}), bf16[32,208,128]{2,1,0:T(8,128)(2,1)S(1)}, u32[]{:S(2)}, u32[]{:S(2)}) async-start(bf16[32,208,128]{2,1,0:T(8,128)(2,1)} %owner_pack.1), calls=%async_computation.1 | async-start | bytes 3407872 | tf_op jit(solution)/shard_map/all_to_all | solution.py:472
  40.4 0.9 copy.15.owners_col_ref
  41.3 2.4 %normalise_texts.1.half_hbm = bf16[256,1536]{1,0:T(8,128)(2,1)} custom-call(bf16[64,1536]{1,0:T(8,128)(2,1)} %pad_maximum_fusion.near_ref, bf16[64,1536]{1,0:T(8,128)(2,1)} %collective-permute-done.3.first_ref, bf16[64,1536]{1,0:T(8,128)(2,1)} %collective-permute-done.4.second_ref, bf16[64,1536]{1,0:T(8,128)(2,1)} %collective-permute-done.5.third_ref), custom_call_target="tpu_custom_call" | custom-call | flops 1 | bytes 1048576 | tf_op jit(solution)/shard_map/normalise_texts/pallas_call | solution.py:191
  43.7 0.9 copy-done.2
  44.6 2.3 %prepare_onehots.1 = (bf16[512,640]{1,0:T(8,128)(2,1)}, bf16[544,512]{1,0:T(8,128)(2,1)}, bf16[288,640]{1,0:T(8,128)(2,1)}, f32[48,512]{1,0:T(8,128)}, bf16[512,48]{1,0:T(8,128)(2,1)}) custom-call(s32[1,512]{1,0:T(1,128)S(1)} %bitcast.16, s32[512,1]{1,0:T(8,128)S(1)} %copy-done.2, s32[1,16]{1,0:T(1,128)S(1)} %bitcast.18, s32[16,1]{1,0:T(8,128)S(1)} %copy.16.sizes_col_ref, ...), custom_call_target="tpu_custom_call" | custom-call | flops 99999997952 | bytes 4096 | tf_op jit(solution)/shard_map/prepare_onehots/pallas_call | solution.py:254
  47.0 14.7 %all-to-all-done.1.arrived_ref = bf16[32,208,128]{2,1,0:T(8,128)(2,1)S(1)} async-done(((bf16[32,208,128]{2,1,0:T(8,128)(2,1)}), bf16[32,208,128]{2,1,0:T(8,128)(2,1)S(1)}, u32[]{:S(2)}, u32[]{:S(2)}) %all-to-all-start.1) | async-done | bytes 1703968 | tf_op jit(solution)/shard_map/all_to_all | solution.py:472
  61.7 7.6 %slot_gradients.1 = (bf16[512,1536]{1,0:T(8,128)(2,1)}, bf16[32,208,128]{2,1,0:T(8,128)(2,1)S(1)}, bf16[3072,1536]{1,0:T(8,128)(2,1)S(1)}) custom-call(bf16[32,208,128]{2,1,0:T(8,128)(2,1)S(1)} %all-to-all-done.1.arrived_ref, bf16[512,1536]{1,0:T(8,128)(2,1)} %patch_hbm.1, bf16[256,1536]{1,0:T(8,128)(2,1)} %normalise_texts.1.half_hbm, ...), custom_call_target="tpu_custom_call" | custom-call | flops 2013265920 | bytes 10485760 | tf_op jit(solution)/shard_map/slot_gradients/pallas_call | solution.py:361
  69.3 23.6 %all_to_all.21.arrived_ref = bf16[32,208,128]{2,1,0:T(8,128)(2,1)S(1)} all-to-all(bf16[32,208,128]{2,1,0:T(8,128)(2,1)S(1)} %get-tuple-element.53), channel_id=1, replica_groups=mesh['blk'=32,'grp'=8] {'blk'}, dimensions={0} | all-to-all | bytes 3407872 | tf_op jit(solution)/shard_map/all_to_all | solution.py:491
  92.9 5.3 %owner_backward.1 = bf16[288,3072]{1,0:T(8,128)(2,1)} custom-call(bf16[32,208,128]{2,1,0:T(8,128)(2,1)S(1)} %all_to_all.21.arrived_ref, bf16[288,640]{1,0:T(8,128)(2,1)S(1)} %copy-done.1, bf16[288,3072]{1,0:T(8,128)(2,1)S(1)} %copy-done, bf16[3072,1536]{1,0:T(8,128)(2,1)S(1)} %get-tuple-element.55.weight_ref), custom_call_target="tpu_custom_call" | custom-call | flops 2717908992 | bytes 12976128 | tf_op jit(solution)/shard_map/owner_backward/pallas_call | solution.py:424
  (28 shorter events, 0.2 us)
Async XLA Ops:
  0.6 6.1 %slice-start = ((s8[9437184]{0:T(1024)(128)(4,1)}), s8[4194304]{0:T(1024)(128)(4,1)S(1)}, s32[]{:S(2)}) async-start(s8[9437184]{0:T(1024)(128)(4,1)} %bitcast.10), calls=%async_computation.3 | async-start | bytes 8388608
  0.6 1.6 %copy-start.5 = (bf16[16,1536]{1,0:T(8,128)(2,1)S(1)}, bf16[16,1536]{1,0:T(8,128)(2,1)}, u32[]{:S(2)}) copy-start(bf16[16,1536]{1,0:T(8,128)(2,1)} %param.10) | copy-start | bytes 147460
  0.7 6.0 %slice-start.1 = ((s8[9437184]{0:T(1024)(128)(4,1)}), s8[4194304]{0:T(1024)(128)(4,1)S(1)}, s32[]{:S(2)}) async-start(s8[9437184]{0:T(1024)(128)(4,1)} %bitcast.10), calls=%async_computation.4 | async-start | bytes 8388608
  0.7 6.0 %slice-start.2 = ((s8[9437184]{0:T(1024)(128)(4,1)}), s8[1048576]{0:T(1024)(128)(4,1)S(1)}, s32[]{:S(2)}) async-start(s8[9437184]{0:T(1024)(128)(4,1)} %bitcast.10), calls=%async_computation.5 | async-start | bytes 2097152
  0.7 6.0 %copy-start = (bf16[288,3072]{1,0:T(8,128)(2,1)S(1)}, bf16[288,3072]{1,0:T(8,128)(2,1)}, u32[]{:S(2)}) copy-start(bf16[288,3072]{1,0:T(8,128)(2,1)} %hidden_ref.3) | copy-start | bytes 5308420
  2.2 8.6 %collective-permute-start.2 = (bf16[16,1536]{1,0:T(8,128)(2,1)S(1)}, bf16[16,1536]{1,0:T(8,128)(2,1)S(1)}, u32[]{:S(2)}, u32[]{:S(2)}) collective-permute-start(bf16[16,1536]{1,0:T(8,128)(2,1)S(1)} %copy-done.5), channel_id=1, source_target_pairs={{232,0},{240,8},{248,16},{0,24},{8,32},{16,40},{24,48},{32,56},{40... | collective-permute-start | bytes 147464 | tf_op jit(solution)/shard_map/ppermute | solution.py:453
  5.1 5.8 %collective-permute-start.1 = (bf16[16,1536]{1,0:T(8,128)(2,1)S(1)}, bf16[16,1536]{1,0:T(8,128)(2,1)S(1)}, u32[]{:S(2)}, u32[]{:S(2)}) collective-permute-start(bf16[16,1536]{1,0:T(8,128)(2,1)S(1)} %copy-done.5), channel_id=1, source_target_pairs={{240,0},{248,8},{0,16},{8,24},{16,32},{24,40},{32,48},{40,56},{48,... | collective-permute-start | bytes 147464 | tf_op jit(solution)/shard_map/ppermute | solution.py:453
  6.3 5.0 %collective-permute-start = (bf16[16,1536]{1,0:T(8,128)(2,1)S(1)}, bf16[16,1536]{1,0:T(8,128)(2,1)S(1)}, u32[]{:S(2)}, u32[]{:S(2)}) collective-permute-start(bf16[16,1536]{1,0:T(8,128)(2,1)S(1)} %copy-done.5), channel_id=1, source_target_pairs={{248,0},{0,8},{8,16},{16,24},{24,32},{32,40},{40,48},{48,56},{56,6... | collective-permute-start | bytes 147464 | tf_op jit(solution)/shard_map/ppermute | solution.py:453
  11.9 13.9 %collective-permute-start.3 = (bf16[64,1536]{1,0:T(8,128)(2,1)}, bf16[64,1536]{1,0:T(8,128)(2,1)}, u32[]{:S(2)}, u32[]{:S(2)}) collective-permute-start(bf16[64,1536]{1,0:T(8,128)(2,1)} %pad_maximum_fusion.near_ref), channel_id=1, source_target_pairs={{0,6},{1,3},{2,4},{3,1},{4,2},{5,7},{6,0},{7,5},{8,14},{9,11},{10,... | collective-permute-start | bytes 589832 | tf_op jit(solution)/shard_map/ppermute | solution.py:460
  17.8 15.0 %all-to-all-start = ((s32[32,1,128]{2,1,0:T(1,128)}), s32[32,1,128]{2,1,0:T(1,128)S(1)}, u32[]{:S(2)}, u32[]{:S(2)}) async-start(s32[32,1,128]{2,1,0:T(1,128)} %bitcast.2), calls=%async_computation | async-start | bytes 32768 | tf_op jit(solution)/shard_map/all_to_all | solution.py:463
  25.8 15.4 %collective-permute-start.4 = (bf16[64,1536]{1,0:T(8,128)(2,1)}, bf16[64,1536]{1,0:T(8,128)(2,1)}, u32[]{:S(2)}, u32[]{:S(2)}) collective-permute-start(bf16[64,1536]{1,0:T(8,128)(2,1)} %pad_maximum_fusion.near_ref), channel_id=1, source_target_pairs={{0,2},{1,7},{2,0},{3,5},{4,6},{5,3},{6,4},{7,1},{8,10},{9,15},{10,... | collective-permute-start | bytes 589832 | tf_op jit(solution)/shard_map/ppermute | solution.py:460
  27.4 13.9 %collective-permute-start.5 = (bf16[64,1536]{1,0:T(8,128)(2,1)}, bf16[64,1536]{1,0:T(8,128)(2,1)}, u32[]{:S(2)}, u32[]{:S(2)}) collective-permute-start(bf16[64,1536]{1,0:T(8,128)(2,1)} %collective-permute-done.3.first_ref), channel_id=1, source_target_pairs={{0,2},{1,7},{2,0},{3,5},{4,6},{5,3},{6,4},{7,1},{8,10},{9,15},{10,... | collective-permute-start | bytes 589832 | tf_op jit(solution)/shard_map/ppermute | solution.py:460
  32.8 2.2 %copy-start.6 = (s32[16]{0:T(128)S(1)}, s32[16]{0:T(128)}, u32[]{:S(2)}) copy-start(s32[16]{0:T(128)} %param.13) | copy-start | bytes 196
  32.8 2.3 %copy-start.4 = (s32[16]{0:T(128)S(1)}, s32[16]{0:T(128)}, u32[]{:S(2)}) copy-start(s32[16]{0:T(128)} %param.11) | copy-start | bytes 196
  35.2 5.2 %copy-start.3 = (s32[512]{0:T(512)S(1)}, s32[512]{0:T(512)}, u32[]{:S(2)}) copy-start(s32[512]{0:T(512)} %param.12) | copy-start | bytes 6148
  35.2 26.5 %all-to-all-start.1 = ((bf16[32,208,128]{2,1,0:T(8,128)(2,1)}), bf16[32,208,128]{2,1,0:T(8,128)(2,1)S(1)}, u32[]{:S(2)}, u32[]{:S(2)}) async-start(bf16[32,208,128]{2,1,0:T(8,128)(2,1)} %owner_pack.1), calls=%async_computation.1 | async-start | bytes 3407872 | tf_op jit(solution)/shard_map/all_to_all | solution.py:472
  43.7 3.3 %collective-permute-start.6 = (bf16[256,1536]{1,0:T(8,128)(2,1)}, bf16[256,1536]{1,0:T(8,128)(2,1)}, u32[]{:S(2)}, u32[]{:S(2)}) collective-permute-start(bf16[256,1536]{1,0:T(8,128)(2,1)} %normalise_texts.1.half_hbm), channel_id=1, source_target_pairs={{0,1},{1,0},{2,3},{3,2},{4,5},{5,4},{6,7},{7,6},{8,9},{9,8},{10,11... | collective-permute-start | bytes 2359304 | tf_op jit(solution)/shard_map/ppermute | solution.py:475
  43.7 1.0 copy-start.2
  69.3 23.6 %copy-start.1 = (bf16[288,640]{1,0:T(8,128)(2,1)S(1)}, bf16[288,640]{1,0:T(8,128)(2,1)}, u32[]{:S(2)}) copy-start(bf16[288,640]{1,0:T(8,128)(2,1)} %get-tuple-element.54.to_rows_ref) | copy-start | bytes 1105924
